TPU v7x, 32 devices: a whole 2x2x4 slice. The times are simulated.
32 devices in a mesh: seq: 16 (over z, y, x), batch: 2 (over core).
Axes of the slice: x: 2, y: 2, z: 4, core: 2. Of those that a mesh axis runs over, the one named last changes fastest.
Arguments:
- inputs: bfloat16 [2, 16384, 768], P('batch', 'seq'), may hold values from -6 to 6
- selection: int32 [2, 256, 16], P('batch', 'seq'), may hold values from 0 to 255, as said below
- cotangent: bfloat16 [2, 16384, 768], P('batch', 'seq'), may hold values from -6 to 6
- ln1_gain: bfloat16 [768], P(('seq', 'batch')), may hold values from 0.5 to 1.5
- ln1_bias: bfloat16 [768], P(('seq', 'batch')), may hold values from -1 to 1
- w_qkv: bfloat16 [768, 2304], P(('seq', 'batch')), may hold values from -0.21875 to 0.21875
- w_out: bfloat16 [768, 768], P(('seq', 'batch')), may hold values from -1.75 to 1.75
- ln2_gain: bfloat16 [768], P(('seq', 'batch')), may hold values from 0.5 to 1.5
- ln2_bias: bfloat16 [768], P(('seq', 'batch')), may hold values from -1 to 1
- w_up: bfloat16 [768, 3072], P(('seq', 'batch')), may hold values from -0.21875 to 0.21875
- w_down: bfloat16 [3072, 768], P(('seq', 'batch')), may hold values from -0.109375 to 0.109375
Outputs:
- output: bfloat16 [2, 16384, 768], P('batch', 'seq')
- input_grad: float32 [2, 16384, 768], P('batch', 'seq')
- grad_ln1_gain: float32 [768], P(('seq', 'batch'))
- grad_ln1_bias: float32 [768], P(('seq', 'batch'))
- grad_qkv: float32 [768, 2304], P(('seq', 'batch'))
- grad_out: float32 [768, 768], P(('seq', 'batch'))
- grad_ln2_gain: float32 [768], P(('seq', 'batch'))
- grad_ln2_bias: float32 [768], P(('seq', 'batch'))
- grad_up: float32 [768, 3072], P(('seq', 'batch'))
- grad_down: float32 [3072, 768], P(('seq', 'batch'))
Inputs may be any that keep to these rules, and one draw needn't show every extreme that they name: For query block b of a sequence the 16 entries of selection are distinct and exactly min(b, 16) of them are below b.
All inputs are finite; a program needn't handle non-finite values.
Results may differ from a plain program's by a relative error of at most 0.01.
Values may be sent and summed in bfloat16 or wider, within the bound.
No kernel may reach another device: no remote copies, remote signals or barrier semaphores. Data moves between devices by JAX's collectives and lax.ppermute only.
A program may use at most 192 MiB of HBM per device.

v0:
```python
from functools import partial

import jax
import jax.numpy as jnp
from jax import lax
from jax.sharding import PartitionSpec as P

HEADS = 12
HEAD = 64
BLOCK = 64
TOPK = 16


def from_behind(block, axis, distance):
    devices = range(lax.axis_size(axis))
    route = [(i - distance, i) for i in devices if i - distance in devices]
    return lax.ppermute(block, axis, route)


def norm_apply(values, norm_gain, offset):
    center = values - jnp.mean(values, axis=-1, keepdims=True)
    spread = jnp.mean(center * center, axis=-1, keepdims=True)
    return center * lax.rsqrt(spread + 1e-05) * norm_gain + offset


def contract_rows(left_side, right_side):
    return lax.dot_general(
        left_side, right_side, (((0,), (0,)), ((), ())), preferred_element_type=jnp.float32
    )


def contract_cols(left_side, right_side):
    return lax.dot_general(
        left_side, right_side, (((1,), (1,)), ((), ())), preferred_element_type=jnp.float32
    )


def window_pairs(extended, blocks):
    pieces = extended.reshape(blocks + 1, BLOCK, extended.shape[-1])
    return jnp.concatenate([pieces[:-1], pieces[1:]], 1).reshape(blocks, 2 * BLOCK, HEADS, HEAD)


def unpair(paired, blocks):
    flattened = paired.reshape(blocks, 2, BLOCK, HEADS * HEAD)
    front_part = jnp.pad(
        flattened[:, 0].reshape(blocks * BLOCK, HEADS * HEAD), ((0, BLOCK), (0, 0))
    )
    back_part = jnp.pad(flattened[:, 1].reshape(blocks * BLOCK, HEADS * HEAD), ((BLOCK, 0), (0, 0)))
    return front_part + back_part


def masked_scores(query4, keys_win, key_pick, allowed):
    near_scores = jnp.einsum(
        "bqhe,bkhe->bhqk", query4, keys_win, preferred_element_type=jnp.float32
    )
    far_scores = jnp.einsum("bqhe,bshe->bhqs", query4, key_pick, preferred_element_type=jnp.float32)
    scores = jnp.concatenate([near_scores, far_scores], -1) * HEAD ** (-0.5)
    return jnp.where(allowed, scores, -1e30)


def local(
    inputs, selection, cotangent, ln1_gain, ln1_bias, w_qkv, w_out, ln2_gain, ln2_bias, w_up, w_down
):
    shards = (ln1_gain, ln1_bias, w_qkv, w_out, ln2_gain, ln2_bias, w_up, w_down)
    gathered = (
        lax.all_gather(shards[0], ("seq", "batch"), axis=0, tiled=True),
        lax.all_gather(shards[1], ("seq", "batch"), axis=0, tiled=True),
        lax.all_gather(shards[2], ("seq", "batch"), axis=0, tiled=True),
        lax.all_gather(shards[3], ("seq", "batch"), axis=0, tiled=True),
        lax.all_gather(shards[4], ("seq", "batch"), axis=0, tiled=True),
        lax.all_gather(shards[5], ("seq", "batch"), axis=0, tiled=True),
        lax.all_gather(shards[6], ("seq", "batch"), axis=0, tiled=True),
        lax.all_gather(shards[7], ("seq", "batch"), axis=0, tiled=True),
    )
    gain_one, bias_one, mat_qkv, mat_out, gain_two, bias_two, mat_up, mat_down = gathered
    gain_one = gain_one.astype(jnp.float32)
    bias_one = bias_one.astype(jnp.float32)
    gain_two = gain_two.astype(jnp.float32)
    bias_two = bias_two.astype(jnp.float32)
    tokens = inputs[0].astype(jnp.float32)
    chosen = selection[0]
    row_count = tokens.shape[0]
    model_width = tokens.shape[1]
    blocks_here = row_count // BLOCK
    score_scale = HEAD ** (-0.5)
    normed = norm_apply(tokens, gain_one, bias_one).astype(jnp.bfloat16)
    mixed = jnp.dot(normed, mat_qkv, preferred_element_type=jnp.float32).astype(jnp.bfloat16)
    queries = mixed[:, :model_width]
    keys_loc = mixed[:, model_width : 2 * model_width]
    values_loc = mixed[:, 2 * model_width :]
    pooled_keys = jnp.mean(
        keys_loc.reshape(blocks_here, BLOCK, model_width).astype(jnp.float32), axis=1
    ).astype(jnp.bfloat16)
    pooled_values = jnp.mean(
        values_loc.reshape(blocks_here, BLOCK, model_width).astype(jnp.float32), axis=1
    ).astype(jnp.bfloat16)
    halo_k, halo_v = from_behind((keys_loc[-BLOCK:], values_loc[-BLOCK:]), "seq", 1)
    all_keys, all_values = (
        lax.all_gather(pooled_keys, "seq", axis=0, tiled=True),
        lax.all_gather(pooled_values, "seq", axis=0, tiled=True),
    )
    block_ids = lax.axis_index("seq") * blocks_here + jnp.arange(blocks_here, dtype=jnp.int32)
    query_pos = block_ids[:, None] * BLOCK + jnp.arange(BLOCK, dtype=jnp.int32)[None, :]
    key_pos = (block_ids[:, None] - 1) * BLOCK + jnp.arange(2 * BLOCK, dtype=jnp.int32)[None, :]
    near_allowed = (
        (key_pos[:, None, :] <= query_pos[:, :, None])
        & (key_pos[:, None, :] > query_pos[:, :, None] - BLOCK)
        & (key_pos[:, None, :] >= 0)
    )
    far_allowed = jnp.broadcast_to(
        (chosen < block_ids[:, None])[:, None, :], (blocks_here, BLOCK, TOPK)
    )
    allowed = jnp.concatenate([near_allowed, far_allowed], -1)[:, None]
    query4 = queries.reshape(blocks_here, BLOCK, HEADS, HEAD)
    keys_win = window_pairs(jnp.concatenate([halo_k, keys_loc], 0), blocks_here)
    values_win = window_pairs(jnp.concatenate([halo_v, values_loc], 0), blocks_here)
    key_pick = all_keys[chosen].reshape(blocks_here, TOPK, HEADS, HEAD)
    value_pick = all_values[chosen].reshape(blocks_here, TOPK, HEADS, HEAD)
    masked = masked_scores(query4, keys_win, key_pick, allowed)
    row_max = jnp.max(masked, axis=-1, keepdims=True)
    log_total = row_max + jnp.log(jnp.sum(jnp.exp(masked - row_max), axis=-1, keepdims=True))
    attn_probs = jnp.exp(masked - log_total).astype(jnp.bfloat16)
    attended = jnp.einsum(
        "bhqk,bkhe->bqhe",
        attn_probs[..., : 2 * BLOCK],
        values_win,
        preferred_element_type=jnp.float32,
    )
    attended = attended + jnp.einsum(
        "bhqs,bshe->bqhe",
        attn_probs[..., 2 * BLOCK :],
        value_pick,
        preferred_element_type=jnp.float32,
    )
    attended = attended.reshape(row_count, model_width).astype(jnp.bfloat16)
    after_attn = tokens + jnp.dot(attended, mat_out, preferred_element_type=jnp.float32)
    normed_two = norm_apply(after_attn, gain_two, bias_two).astype(jnp.bfloat16)
    hidden = jnp.dot(normed_two, mat_up, preferred_element_type=jnp.float32)
    active = jax.nn.gelu(hidden, approximate=True).astype(jnp.bfloat16)
    output = (after_attn + jnp.dot(active, mat_down, preferred_element_type=jnp.float32)).astype(
        jnp.bfloat16
    )
    upstream = cotangent[0].astype(jnp.float32)
    branch_grad = upstream.astype(jnp.bfloat16)
    grad_down = contract_rows(active, branch_grad)
    grad_active = contract_cols(branch_grad, mat_down)
    unused_gelu, gelu_back = jax.vjp(partial(jax.nn.gelu, approximate=True), hidden)
    grad_hidden = gelu_back(grad_active)[0].astype(jnp.bfloat16)
    grad_up = contract_rows(normed_two, grad_hidden)
    grad_normed_two = contract_cols(grad_hidden, mat_up)
    unused_two, norm_two_back = jax.vjp(norm_apply, after_attn, gain_two, bias_two)
    grad_after, grad_gain_two, grad_bias_two = norm_two_back(grad_normed_two)
    grad_after = grad_after + upstream
    after_grad_b = grad_after.astype(jnp.bfloat16)
    grad_out_w = contract_rows(attended, after_grad_b)
    grad_attended = contract_cols(after_grad_b, mat_out).astype(jnp.bfloat16)
    grad_att4 = grad_attended.reshape(blocks_here, BLOCK, HEADS, HEAD)
    again_masked = masked_scores(query4, keys_win, key_pick, allowed)
    probs_full = jnp.exp(again_masked - log_total)
    probs_low = probs_full.astype(jnp.bfloat16)
    grad_probs = jnp.concatenate(
        [
            jnp.einsum(
                "bqhe,bkhe->bhqk", grad_att4, values_win, preferred_element_type=jnp.float32
            ),
            jnp.einsum(
                "bqhe,bshe->bhqs", grad_att4, value_pick, preferred_element_type=jnp.float32
            ),
        ],
        -1,
    )
    row_inner = jnp.sum(grad_probs * probs_full, axis=-1, keepdims=True)
    grad_scores = (probs_full * (grad_probs - row_inner)).astype(jnp.bfloat16)
    near_grad = grad_scores[..., : 2 * BLOCK]
    far_grad = grad_scores[..., 2 * BLOCK :]
    grad_query = jnp.einsum(
        "bhqk,bkhe->bqhe", near_grad, keys_win, preferred_element_type=jnp.float32
    )
    grad_query = (
        grad_query
        + jnp.einsum("bhqs,bshe->bqhe", far_grad, key_pick, preferred_element_type=jnp.float32)
    ) * score_scale
    grad_kwin = (
        jnp.einsum("bhqk,bqhe->bkhe", near_grad, query4, preferred_element_type=jnp.float32)
        * score_scale
    )
    grad_vwin = jnp.einsum(
        "bhqk,bqhe->bkhe",
        probs_low[..., : 2 * BLOCK],
        grad_att4,
        preferred_element_type=jnp.float32,
    )
    grad_kpick = (
        jnp.einsum("bhqs,bqhe->bshe", far_grad, query4, preferred_element_type=jnp.float32)
        * score_scale
    )
    grad_vpick = jnp.einsum(
        "bhqs,bqhe->bshe",
        probs_low[..., 2 * BLOCK :],
        grad_att4,
        preferred_element_type=jnp.float32,
    )
    ext_keys = unpair(grad_kwin, blocks_here)
    ext_values = unpair(grad_vwin, blocks_here)
    flat_index = chosen.reshape(blocks_here * TOPK)
    dense_keys = (
        jnp.zeros((all_keys.shape[0], model_width), jnp.float32)
        .at[flat_index]
        .add(grad_kpick.reshape(blocks_here * TOPK, model_width))
    )
    dense_values = (
        jnp.zeros((all_values.shape[0], model_width), jnp.float32)
        .at[flat_index]
        .add(grad_vpick.reshape(blocks_here * TOPK, model_width))
    )
    own_keys, own_values = (
        lax.psum_scatter(
            dense_keys.astype(jnp.bfloat16), "seq", scatter_dimension=0, tiled=True
        ).astype(jnp.float32),
        lax.psum_scatter(
            dense_values.astype(jnp.bfloat16), "seq", scatter_dimension=0, tiled=True
        ).astype(jnp.float32),
    )
    right_keys, right_values = (
        from_behind(ext_keys[:BLOCK].astype(jnp.bfloat16), "seq", -1).astype(jnp.float32),
        from_behind(ext_values[:BLOCK].astype(jnp.bfloat16), "seq", -1).astype(jnp.float32),
    )
    grad_keys = (
        ext_keys[BLOCK:]
        + jnp.pad(right_keys, ((row_count - BLOCK, 0), (0, 0)))
        + jnp.repeat(own_keys / BLOCK, BLOCK, axis=0)
    )
    grad_values = (
        ext_values[BLOCK:]
        + jnp.pad(right_values, ((row_count - BLOCK, 0), (0, 0)))
        + jnp.repeat(own_values / BLOCK, BLOCK, axis=0)
    )
    grad_mixed = jnp.concatenate(
        [grad_query.reshape(row_count, model_width), grad_keys, grad_values], 1
    ).astype(jnp.bfloat16)
    grad_qkv = contract_rows(normed, grad_mixed)
    grad_normed = contract_cols(grad_mixed, mat_qkv)
    unused_one, norm_one_back = jax.vjp(norm_apply, tokens, gain_one, bias_one)
    grad_tokens, grad_gain_one, grad_bias_one = norm_one_back(grad_normed)
    grad_tokens = grad_tokens + grad_after
    local_grads = (
        grad_gain_one,
        grad_bias_one,
        grad_qkv,
        grad_out_w,
        grad_gain_two,
        grad_bias_two,
        grad_up,
        grad_down,
    )
    summed = (
        lax.psum_scatter(local_grads[0], ("seq", "batch"), scatter_dimension=0, tiled=True),
        lax.psum_scatter(local_grads[1], ("seq", "batch"), scatter_dimension=0, tiled=True),
        lax.psum_scatter(local_grads[2], ("seq", "batch"), scatter_dimension=0, tiled=True),
        lax.psum_scatter(local_grads[3], ("seq", "batch"), scatter_dimension=0, tiled=True),
        lax.psum_scatter(local_grads[4], ("seq", "batch"), scatter_dimension=0, tiled=True),
        lax.psum_scatter(local_grads[5], ("seq", "batch"), scatter_dimension=0, tiled=True),
        lax.psum_scatter(local_grads[6], ("seq", "batch"), scatter_dimension=0, tiled=True),
        lax.psum_scatter(local_grads[7], ("seq", "batch"), scatter_dimension=0, tiled=True),
    )
    return (
        output[None],
        grad_tokens[None],
        summed[0],
        summed[1],
        summed[2],
        summed[3],
        summed[4],
        summed[5],
        summed[6],
        summed[7],
    )


def solution(mesh):
    return jax.shard_map(
        local,
        mesh=mesh,
        in_specs=(
            P("batch", "seq", None),
            P("batch", "seq", None),
            P("batch", "seq", None),
            P(("seq", "batch")),
            P(("seq", "batch")),
            P(("seq", "batch"), None),
            P(("seq", "batch"), None),
            P(("seq", "batch")),
            P(("seq", "batch")),
            P(("seq", "batch"), None),
            P(("seq", "batch"), None),
        ),
        out_specs=(
            P("batch", "seq", None),
            P("batch", "seq", None),
            P(("seq", "batch")),
            P(("seq", "batch")),
            P(("seq", "batch"), None),
            P(("seq", "batch"), None),
            P(("seq", "batch")),
            P(("seq", "batch")),
            P(("seq", "batch"), None),
            P(("seq", "batch"), None),
        ),
        check_vma=False,
    )
```

profile of v0, /device:TPU:0, one launch (start us, length us, event | category | flops | bytes accessed | tf_op | source)
XLA Modules:
  0.0 1229.9 jit_solution(10603691324814968905)
XLA Ops:
  16.4 42.4 %all-reduce.15 = (bf16[768]{0:T(1024)(128)(2,1)S(1)}, bf16[768]{0:T(1024)(128)(2,1)S(1)}, bf16[768]{0:T(1024)(128)(2,1)S(1)}, bf16[768]{0:T(1024)(128)(2,1)S(1)}) all-reduce(bf16[768]{0:T(1024)(128)(2,1)S(1)} %dynamic-update-slice.1, bf16[768]{0:T(1024)(128)(2,1)S(1)} %dynamic-update-slice, ...), channel_id=1, replica_groups=mesh['seq'=16,'batch'=2] {'seq','batch'}, use_global_device_ids=true, to_apply=%add.7 | all-reduce | flops 3072 | bytes 12288
  64.5 9.4 all-gather.5.cloned.1.call-done
  89.1 38.1 %all_gather.33 = bf16[256,768]{1,0:T(8,128)(2,1)S(1)} all-gather(bf16[16,768]{1,0:T(8,128)(2,1)S(1)} %multiply_convert_fusion.4), channel_id=1, replica_groups=mesh['seq'=16,'batch'=2] {'seq'}, dimensions={0}, use_global_device_ids=true | all-gather | bytes 417792 | tf_op jit(solution)/shard_map/all_gather | solution.py:99
  150.5 41.5 %all_gather.34 = bf16[256,768]{1,0:T(8,128)(2,1)S(1)} all-gather(bf16[16,768]{1,0:T(8,128)(2,1)S(1)} %multiply_convert_fusion.3), channel_id=1, replica_groups=mesh['seq'=16,'batch'=2] {'seq'}, dimensions={0}, use_global_device_ids=true | all-gather | bytes 417792 | tf_op jit(solution)/shard_map/all_gather | solution.py:100
  286.1 11.2 fusion.101
  297.3 14.3 %fusion.7 = bf16[1024,3072]{1,0:T(8,128)(2,1)S(1)} fusion(f32[1024,3072]{1,0:T(8,128)} %fusion.101, bf16[3072,768]{1,0:T(8,128)(2,1)} %all-gather.11.cloned.1.call-done, bf16[1,1024,768]{2,1,0:T(8,128)(2,1)S(1)} %copy-done.32), kind=kOutput, calls=%fused_computation.13 | convolution fusion | flops 4894752768 | bytes 25165824 | tf_op jit(solution)/shard_map/dot_general | solution.py:33
  358.7 73.1 %multiply_convert_fusion = bf16[16,12,64,144]{3,2,1,0:T(8,128)(2,1)} fusion(f32[16,12,64,16]{3,2,1,0:T(8,128)} %fusion.74, f32[16,12,64,128]{3,2,1,0:T(8,128)} %fusion.82, f32[16,12,64]{2,1,0:T(8,128)S(1)} %log_add_fusion, f32[16,12,64,16]{3,2,1,0:T(8,128)S(1)} %bitcast.121, f32[16,12,64,128]{3,2,1,0:T(8,128)S(1)} %bitcast.123, ...), kind=kOutput, calls=%fused_computation.17 | output fusion | flops 24785040 | bytes 17891328 | tf_op jit(solution)/shard_map/sub | solution.py:173
  466.7 13.3 %reshape.319 = f32[16,2,64,768]{2,1,3,0:T(2,128)} reshape(f32[16,128,12,64]{1,3,2,0:T(8,128)} %multiply_bitcast_fusion) | data formatting | bytes 12582912 | tf_op jit(solution)/shard_map/reshape | solution.py:44
  480.1 16.9 %fusion.105 = (f32[16,1,64,768]{2,1,3,0:T(1,128)}, f32[16,1,64,768]{2,1,3,0:T(1,128)}) fusion(f32[16,2,64,768]{2,1,3,0:T(2,128)} %reshape.319), kind=kLoop, calls=%fused_computation.157 | loop fusion | bytes 12582912 | tf_op jit(solution)/shard_map/slice | solution.py:48
  513.6 15.1 %copy.185 = f32[16,1,64,768]{3,2,0,1:T(8,128)} copy(f32[16,1,64,768]{2,1,3,0:T(1,128)} %get-tuple-element.66) | data formatting | bytes 6291456 | tf_op jit(solution)/shard_map/slice | solution.py:48
  532.2 15.1 %copy.183 = f32[16,1,64,768]{3,2,0,1:T(8,128)} copy(f32[16,1,64,768]{2,1,3,0:T(1,128)} %get-tuple-element.67) | data formatting | bytes 6291456 | tf_op jit(solution)/shard_map/slice | solution.py:46
  558.8 13.9 %reshape.322 = f32[16,2,64,768]{2,1,3,0:T(2,128)} reshape(f32[16,128,12,64]{1,3,2,0:T(8,128)} %fusion.53) | data formatting | bytes 12582912 | tf_op jit(solution)/shard_map/reshape | solution.py:44
  575.6 14.9 %fusion.106 = (f32[16,1,64,768]{2,1,3,0:T(1,128)}, f32[16,1,64,768]{2,1,3,0:T(1,128)}) fusion(f32[16,2,64,768]{2,1,3,0:T(2,128)} %reshape.322), kind=kLoop, calls=%fused_computation.158 | loop fusion | bytes 12582912 | tf_op jit(solution)/shard_map/slice | solution.py:48
  590.6 15.1 %copy.194 = f32[16,1,64,768]{3,2,0,1:T(8,128)} copy(f32[16,1,64,768]{2,1,3,0:T(1,128)} %get-tuple-element.68) | data formatting | bytes 6291456 | tf_op jit(solution)/shard_map/slice | solution.py:48
  608.0 15.3 %copy.192 = f32[16,1,64,768]{3,2,0,1:T(8,128)} copy(f32[16,1,64,768]{2,1,3,0:T(1,128)} %get-tuple-element.69) | data formatting | bytes 6291456 | tf_op jit(solution)/shard_map/slice | solution.py:46
  640.7 69.3 %reduce-scatter.9.cloned.1.call-done = bf16[16,768]{1,0:T(8,128)(2,1)} async-done(((bf16[256,768]{1,0:T(8,128)(2,1)}), bf16[16,768]{1,0:T(8,128)(2,1)}) %reduce-scatter.9.cloned.1.call-update) | async-done | bytes 24592 | tf_op jit(solution)/shard_map/reduce_scatter | solution.py:220
  728.0 12.4 %fusion.65 = f32[3072,768]{1,0:T(8,128)} fusion(bf16[1,1024,768]{2,1,0:T(8,128)(2,1)S(1)} %copy-done.33, f32[1024,3072]{1,0:T(8,128)} %fusion.101), kind=kOutput, calls=%fused_computation.95 | convolution fusion | flops 4860149760 | bytes 23592960 | tf_op jit(solution)/shard_map/dot_general | solution.py:27
  741.1 10.7 fusion.100
  751.9 10.9 fusion.73
  764.3 9.0 fusion.110
  781.0 40.6 %all-reduce.14 = (f32[768]{0:T(1024)S(1)}, f32[768]{0:T(1024)S(1)}, f32[768]{0:T(1024)S(1)}, f32[768]{0:T(1024)S(1)}) all-reduce(f32[768]{0:T(1024)S(1)} %get-tuple-element.52, f32[768]{0:T(1024)S(1)} %get-tuple-element.79, f32[768]{0:T(1024)S(1)} %copy-done.61, ...), channel_id=4, replica_groups=mesh['seq'=16,'batch'=2] {'seq','batch'}, use_global_device_ids=true, to_apply=%region_18.19.clone | all-reduce | flops 3072 | bytes 24576
  833.6 105.9 %reduce-scatter.11.cloned.1.call-done = f32[24,2304]{1,0:T(8,128)} async-done(((f32[768,2304]{1,0:T(8,128)}), f32[24,2304]{1,0:T(8,128)}) %reduce-scatter.11.cloned.1.call-update) | async-done | bytes 221200 | tf_op jit(solution)/shard_map/reduce_scatter | solution.py:259
  939.5 141.4 %reduce-scatter.17.cloned.1.call-done = f32[96,768]{1,0:T(8,128)} async-done(((f32[3072,768]{1,0:T(8,128)}), f32[96,768]{1,0:T(8,128)}) %reduce-scatter.17.cloned.1.call-update) | async-done | bytes 294928 | tf_op jit(solution)/shard_map/reduce_scatter | solution.py:264
  1080.9 142.0 %reduce-scatter.15.cloned.1.call-done = f32[24,3072]{1,0:T(8,128)} async-done(((f32[768,3072]{1,0:T(8,128)}), f32[24,3072]{1,0:T(8,128)}) %reduce-scatter.15.cloned.1.call-update) | async-done | bytes 294928 | tf_op jit(solution)/shard_map/reduce_scatter | solution.py:263
  (305 shorter events, 322.9 us)
Async XLA Ops:
  7.2 66.7 %all-gather.5.cloned.1.call-start = ((), (), s32[]{:S(2)}) async-start(), calls=%async_computation.6 | async-start | bytes 3649536 | tf_op jit(solution)/shard_map/all_gather | solution.py:68
  7.9 272.1 %all-gather.7.cloned.1.call-start = ((), (), s32[]{:S(2)}) async-start(), calls=%async_computation.7 | async-start | bytes 1216512 | tf_op jit(solution)/shard_map/all_gather | solution.py:69
  8.7 277.4 %all-gather.9.cloned.1.call-start = ((), (), s32[]{:S(2)}) async-start(), calls=%async_computation.8 | async-start | bytes 4866048 | tf_op jit(solution)/shard_map/all_gather | solution.py:72
  9.4 287.9 %all-gather.11.cloned.1.call-start = ((), (), s32[]{:S(2)}) async-start(), calls=%async_computation.9 | async-start | bytes 4866048 | tf_op jit(solution)/shard_map/all_gather | solution.py:73
  10.0 619.3 %reduce-scatter.7.cloned.1.call-start = ((), (), s32[]{:S(2)}) async-start(), calls=%async_computation.10 | async-start | bytes 417792 | tf_op jit(solution)/shard_map/reduce_scatter | solution.py:217
  58.8 267.4 %copy-start.43 = (f32[768]{0:T(1024)}, f32[768]{0:T(1024)S(1)}, u32[]{:S(2)}) copy-start(f32[768]{0:T(1024)S(1)} %convert_element_type.122) | copy-start | bytes 9220
  58.8 227.3 %copy-start.47 = (f32[768]{0:T(1024)}, f32[768]{0:T(1024)S(1)}, u32[]{:S(2)}) copy-start(f32[768]{0:T(1024)S(1)} %convert_element_type.123) | copy-start | bytes 9220
  61.1 19.2 %copy-start.49 = (f32[1024]{0:T(1024)}, f32[1024]{0:T(1024)S(1)}, u32[]{:S(2)}) copy-start(f32[1024]{0:T(1024)S(1)} %broadcast_multiply_fusion.1) | copy-start | bytes 12292
  61.6 18.7 %copy-start.55 = (f32[1024]{0:T(1024)}, f32[1024]{0:T(1024)S(1)}, u32[]{:S(2)}) copy-start(f32[1024]{0:T(1024)S(1)} %fusion.33) | copy-start | bytes 12292
  81.1 134.7 %collective-permute-start = (bf16[64,768]{1,0:T(8,128)(2,1)}, bf16[64,768]{1,0:T(8,128)(2,1)}, u32[]{:S(2)}, u32[]{:S(2)}) collective-permute-start(bf16[64,768]{1,0:T(8,128)(2,1)} %get-tuple-element.70), channel_id=1, source_target_pairs={{0,2},{2,4},{4,6},{6,8},{8,10},{10,12},{12,14},{14,16},{16,18},{18... | collective-permute-start | bytes 294920 | tf_op jit(solution)/shard_map/ppermute | solution.py:17
  85.0 130.7 %collective-permute-start.1 = (bf16[64,768]{1,0:T(8,128)(2,1)}, bf16[64,768]{1,0:T(8,128)(2,1)}, u32[]{:S(2)}, u32[]{:S(2)}) collective-permute-start(bf16[64,768]{1,0:T(8,128)(2,1)} %get-tuple-element.71), channel_id=1, source_target_pairs={{0,2},{2,4},{4,6},{6,8},{8,10},{10,12},{12,14},{14,16},{16,18},{18... | collective-permute-start | bytes 294920 | tf_op jit(solution)/shard_map/ppermute | solution.py:17
  283.4 42.8 %copy-start.41 = (f32[1024]{0:T(1024)}, f32[1024]{0:T(1024)S(1)}, u32[]{:S(2)}) copy-start(f32[1024]{0:T(1024)S(1)} %broadcast_multiply_fusion) | copy-start | bytes 12292
  286.0 40.2 %copy-start.45 = (f32[1024]{0:T(1024)}, f32[1024]{0:T(1024)S(1)}, u32[]{:S(2)}) copy-start(f32[1024]{0:T(1024)S(1)} %fusion.90) | copy-start | bytes 12292
  358.7 73.1 %copy-start.2 = (bf16[16,64,12,64]{1,3,2,0:T(8,128)(2,1)S(1)}, bf16[16,64,12,64]{1,3,2,0:T(8,128)(2,1)}, u32[]{:S(2)}) copy-start(bf16[16,64,12,64]{1,3,2,0:T(8,128)(2,1)} %copy-done.1) | copy-start | bytes 4718596
  466.7 243.3 %reduce-scatter.9.cloned.1.call-start = ((), (), s32[]{:S(2)}) async-start(), calls=%async_computation.11 | async-start | bytes 417792 | tf_op jit(solution)/shard_map/reduce_scatter | solution.py:220
  551.8 83.9 %collective-permute-start.2 = (bf16[64,768]{0,1:T(8,128)(2,1)S(1)}, bf16[64,768]{0,1:T(8,128)(2,1)}, u32[]{:S(2)}, u32[]{:S(2)}) collective-permute-start(bf16[64,768]{0,1:T(8,128)(2,1)S(1)} %fusion.84), channel_id=1, source_target_pairs={{2,0},{4,2},{6,4},{8,6},{10,8},{12,10},{14,12},{16,14},{18,16},{20... | collective-permute-start | bytes 294920 | tf_op jit(solution)/shard_map/ppermute | solution.py:17
  553.1 280.5 %reduce-scatter.13.cloned.1.call-start = ((), (), s32[]{:S(2)}) async-start(), calls=%async_computation.13 | async-start | bytes 2433024 | tf_op jit(solution)/shard_map/reduce_scatter | solution.py:260
  575.6 363.9 %reduce-scatter.11.cloned.1.call-start = ((), (), s32[]{:S(2)}) async-start(), calls=%async_computation.12 | async-start | bytes 7299072 | tf_op jit(solution)/shard_map/reduce_scatter | solution.py:259
  608.0 18.9 %copy-start.15 = (f32[1024,768]{0,1:T(8,128)}, f32[1024,768]{0,1:T(8,128)S(1)}, u32[]{:S(2)}) copy-start(f32[1024,768]{0,1:T(8,128)S(1)} %copy.195) | copy-start | bytes 9437188
  627.9 85.5 %collective-permute-start.3 = (bf16[64,768]{0,1:T(8,128)(2,1)S(1)}, bf16[64,768]{0,1:T(8,128)(2,1)}, u32[]{:S(2)}, u32[]{:S(2)}) collective-permute-start(bf16[64,768]{0,1:T(8,128)(2,1)S(1)} %fusion.83), channel_id=1, source_target_pairs={{2,0},{4,2},{6,4},{8,6},{10,8},{12,10},{14,12},{16,14},{18,16},{20... | collective-permute-start | bytes 294920 | tf_op jit(solution)/shard_map/ppermute | solution.py:17
  726.6 354.3 %reduce-scatter.17.cloned.1.call-start = ((), (), s32[]{:S(2)}) async-start(), calls=%async_computation.15 | async-start | bytes 9732096 | tf_op jit(solution)/shard_map/reduce_scatter | solution.py:264
  740.4 482.4 %reduce-scatter.15.cloned.1.call-start = ((), (), s32[]{:S(2)}) async-start(), calls=%async_computation.14 | async-start | bytes 9732096 | tf_op jit(solution)/shard_map/reduce_scatter | solution.py:263
  779.5 44.5 %copy-start.22 = (bf16[1,1024,768]{1,2,0:T(8,128)(2,1)S(1)}, bf16[1,1024,768]{1,2,0:T(8,128)(2,1)}, u32[]{:S(2)}) copy-start(bf16[1,1024,768]{1,2,0:T(8,128)(2,1)} %copy.172) | copy-start | bytes 4718596
  779.5 44.5 %copy-start.60 = (f32[1024]{0:T(1024)S(1)}, f32[1024]{0:T(1024)}, u32[]{:S(2)}) copy-start(f32[1024]{0:T(1024)} %copy-done.59) | copy-start | bytes 12292
  (63 other events, 388.0 us)
Sparse Core Ops, SparseCore 0:
  10.9 62.9 all-gather.4
  76.8 53.8 all-gather.6
  133.6 63.4 all-gather.8
  199.9 62.6 all-gather.10
  466.8 117.1 reduce-scatter.6
  589.3 120.7 reduce-scatter.8
  715.9 98.1 reduce-scatter.12
  821.2 118.2 reduce-scatter.10
  946.0 134.8 reduce-scatter.16
  1088.2 134.5 reduce-scatter.14
where the time goes:
time: 1240 us; the launch traced here: 1230 us
  waiting for transfers between devices  471 us (38%)
  local copies, waits for them, and re-layouts  278 us (22%)
  blocking collectives  163 us (13%)
  matrix products  161 us (13%)
  other arithmetic  131 us (11%)
  between operations  15.3 us (1%)
    reduce_scatter x1, waiting for transfers between devices, local(): lax.psum_scatter(local_grads[6], ('seq', 'batch'), scatter_dimension=0, t...  142 us
    reduce_scatter x1, waiting for transfers between devices, local(): lax.psum_scatter(local_grads[7], ('seq', 'batch'), scatter_dimension=0, t...  141 us
    reduce_scatter x1, waiting for transfers between devices, local(): lax.psum_scatter(local_grads[2], ('seq', 'batch'), scatter_dimension=0, t...  106 us
    unnamed x2, blocking collectives  83 us
    sub x1, other arithmetic, local(): grad_scores = (probs_full * (grad_probs - row_inner)).astype(jnp.bfloat16)  73.1 us
    reduce_scatter x1, waiting for transfers between devices, local(): lax.psum_scatter(dense_values.astype(jnp.bfloat16), 'seq', scatter_dimens...  69.3 us
    slice x4, local copies, waits for them, and re-layouts, unpair(): flattened[:, 1].reshape(blocks * BLOCK, HEADS * HEAD)  62 us
    concatenate x8, local copies, waits for them, and re-layouts, window_pairs(): jnp.concatenate([pieces[:-1], pieces[1:]], 1)  44 us
  transfers between devices with their start and end apart: 14, of which 5 were waited for; matrix products, arithmetic and copies ran while one was open for 32% of the time, Pallas kernels for 0%

commit v1 on v0

v1 whole, which is shorter than its diff:
```python
from functools import partial

import jax
import jax.numpy as jnp
from jax import lax
from jax.experimental import pallas as pl
from jax.experimental.pallas import tpu as pltpu
from jax.sharding import PartitionSpec as P

HEADS = 12
HEAD = 64
BLOCK = 64
TOPK = 16
QUAD = 4 * HEAD
FOLD = BLOCK + TOPK
NEG = -1e30


def dot_nn(a, b):
    return lax.dot_general(a, b, (((1,), (0,)), ((), ())), preferred_element_type=jnp.float32)


def dot_nt(a, b):
    return lax.dot_general(a, b, (((1,), (1,)), ((), ())), preferred_element_type=jnp.float32)


def dot_tn(a, b):
    return lax.dot_general(a, b, (((0,), (0,)), ((), ())), preferred_element_type=jnp.float32)


def spread_heads(rows):
    lane = lax.broadcasted_iota(jnp.int32, rows.shape, 1) // HEAD
    zero = jnp.zeros_like(rows)
    return jnp.concatenate([jnp.where(lane == h, rows, zero) for h in range(4)], 0)


def gather_heads(full):
    lane = lax.broadcasted_iota(jnp.int32, (BLOCK, QUAD), 1) // HEAD
    out = full[:BLOCK]
    for h in range(1, 4):
        out = jnp.where(lane == h, full[h * BLOCK : (h + 1) * BLOCK], out)
    return out


def prev_side():
    k = lax.broadcasted_iota(jnp.int32, (BLOCK, QUAD), 0)
    q = lax.broadcasted_iota(jnp.int32, (BLOCK, QUAD), 1) % BLOCK
    return k > q


def unfold(near, far, prev):
    zero = jnp.zeros_like(near)
    both = [jnp.where(prev, near, zero), jnp.where(prev, zero, near), far]
    return jnp.concatenate(both, 0).astype(jnp.bfloat16)


def attend_kernel(
    first_ref, sel_ref, bias_ref, pool_ref, prev_ref, cur_ref, att_ref, probs_ref, picks_ref
):
    c = pl.program_id(0)
    width = HEADS * HEAD

    @pl.when(c == 0)
    def _():
        pool_rows = pool_ref.shape[0]
        ids = lax.broadcasted_iota(jnp.int32, (sel_ref.shape[0], pool_rows), 1)
        one_hot = (ids == sel_ref[...]).astype(jnp.float32).astype(jnp.bfloat16)
        picks_ref[...] = dot_nn(one_hot, pool_ref[:, width:]).astype(jnp.bfloat16)

    prev = prev_side()
    edge = jnp.where((c == 0) & (first_ref[0] == 1), NEG, 0.0)
    picked = picks_ref[pl.ds(pl.multiple_of(c * TOPK, TOPK), TOPK), :]
    for g in range(HEADS // 4):
        lanes = slice(g * QUAD, (g + 1) * QUAD)
        klanes = slice(width + g * QUAD, width + (g + 1) * QUAD)
        vlanes = slice(2 * width + g * QUAD, 2 * width + (g + 1) * QUAD)
        plk = slice(g * QUAD, (g + 1) * QUAD)
        plv = slice(width + g * QUAD, width + (g + 1) * QUAD)
        keys = jnp.concatenate([prev_ref[:, klanes], cur_ref[:, klanes], picked[:, plk]], 0)
        values = jnp.concatenate([prev_ref[:, vlanes], cur_ref[:, vlanes], picked[:, plv]], 0)
        wide_q = spread_heads(cur_ref[:, lanes])
        scores = dot_nt(keys, wide_q) * HEAD ** (-0.5)
        near = jnp.where(prev, scores[:BLOCK] + edge, scores[BLOCK : 2 * BLOCK])
        far = scores[2 * BLOCK :] + bias_ref[...]
        folded = jnp.concatenate([near, far], 0)
        top = jnp.max(folded, axis=0, keepdims=True)
        weights = jnp.exp(folded - top)
        probs = weights * (1.0 / jnp.sum(weights, axis=0, keepdims=True))
        probs_ref[0, g] = probs
        full = unfold(probs[:BLOCK], probs[BLOCK:], prev)
        att_ref[:, lanes] = gather_heads(dot_tn(full, values)).astype(jnp.bfloat16)


def attend(mixed, sel_col, bias_col, first, blocks, pool_rows):
    width = HEADS * HEAD
    base = pool_rows // BLOCK
    return pl.pallas_call(
        attend_kernel,
        grid_spec=pltpu.PrefetchScalarGridSpec(
            num_scalar_prefetch=1,
            grid=(blocks,),
            in_specs=[
                pl.BlockSpec((blocks * TOPK, 1), lambda c, f: (0, 0)),
                pl.BlockSpec((TOPK, 1), lambda c, f: (c, 0)),
                pl.BlockSpec((pool_rows, 3 * width), lambda c, f: (0, 0)),
                pl.BlockSpec((BLOCK, 3 * width), lambda c, f: (base + c, 0)),
                pl.BlockSpec((BLOCK, 3 * width), lambda c, f: (base + c + 1, 0)),
            ],
            out_specs=[
                pl.BlockSpec((BLOCK, width), lambda c, f: (c, 0)),
                pl.BlockSpec((1, HEADS // 4, FOLD, QUAD), lambda c, f: (c, 0, 0, 0)),
                pl.BlockSpec((blocks * TOPK, 2 * width), lambda c, f: (0, 0)),
            ],
        ),
        out_shape=[
            jax.ShapeDtypeStruct((blocks * BLOCK, width), jnp.bfloat16),
            jax.ShapeDtypeStruct((blocks, HEADS // 4, FOLD, QUAD), jnp.float32),
            jax.ShapeDtypeStruct((blocks * TOPK, 2 * width), jnp.bfloat16),
        ],
        compiler_params=pltpu.CompilerParams(vmem_limit_bytes=32 * 1024 * 1024),
        name="attend",
    )(first, sel_col, bias_col, mixed, mixed, mixed)


def attend_back_kernel(
    blocks, sel_ref, prev_ref, cur_ref, picks_ref, probs_ref, datt_ref, out_ref, carry, dpicks
):
    i = pl.program_id(0)
    width = HEADS * HEAD

    @pl.when(i == 0)
    def _():
        carry[...] = jnp.zeros_like(carry)

    @pl.when(i < blocks)
    def _():
        prev = prev_side()
        row = pl.multiple_of(i * TOPK, TOPK)
        for g in range(HEADS // 4):
            lanes = slice(g * QUAD, (g + 1) * QUAD)
            klanes = slice(width + g * QUAD, width + (g + 1) * QUAD)
            vlanes = slice(2 * width + g * QUAD, 2 * width + (g + 1) * QUAD)
            keys = jnp.concatenate([prev_ref[:, klanes], cur_ref[:, klanes], picks_ref[:, lanes]], 0)
            values = jnp.concatenate(
                [prev_ref[:, vlanes], cur_ref[:, vlanes], picks_ref[:, klanes]], 0
            )
            wide_q = spread_heads(cur_ref[:, lanes])
            wide_d = spread_heads(datt_ref[:, lanes])
            probs = probs_ref[0, g]
            dprobs = dot_nt(values, wide_d)
            near = jnp.where(prev, dprobs[:BLOCK], dprobs[BLOCK : 2 * BLOCK])
            folded = jnp.concatenate([near, dprobs[2 * BLOCK :]], 0)
            inner = jnp.sum(probs * folded, axis=0, keepdims=True)
            dscores = probs * (folded - inner) * HEAD ** (-0.5)
            full_p = unfold(probs[:BLOCK], probs[BLOCK:], prev)
            full_d = unfold(dscores[:BLOCK], dscores[BLOCK:], prev)
            dvals = dot_nn(full_p, wide_d)
            dkeys = dot_nn(full_d, wide_q)
            dq = gather_heads(dot_tn(full_d, keys))
            out_ref[:, lanes] = carry[:, lanes].astype(jnp.bfloat16)
            out_ref[:, klanes] = (carry[:, klanes] + dkeys[:BLOCK]).astype(jnp.bfloat16)
            out_ref[:, vlanes] = (carry[:, vlanes] + dvals[:BLOCK]).astype(jnp.bfloat16)
            carry[:, lanes] = dq
            carry[:, klanes] = dkeys[BLOCK : 2 * BLOCK]
            carry[:, vlanes] = dvals[BLOCK : 2 * BLOCK]
            dpicks[pl.ds(row, TOPK), lanes] = dkeys[2 * BLOCK :].astype(jnp.bfloat16)
            dpicks[pl.ds(row, TOPK), klanes] = dvals[2 * BLOCK :].astype(jnp.bfloat16)

    @pl.when(i == blocks)
    def _():
        out_ref[...] = carry[...].astype(jnp.bfloat16)

    @pl.when(i > blocks)
    def _():
        ids = lax.broadcasted_iota(jnp.int32, (BLOCK, blocks * TOPK), 0) + (i - blocks - 1) * BLOCK
        one_hot = (ids == sel_ref[...]).astype(jnp.float32).astype(jnp.bfloat16)
        out_ref[:, :width] = jnp.zeros((BLOCK, width), jnp.bfloat16)
        out_ref[:, width:] = dot_nn(one_hot, dpicks[...]).astype(jnp.bfloat16)


def attend_back(mixed, sel_row, picks, probs, datt, blocks, pool_rows):
    width = HEADS * HEAD
    base = pool_rows // BLOCK
    last = blocks - 1

    def query_block(i):
        return jnp.minimum(i, last)

    return pl.pallas_call(
        partial(attend_back_kernel, blocks),
        grid=(blocks + 1 + base,),
        in_specs=[
            pl.BlockSpec((1, blocks * TOPK), lambda i: (0, 0)),
            pl.BlockSpec((BLOCK, 3 * width), lambda i: (base + query_block(i), 0)),
            pl.BlockSpec((BLOCK, 3 * width), lambda i: (base + query_block(i) + 1, 0)),
            pl.BlockSpec((TOPK, 2 * width), lambda i: (query_block(i), 0)),
            pl.BlockSpec((1, HEADS // 4, FOLD, QUAD), lambda i: (query_block(i), 0, 0, 0)),
            pl.BlockSpec((BLOCK, width), lambda i: (query_block(i), 0)),
        ],
        out_specs=pl.BlockSpec(
            (BLOCK, 3 * width), lambda i: (jnp.where(i > blocks, i - blocks - 1, base + i), 0)
        ),
        out_shape=jax.ShapeDtypeStruct((pool_rows + (blocks + 1) * BLOCK, 3 * width), jnp.bfloat16),
        scratch_shapes=[
            pltpu.VMEM((BLOCK, 3 * width), jnp.float32),
            pltpu.VMEM((blocks * TOPK, 2 * width), jnp.bfloat16),
        ],
        compiler_params=pltpu.CompilerParams(vmem_limit_bytes=32 * 1024 * 1024),
        name="attend_back",
    )(sel_row, mixed, mixed, picks, probs, datt)


def standardize(values):
    center = values - jnp.mean(values, axis=-1, keepdims=True)
    spread = jnp.mean(center * center, axis=-1, keepdims=True)
    scale = lax.rsqrt(spread + 1e-05)
    return center * scale, scale


def standardize_back(unit, scale, dunit):
    return scale * (
        dunit
        - jnp.mean(dunit, axis=-1, keepdims=True)
        - unit * jnp.mean(dunit * unit, axis=-1, keepdims=True)
    )


def shift_seq(value, distance):
    size = lax.axis_size("seq")
    route = [(i - distance, i) for i in range(size) if 0 <= i - distance < size]
    return lax.ppermute(value, "seq", route)


def gather_small(rows):
    size = lax.axis_size("seq")
    return lax.all_to_all(jnp.tile(rows, (size, 1)), "seq", 0, 0, tiled=True)


def scatter_small(rows):
    size = lax.axis_size("seq")
    parts = lax.all_to_all(rows, "seq", 0, 0, tiled=True)
    return jnp.sum(parts.reshape(size, -1, rows.shape[1]).astype(jnp.float32), axis=0)


BOTH = ("seq", "batch")


def local(
    inputs, selection, cotangent, ln1_gain, ln1_bias, w_qkv, w_out, ln2_gain, ln2_bias, w_up, w_down
):
    bf16, f32 = jnp.bfloat16, jnp.float32
    tokens_low = inputs[0]
    chosen = selection[0]
    count, width = tokens_low.shape
    blocks = count // BLOCK
    pool_rows = blocks * lax.axis_size("seq")
    at = lax.axis_index("seq")

    vectors = lax.all_gather(
        jnp.stack([ln1_gain, ln1_bias, ln2_gain, ln2_bias]), BOTH, axis=1, tiled=True
    ).astype(f32)
    gain_one, bias_one, gain_two, bias_two = vectors
    mat_qkv = lax.all_gather(w_qkv, BOTH, axis=0, tiled=True)
    mat_out = lax.all_gather(w_out, BOTH, axis=0, tiled=True)
    mat_up = lax.all_gather(w_up, BOTH, axis=0, tiled=True)
    mat_down = lax.all_gather(w_down, BOTH, axis=0, tiled=True)

    tokens = tokens_low.astype(f32)
    unit, unit_scale = standardize(tokens)
    unit_halo, _ = standardize(shift_seq(tokens_low[-BLOCK:], 1).astype(f32))
    unit_pool = gather_small(jnp.mean(unit.reshape(blocks, BLOCK, width), axis=1).astype(bf16))
    unit_ext = jnp.concatenate([unit_pool.astype(f32), unit_halo, unit], 0)
    normed = (unit_ext * gain_one + bias_one).astype(bf16)
    mixed = dot_nn(normed, mat_qkv).astype(bf16)

    block_ids = at * blocks + jnp.arange(blocks, dtype=jnp.int32)
    flat = chosen.reshape(blocks * TOPK)
    far_bias = jnp.where(chosen < block_ids[:, None], 0.0, NEG).reshape(blocks * TOPK, 1)
    first = (at == 0).astype(jnp.int32)[None]
    attended, probs, picks = attend(mixed, flat[:, None], far_bias, first, blocks, pool_rows)

    after = tokens + dot_nn(attended, mat_out)
    unit_two, scale_two = standardize(after)
    normed_two = (unit_two * gain_two + bias_two).astype(bf16)
    hidden = dot_nn(normed_two, mat_up)
    active, gelu_back = jax.vjp(partial(jax.nn.gelu, approximate=True), hidden)
    active = active.astype(bf16)
    output = (after + dot_nn(active, mat_down)).astype(bf16)

    upstream = cotangent[0]
    dhidden = gelu_back(dot_nt(upstream, mat_down))[0].astype(bf16)
    grad_down = dot_tn(active, upstream).astype(bf16)
    grad_up = dot_tn(normed_two, dhidden).astype(bf16)
    dnormed_two = dot_nt(dhidden, mat_up)
    grad_gain_two = jnp.sum(dnormed_two * unit_two, axis=0)
    grad_bias_two = jnp.sum(dnormed_two, axis=0)
    dafter = upstream.astype(f32) + standardize_back(unit_two, scale_two, dnormed_two * gain_two)
    dafter_low = dafter.astype(bf16)
    grad_out = dot_tn(attended, dafter_low).astype(bf16)
    dattended = dot_nt(dafter_low, mat_out).astype(bf16)

    dmixed = attend_back(mixed, flat[None, :], picks, probs, dattended, blocks, pool_rows)
    grad_qkv = dot_tn(normed, dmixed).astype(bf16)
    dnormed = dot_nt(dmixed, mat_qkv)
    grad_gain_one = jnp.sum(dnormed * unit_ext, axis=0)
    grad_bias_one = jnp.sum(dnormed, axis=0)
    from_pool = scatter_small(dnormed[:pool_rows].astype(bf16)) * (1.0 / BLOCK)
    from_next = shift_seq(dnormed[pool_rows : pool_rows + BLOCK].astype(bf16), -1).astype(f32)
    dtoken = (
        dnormed[pool_rows + BLOCK :]
        + jnp.repeat(from_pool, BLOCK, axis=0)
        + jnp.pad(from_next, ((count - BLOCK, 0), (0, 0)))
    )
    input_grad = dafter + standardize_back(unit, unit_scale, dtoken * gain_one)

    columns = jnp.stack([grad_gain_one, grad_bias_one, grad_gain_two, grad_bias_two], 1)
    columns = jnp.pad(columns.astype(bf16), ((0, 0), (0, 124)))

    def scatter(value):
        return lax.psum_scatter(value, BOTH, scatter_dimension=0, tiled=True).astype(f32)

    own_down = scatter(grad_down)
    own_up = scatter(grad_up)
    own_qkv = scatter(jnp.concatenate([grad_qkv, grad_out, columns], 1))
    split = 3 * width
    tail = own_qkv[:, split + width :]
    return (
        output[None],
        input_grad[None],
        tail[:, 0],
        tail[:, 1],
        own_qkv[:, :split],
        own_qkv[:, split : split + width],
        tail[:, 2],
        tail[:, 3],
        own_up,
        own_down,
    )


def solution(mesh):
    tokens = P("batch", "seq", None)
    vector = P(BOTH)
    matrix = P(BOTH, None)
    return jax.shard_map(
        local,
        mesh=mesh,
        in_specs=(
            tokens,
            tokens,
            tokens,
            vector,
            vector,
            matrix,
            matrix,
            vector,
            vector,
            matrix,
            matrix,
        ),
        out_specs=(
            tokens,
            tokens,
            vector,
            vector,
            matrix,
            matrix,
            vector,
            vector,
            matrix,
            matrix,
        ),
        check_vma=False,
    )
```

time: 1240 us -> 631 us (0.51)
  local copies, waits for them, and re-layouts: 278 us -> 54 us
  waiting for transfers between devices: 471 us -> 336 us
  blocking collectives: 163 us -> 40.5 us
  other arithmetic: 131 us -> 32.2 us
  matrix products: 161 us -> 98 us
  Pallas kernels: 0 us -> 32.1 us
    reduce_scatter x6 -> x2, waiting for transfers between devices: 459 us -> 88.1 us  [scatter(): lax.psum_scatter(value, BOTH, scatter_dimension=0, tiled=True).astype(f32)]
    all_gather x4, waiting for transfers between devices: 9.42 us -> 137 us  [the longest x1 60.1 us: local(): mat_up = lax.all_gather(w_up, BOTH, axis=0, tiled=True)]
    unnamed x10 -> x8, waiting for transfers between devices: 2.68 us -> 110 us
    slice x8 -> x7, local copies, waits for them, and re-layouts: 97.4 us -> 6.88 us  [the longest x2 2.08 us: local(): from_pool = scatter_small(dnormed[:pool_rows].astype(bf16)) * (1.0 / BLOCK)]
    unnamed x2 -> x0, blocking collectives: 83 us -> none
    sub x1 -> x0, other arithmetic: 73.1 us -> none  [local(): grad_scores = (probs_full * (grad_probs - row_inner)).astype(jnp.bfloat16)]
    reshape x13 -> x1, local copies, waits for them, and re-layouts: 68.5 us -> 3.72 us  [local(): jnp.repeat(from_pool, BLOCK, axis=0)]
    dot_general x24 -> x12, matrix products: 161 us -> 98 us  [the longest x4 34.3 us: dot_nn(): lax.dot_general(a, b, (((1,), (0,)), ((), ())), preferred_element_type=jn...]
  transfers between devices with their start and end apart: 14 -> 11, of which waited for: 5 -> 6; matrix products, arithmetic and copies ran while one was open for 32% -> 23% of each run, Pallas kernels for 0% -> 5%
where the time goes in v1:
time: 631 us; the launch traced here: 626 us
  waiting for transfers between devices  336 us (53%)
  matrix products  98 us (16%)
  local copies, waits for them, and re-layouts  54 us (9%)
  blocking collectives  40.5 us (6%)
  other arithmetic  32.2 us (5%)
  Pallas kernels  32.1 us (5%)
  starting transfers between devices  18.1 us (3%)
  between operations  14.9 us (2%)
    unnamed x8, waiting for transfers between devices  110 us
    reduce_scatter x2, waiting for transfers between devices, scatter(): lax.psum_scatter(value, BOTH, scatter_dimension=0, tiled=True).astype(f32)  88.1 us
    all_gather x1, waiting for transfers between devices, local(): mat_up = lax.all_gather(w_up, BOTH, axis=0, tiled=True)  60.1 us
    all_gather x1, waiting for transfers between devices, local(): mat_down = lax.all_gather(w_down, BOTH, axis=0, tiled=True)  54 us
    all_gather x1, blocking collectives, local(): lax.all_gather(jnp.stack([ln1_gain, ln1_bias, ln2_gain, ln2_bias]), BOTH,...  40.5 us
    dot_general x4, matrix products, dot_nn(): lax.dot_general(a, b, (((1,), (0,)), ((), ())), preferred_element_type=jn...  34.3 us
    dot_general x4, matrix products, dot_nt(): lax.dot_general(a, b, (((1,), (1,)), ((), ())), preferred_element_type=jn...  32.7 us
    dot_general x4, matrix products, dot_tn(): lax.dot_general(a, b, (((0,), (0,)), ((), ())), preferred_element_type=jn...  31 us
  transfers between devices with their start and end apart: 11, of which 6 were waited for; matrix products, arithmetic and copies ran while one was open for 23% of the time, Pallas kernels for 5%

profile of v1, /device:TPU:0, one launch (start us, length us, event | category | flops | bytes accessed | tf_op | source)
XLA Modules:
  0.0 626.3 jit_solution(712394971325959295)
XLA Ops:
  18.0 8.3 %all-to-all-start = ((bf16[16,16,768]{2,1,0:T(8,128)(2,1)}), bf16[16,16,768]{2,1,0:T(8,128)(2,1)S(1)}, u32[]{:S(2)}, u32[]{:S(2)}) async-start(bf16[16,16,768]{2,1,0:T(8,128)(2,1)} %tile.2), calls=%async_computation | async-start | bytes 786432 | tf_op jit(solution)/shard_map/all_to_all | solution.py:236
  30.7 40.5 %all-gather = bf16[32,24,4]{1,2,0:T(4,128)(2,1)S(1)} all-gather(bf16[1,24,4]{1,2,0:T(4,128)(2,1)S(1)} %maximum_bitcast_fusion), channel_id=1, replica_groups=mesh['seq'=16,'batch'=2] {'seq','batch'}, dimensions={0}, use_global_device_ids=true | all-gather | bytes 6336 | tf_op jit(solution)/shard_map/all_gather | solution.py:259
  74.5 6.0 concatenate.6
  80.4 8.5 %convolution_convert_fusion.pool_ref.prev_ref.cur_ref = bf16[1344,2304]{1,0:T(8,128)(2,1)S(1)} fusion(bf16[768,2304]{1,0:T(8,128)(2,1)} %all-gather.6.cloned.1.call-done, f32[1344,768]{0,1:T(8,128)} %concatenate.6, f32[768]{0:T(1024)S(1)} %get-tuple-element.67, f32[768]{0:T(1024)S(1)} %get-tuple-element.68), kind=kOutput, calls=%fused_computation.10 | convolution fusion | flops 4762533888 | bytes 13867008 | tf_op jit(solution)/shard_map/dot_general | solution.py:20
  89.0 15.0 %attend.1 = (bf16[1024,768]{1,0:T(8,128)(2,1)S(1)}, f32[16,3,80,256]{3,2,1,0:T(8,128)S(1)}, bf16[256,1536]{1,0:T(8,128)(2,1)S(1)}) custom-call(s32[1]{0:T(128)} %bitcast.1.first_ref, s32[256,1]{1,0:T(8,128)S(1)} %broadcast_in_dim_reshape_squeeze.8.sel_ref, f32[256,1]{1,0:T(8,128)S(1)} %compare_select_fusion.bias_ref, ...), custom_call_target="tpu_custom_call" | custom-call | tf_op jit(solution)/shard_map/attend/pallas_call | solution.py:97
  108.4 22.9 %all-gather.8.cloned.1.call-done = bf16[768,768]{1,0:T(8,128)(2,1)} async-done(((bf16[24,768]{1,0:T(8,128)(2,1)}), bf16[768,768]{1,0:T(8,128)(2,1)}) %all-gather.8.cloned.1.call-update) | async-done | bytes 1179664 | tf_op jit(solution)/shard_map/all_gather | solution.py:264
  136.7 60.1 %all-gather.10.cloned.1.call-done = bf16[768,3072]{1,0:T(8,128)(2,1)} async-done(((bf16[24,3072]{1,0:T(8,128)(2,1)}), bf16[768,3072]{1,0:T(8,128)(2,1)}) %all-gather.10.cloned.1.call-update) | async-done | bytes 4718608 | tf_op jit(solution)/shard_map/all_gather | solution.py:265
  196.8 11.2 %fusion.20 = f32[1024,3072]{1,0:T(8,128)} fusion(bf16[768,3072]{1,0:T(8,128)(2,1)} %all-gather.10.cloned.1.call-done, f32[1024,768]{0,1:T(8,128)} %copy-done.7, f32[768]{0:T(1024)S(1)} %get-tuple-element.66, f32[768]{0:T(1024)S(1)} %get-tuple-element.65, f32[1024]{0:T(1024)S(1)} %add_rsqrt_fusion, f32[1024]{0:T(1024)S(1)} %broadcast_multiply_fusion.5), kind=kOutput, calls=%fused_computation.77 | convolution fusion | flops 4835770368 | bytes 20461568 | tf_op jit(solution)/shard_map/dot_general | solution.py:20
  208.0 54.0 %all-gather.12.cloned.1.call-done = bf16[3072,768]{1,0:T(8,128)(2,1)} async-done(((bf16[96,768]{1,0:T(8,128)(2,1)}), bf16[3072,768]{1,0:T(8,128)(2,1)}) %all-gather.12.cloned.1.call-update) | async-done | bytes 4718608 | tf_op jit(solution)/shard_map/all_gather | solution.py:266
  262.0 14.3 %fusion.6 = bf16[1024,3072]{1,0:T(8,128)(2,1)S(1)} fusion(f32[1024,3072]{1,0:T(8,128)} %fusion.20, bf16[3072,768]{1,0:T(8,128)(2,1)} %all-gather.12.cloned.1.call-done, bf16[1,1024,768]{2,1,0:T(8,128)(2,1)S(1)} %copy-done.14), kind=kOutput, calls=%fused_computation.8 | convolution fusion | flops 4894752768 | bytes 25165824 | tf_op jit(solution)/shard_map/dot_general | solution.py:24
  278.9 7.1 %convolution_convert_fusion.2 = bf16[768,3072]{1,0:T(8,128)(2,1)} fusion(bf16[1024,3072]{1,0:T(8,128)(2,1)S(1)} %fusion.6, f32[1024,768]{0,1:T(8,128)S(1)} %copy-done.8, f32[768]{0:T(1024)S(1)} %get-tuple-element.66, f32[768]{0:T(1024)S(1)} %get-tuple-element.65, f32[1024]{0:T(1024)S(1)} %add_rsqrt_fusion, f32[1024]{0:T(1024)S(1)} %broadcast_multiply_fusion.5), kind=kOutput, calls=%fused_computation.14 | convolution fusion | flops 4838129664 | bytes 14170112 | tf_op jit(solution)/shard_map/dot_general | solution.py:28
  287.8 12.1 %convolution_convert_fusion.1 = bf16[3072,768]{1,0:T(8,128)(2,1)} fusion(bf16[1,1024,768]{2,1,0:T(8,128)(2,1)} %param.13, f32[1024,3072]{1,0:T(8,128)} %fusion.20), kind=kOutput, calls=%fused_computation.13 | convolution fusion | flops 4862509056 | bytes 18874368 | tf_op jit(solution)/shard_map/dot_general | solution.py:28
  300.0 10.4 %fusion.24 = (bf16[768]{0:T(1024)(128)(2,1)S(1)}, f32[1024,768]{1,0:T(8,128)}) fusion(bf16[1024,3072]{1,0:T(8,128)(2,1)} %copy-done.26, bf16[768,3072]{1,0:T(8,128)(2,1)} %all-gather.10.cloned.1.call-done), kind=kOutput, calls=%fused_computation.80 | convolution fusion | flops 4832623616 | bytes 14157312 | tf_op jit(solution)/shard_map/dot_general | solution.py:24
  314.0 4.2 multiply_reduce_fusion.1
  324.3 17.1 %attend_back.1 = bf16[1344,2304]{1,0:T(8,128)(2,1)S(1)} custom-call(s32[1,256]{1,0:T(1,128)S(1)} %broadcast_in_dim_reshape_squeeze.7.sel_ref, bf16[1344,2304]{1,0:T(8,128)(2,1)S(1)} %bitcast.58, bf16[1344,2304]{1,0:T(8,128)(2,1)S(1)} %bitcast.58, bf16[256,1536]{1,0:T(8,128)(2,1)S(1)} %get-tuple-element.14.picks_ref, f32[16,3,80,256]{3,2,1,0:T(8,128)S(1)} %copy-done.3, ...), custom_call_target="tpu_custom_call" | custom-call | tf_op jit(solution)/shard_map/attend_back/pallas_call | solution.py:189
  341.5 6.6 %fusion.25 = (bf16[768]{0:T(1024)(128)(2,1)S(1)}, f32[1344,768]{1,0:T(8,128)}) fusion(bf16[1344,2304]{1,0:T(8,128)(2,1)S(1)} %attend_back.1, bf16[768,2304]{1,0:T(8,128)(2,1)S(1)} %copy-done.24), kind=kOutput, calls=%fused_computation.81 | convolution fusion | flops 4757371904 | bytes 13862400 | tf_op jit(solution)/shard_map/dot_general | solution.py:24
  348.0 5.8 copy.90
  353.8 6.8 %multiply_reduce_fusion = (bf16[768]{0:T(1024)(128)(2,1)S(1)}, bf16[1344,768]{0,1:T(8,128)(2,1)}) fusion(f32[1344,768]{0,1:T(8,128)} %copy.90, f32[1344,768]{0,1:T(8,128)} %concatenate.6), kind=kLoop, calls=%fused_computation.17 | loop fusion | flops 3095808 | bytes 10323456 | tf_op jit(solution)/shard_map/reduce_sum | solution.py:305
  364.9 7.9 %convolution_convert_fusion.3 = bf16[768,2304]{1,0:T(8,128)(2,1)S(1)} fusion(bf16[1344,2304]{1,0:T(8,128)(2,1)S(1)} %bitcast.60, f32[1344,768]{0,1:T(8,128)} %concatenate.6, f32[768]{0:T(1024)S(1)} %get-tuple-element.67, f32[768]{0:T(1024)S(1)} %get-tuple-element.68), kind=kOutput, calls=%fused_computation.15 | convolution fusion | flops 4761206784 | bytes 13867008 | tf_op jit(solution)/shard_map/dot_general | solution.py:28
  377.5 4.4 all-to-all-start.1
  382.0 11.3 %fusion.14 = bf16[1,1024,768]{1,2,0:T(8,128)(2,1)} fusion(f32[1024,768]{0,1:T(8,128)S(1)} %copy-done.10, bf16[3072,768]{1,0:T(8,128)(2,1)} %all-gather.12.cloned.1.call-done, f32[1024,3072]{1,0:T(8,128)} %fusion.20), kind=kOutput, calls=%fused_computation.42 | convolution fusion | flops 4861722624 | bytes 22020096 | tf_op jit(solution)/shard_map/dot_general | solution.py:20
  405.4 4.4 fusion.21
  417.7 88.1 %reduce-scatter.8.cloned.1.call-done = bf16[96,768]{1,0:T(8,128)(2,1)} async-done(((bf16[3072,768]{1,0:T(8,128)(2,1)}), bf16[96,768]{1,0:T(8,128)(2,1)}) %reduce-scatter.8.cloned.1.call-update) | async-done | bytes 147472 | tf_op jit(solution)/shard_map/reduce_scatter | solution.py:320
  507.4 107.1 %reduce-scatter.10.cloned.1.call-done = bf16[24,3200]{1,0:T(8,128)(2,1)} async-done(((bf16[768,3200]{1,0:T(8,128)(2,1)}), bf16[24,3200]{1,0:T(8,128)(2,1)}) %reduce-scatter.10.cloned.1.call-update) | async-done | bytes 153616
  (152 shorter events, 77.5 us)
Async XLA Ops:
  7.2 73.2 %all-gather.6.cloned.1.call-start = ((), (), s32[]{:S(2)}) async-start(), calls=%async_computation.5 | async-start | bytes 3649536 | tf_op jit(solution)/shard_map/all_gather | solution.py:263
  7.9 123.3 %all-gather.8.cloned.1.call-start = ((), (), s32[]{:S(2)}) async-start(), calls=%async_computation.6 | async-start | bytes 1216512 | tf_op jit(solution)/shard_map/all_gather | solution.py:264
  8.7 188.1 %all-gather.10.cloned.1.call-start = ((), (), s32[]{:S(2)}) async-start(), calls=%async_computation.7 | async-start | bytes 4866048 | tf_op jit(solution)/shard_map/all_gather | solution.py:265
  9.4 252.6 %all-gather.12.cloned.1.call-start = ((), (), s32[]{:S(2)}) async-start(), calls=%async_computation.8 | async-start | bytes 4866048 | tf_op jit(solution)/shard_map/all_gather | solution.py:266
  11.7 59.9 %copy-start.5 = (bf16[1,1024,768]{1,2,0:T(8,128)(2,1)}, bf16[1,1024,768]{1,2,0:T(8,128)(2,1)S(1)}, u32[]{:S(2)}) copy-start(bf16[1,1024,768]{1,2,0:T(8,128)(2,1)S(1)} %copy.78) | copy-start | bytes 4718596
  14.1 57.4 %copy-start.15 = (f32[1024]{0:T(1024)}, f32[1024]{0:T(1024)S(1)}, u32[]{:S(2)}) copy-start(f32[1024]{0:T(1024)S(1)} %broadcast_multiply_fusion.6) | copy-start | bytes 12292
  14.2 16.2 %copy-start.19 = (s32[1,16,16]{2,1,0:T(8,128)S(1)}, s32[1,16,16]{2,1,0:T(8,128)}, u32[]{:S(2)}) copy-start(s32[1,16,16]{2,1,0:T(8,128)} %param.12) | copy-start | bytes 3076
  14.2 16.5 %copy-start.20 = (bf16[24]{0:T(256)(128)(2,1)S(1)}, bf16[24]{0:T(256)(128)(2,1)}, u32[]{:S(2)}) copy-start(bf16[24]{0:T(256)(128)(2,1)} %param.19) | copy-start | bytes 148
  14.2 16.5 %copy-start.21 = (bf16[24]{0:T(256)(128)(2,1)S(1)}, bf16[24]{0:T(256)(128)(2,1)}, u32[]{:S(2)}) copy-start(bf16[24]{0:T(256)(128)(2,1)} %param.18) | copy-start | bytes 148
  14.2 16.5 %copy-start.22 = (bf16[24]{0:T(256)(128)(2,1)S(1)}, bf16[24]{0:T(256)(128)(2,1)}, u32[]{:S(2)}) copy-start(bf16[24]{0:T(256)(128)(2,1)} %param.15) | copy-start | bytes 148
  14.2 16.5 %copy-start.23 = (bf16[24]{0:T(256)(128)(2,1)S(1)}, bf16[24]{0:T(256)(128)(2,1)}, u32[]{:S(2)}) copy-start(bf16[24]{0:T(256)(128)(2,1)} %param.14) | copy-start | bytes 148
  14.7 59.0 %copy-start.17 = (f32[1024]{0:T(1024)}, f32[1024]{0:T(1024)S(1)}, u32[]{:S(2)}) copy-start(f32[1024]{0:T(1024)S(1)} %add_rsqrt_fusion.1) | copy-start | bytes 12292
  18.0 56.1 %all-to-all-start = ((bf16[16,16,768]{2,1,0:T(8,128)(2,1)}), bf16[16,16,768]{2,1,0:T(8,128)(2,1)S(1)}, u32[]{:S(2)}, u32[]{:S(2)}) async-start(bf16[16,16,768]{2,1,0:T(8,128)(2,1)} %tile.2), calls=%async_computation | async-start | bytes 786432 | tf_op jit(solution)/shard_map/all_to_all | solution.py:236
  26.3 389.7 %reduce-scatter.6.cloned.1.call-start = ((), (), s32[]{:S(2)}) async-start(), calls=%async_computation.9 | async-start | bytes 4866048 | tf_op jit(solution)/shard_map/reduce_scatter | solution.py:320
  26.5 47.3 %collective-permute-start = (bf16[64,768]{0,1:T(8,128)(2,1)S(1)}, bf16[64,768]{0,1:T(8,128)(2,1)S(1)}, u32[]{:S(2)}, u32[]{:S(2)}) collective-permute-start(bf16[64,768]{0,1:T(8,128)(2,1)S(1)} %slice_bitcast_fusion), channel_id=1, source_target_pairs={{0,2},{2,4},{4,6},{6,8},{8,10},{10,12},{12,14},{14,16},{16,18},{18... | collective-permute-start | bytes 294920 | tf_op jit(solution)/shard_map/ppermute | solution.py:231
  108.4 26.2 %copy-start.4 = (bf16[1024,768]{1,0:T(8,128)(2,1)}, bf16[1024,768]{1,0:T(8,128)(2,1)S(1)}, u32[]{:S(2)}) copy-start(bf16[1024,768]{1,0:T(8,128)(2,1)S(1)} %get-tuple-element.13) | copy-start | bytes 4718596
  196.8 65.2 %copy-start.14 = (bf16[1,1024,768]{2,1,0:T(8,128)(2,1)S(1)}, bf16[1,1024,768]{2,1,0:T(8,128)(2,1)}, u32[]{:S(2)}) copy-start(bf16[1,1024,768]{2,1,0:T(8,128)(2,1)} %param.13) | copy-start | bytes 4718596
  262.0 16.9 %copy-start.8 = (f32[1024,768]{0,1:T(8,128)S(1)}, f32[1024,768]{0,1:T(8,128)}, u32[]{:S(2)}) copy-start(f32[1024,768]{0,1:T(8,128)} %copy-done.7) | copy-start | bytes 9437188
  286.0 219.8 %reduce-scatter.8.cloned.1.call-start = ((), (), s32[]{:S(2)}) async-start(), calls=%async_computation.10 | async-start | bytes 4866048 | tf_op jit(solution)/shard_map/reduce_scatter | solution.py:320
  300.0 314.6 %reduce-scatter.10.cloned.1.call-start = ((), (), s32[]{:S(2)}) async-start(), calls=%async_computation.11 | async-start | bytes 5068800
  324.3 17.1 %copy-start.24 = (bf16[768,2304]{1,0:T(8,128)(2,1)S(1)}, bf16[768,2304]{1,0:T(8,128)(2,1)}, u32[]{:S(2)}) copy-start(bf16[768,2304]{1,0:T(8,128)(2,1)} %all-gather.6.cloned.1.call-done) | copy-start | bytes 10616836
  353.8 11.0 %slice-start.2 = ((s8[6193152]{0:T(1024)(128)(4,1)}), s8[1998848]{0:T(1024)(128)(4,1)S(1)}, s32[]{:S(2)}) async-start(s8[6193152]{0:T(1024)(128)(4,1)} %bitcast.59), calls=%async_computation.14 | async-start | bytes 3997696
  377.5 20.5 %all-to-all-start.1 = ((bf16[16,16,768]{2,1,0:T(8,128)(2,1)}), bf16[16,16,768]{2,1,0:T(8,128)(2,1)S(1)}, u32[]{:S(2)}, u32[]{:S(2)}) async-start(bf16[16,16,768]{2,1,0:T(8,128)(2,1)} %bitcast.63), calls=%async_computation.1 | async-start | bytes 786432 | tf_op jit(solution)/shard_map/all_to_all | solution.py:241
  396.7 8.6 %collective-permute-start.1 = (bf16[64,768]{0,1:T(8,128)(2,1)S(1)}, bf16[64,768]{0,1:T(8,128)(2,1)S(1)}, u32[]{:S(2)}, u32[]{:S(2)}) collective-permute-start(bf16[64,768]{0,1:T(8,128)(2,1)S(1)} %slice.54), channel_id=1, source_target_pairs={{2,0},{4,2},{6,4},{8,6},{10,8},{12,10},{14,12},{16,14},{18,16},{20... | collective-permute-start | bytes 294920 | tf_op jit(solution)/shard_map/ppermute | solution.py:231
  (18 other events, 71.6 us)
Sparse Core Ops, SparseCore 0:
  10.9 64.2 all-gather.5
  78.1 53.1 all-gather.7
  134.2 62.5 all-gather.9
  199.5 62.4 all-gather.11
  286.1 107.5 reduce-scatter.5
  399.9 105.8 reduce-scatter.7
  511.5 103.0 reduce-scatter.9

commit v2 on v1

v2 whole, which is shorter than its diff:
```python
from functools import partial

import jax
import jax.numpy as jnp
from jax import lax
from jax.experimental import pallas as pl
from jax.experimental.pallas import tpu as pltpu
from jax.sharding import PartitionSpec as P

HEADS = 12
HEAD = 64
BLOCK = 64
TOPK = 16
QUAD = 4 * HEAD
FOLD = BLOCK + TOPK
NEG = -1e30


def dot_nn(a, b):
    return lax.dot_general(a, b, (((1,), (0,)), ((), ())), preferred_element_type=jnp.float32)


def dot_nt(a, b):
    return lax.dot_general(a, b, (((1,), (1,)), ((), ())), preferred_element_type=jnp.float32)


def dot_tn(a, b):
    return lax.dot_general(a, b, (((0,), (0,)), ((), ())), preferred_element_type=jnp.float32)


def spread_heads(rows):
    lane = lax.broadcasted_iota(jnp.int32, rows.shape, 1) // HEAD
    zero = jnp.zeros_like(rows)
    return jnp.concatenate([jnp.where(lane == h, rows, zero) for h in range(4)], 0)


def gather_heads(full):
    lane = lax.broadcasted_iota(jnp.int32, (BLOCK, QUAD), 1) // HEAD
    out = full[:BLOCK]
    for h in range(1, 4):
        out = jnp.where(lane == h, full[h * BLOCK : (h + 1) * BLOCK], out)
    return out


def prev_side():
    k = lax.broadcasted_iota(jnp.int32, (BLOCK, QUAD), 0)
    q = lax.broadcasted_iota(jnp.int32, (BLOCK, QUAD), 1) % BLOCK
    return k > q


def unfold(near, far, prev):
    zero = jnp.zeros_like(near)
    both = [jnp.where(prev, near, zero), jnp.where(prev, zero, near), far]
    return jnp.concatenate(both, 0).astype(jnp.bfloat16)


HALF = HEADS // 2 * HEAD


def load_quad(own_ref, other_ref, part, g):
    at = part * HALF
    if g == 0:
        return own_ref[:, at : at + QUAD]
    if g == 1:
        return jnp.concatenate(
            [own_ref[:, at + QUAD : at + HALF], other_ref[:, at : at + HALF - QUAD]], 1
        )
    return other_ref[:, at + HALF - QUAD : at + HALF]


def join_quads(quads):
    own = jnp.concatenate([quads[0], quads[1][:, : HALF - QUAD]], 1)
    other = jnp.concatenate([quads[1][:, HALF - QUAD :], quads[2]], 1)
    return own, other


def attend_kernel(
    info_ref,
    sel_ref,
    bias_ref,
    pool_own,
    prev_own,
    cur_own,
    pool_other,
    prev_other,
    cur_other,
    att_ref,
    probs_ref,
    picks_ref,
):
    c = pl.program_id(0)
    core = info_ref[1]

    @pl.when(c == 0)
    def _():
        pool_rows = pool_own.shape[0]
        ids = lax.broadcasted_iota(jnp.int32, (sel_ref.shape[0], pool_rows), 1)
        one_hot = (ids == sel_ref[...]).astype(jnp.float32).astype(jnp.bfloat16)
        picks_ref[0] = dot_nn(one_hot, pool_own[:, HALF:]).astype(jnp.bfloat16)
        picks_ref[1] = dot_nn(one_hot, pool_other[:, HALF:]).astype(jnp.bfloat16)

    prev = prev_side()
    edge = jnp.where((c == 0) & (info_ref[0] == 1), NEG, 0.0)
    rows = pl.ds(pl.multiple_of(c * TOPK, TOPK), TOPK)
    pick_own, pick_other = picks_ref.at[0, rows], picks_ref.at[1, rows]
    outs = []
    for g in range(HEADS // 4):
        keys, values = [
            jnp.concatenate(
                [
                    load_quad(prev_own, prev_other, part, g),
                    load_quad(cur_own, cur_other, part, g),
                    load_quad(pick_own, pick_other, part - 1, g),
                ],
                0,
            )
            for part in (1, 2)
        ]
        wide_q = spread_heads(load_quad(cur_own, cur_other, 0, g))
        scores = dot_nt(keys, wide_q) * HEAD ** (-0.5)
        near = jnp.where(prev, scores[:BLOCK] + edge, scores[BLOCK : 2 * BLOCK])
        far = scores[2 * BLOCK :] + bias_ref[...]
        folded = jnp.concatenate([near, far], 0)
        top = jnp.max(folded, axis=0, keepdims=True)
        weights = jnp.exp(folded - top)
        probs = weights * (1.0 / jnp.sum(weights, axis=0, keepdims=True))
        probs_ref[0, g] = probs
        full = unfold(probs[:BLOCK], probs[BLOCK:], prev)
        outs.append(gather_heads(dot_tn(full, values)).astype(jnp.bfloat16))
    own, other = join_quads(outs)
    att_ref[:, pl.ds(pl.multiple_of(core * HALF, 128), HALF)] = own
    att_ref[:, pl.ds(pl.multiple_of((1 - core) * HALF, 128), HALF)] = other


def attend(mixed_own, mixed_other, sel_col, bias_col, info, blocks, pool_rows):
    width = HEADS * HEAD
    base = pool_rows // BLOCK
    mixed_specs = [
        pl.BlockSpec((pool_rows, 3 * HALF), lambda c, f: (0, 0)),
        pl.BlockSpec((BLOCK, 3 * HALF), lambda c, f: (base + c, 0)),
        pl.BlockSpec((BLOCK, 3 * HALF), lambda c, f: (base + c + 1, 0)),
    ]
    return pl.pallas_call(
        attend_kernel,
        grid_spec=pltpu.PrefetchScalarGridSpec(
            num_scalar_prefetch=1,
            grid=(blocks,),
            in_specs=[
                pl.BlockSpec((blocks * TOPK, 1), lambda c, f: (0, 0)),
                pl.BlockSpec((TOPK, 1), lambda c, f: (c, 0)),
            ]
            + mixed_specs * 2,
            out_specs=[
                pl.BlockSpec((BLOCK, width), lambda c, f: (c, 0)),
                pl.BlockSpec((1, HEADS // 4, FOLD, QUAD), lambda c, f: (c, 0, 0, 0)),
                pl.BlockSpec((2, blocks * TOPK, 2 * HALF), lambda c, f: (0, 0, 0)),
            ],
        ),
        out_shape=[
            jax.ShapeDtypeStruct((blocks * BLOCK, width), jnp.bfloat16),
            jax.ShapeDtypeStruct((blocks, HEADS // 4, FOLD, QUAD), jnp.float32),
            jax.ShapeDtypeStruct((2, blocks * TOPK, 2 * HALF), jnp.bfloat16),
        ],
        compiler_params=pltpu.CompilerParams(vmem_limit_bytes=32 * 1024 * 1024),
        cost_estimate=pl.CostEstimate(
            flops=12_000_000_000, bytes_accessed=12_000_000, transcendentals=1_000_000
        ),
        name="attend",
    )(info, sel_col, bias_col, *[mixed_own] * 3, *[mixed_other] * 3)


def attend_back_kernel(
    blocks,
    info_ref,
    sel_ref,
    prev_own,
    cur_own,
    prev_other,
    cur_other,
    picks_ref,
    probs_ref,
    datt_ref,
    out_own,
    out_other,
    carry,
    dpicks,
):
    i = pl.program_id(0)
    core = info_ref[1]

    @pl.when(i == 0)
    def _():
        carry[...] = jnp.zeros_like(carry)

    @pl.when(i < blocks)
    def _():
        prev = prev_side()
        rows = pl.ds(pl.multiple_of(i * TOPK, TOPK), TOPK)
        datt_own = datt_ref.at[:, pl.ds(pl.multiple_of(core * HALF, 128), HALF)]
        datt_other = datt_ref.at[:, pl.ds(pl.multiple_of((1 - core) * HALF, 128), HALF)]
        grads = []
        for g in range(HEADS // 4):
            keys, values = [
                jnp.concatenate(
                    [
                        load_quad(prev_own, prev_other, part, g),
                        load_quad(cur_own, cur_other, part, g),
                        load_quad(picks_ref.at[0], picks_ref.at[1], part - 1, g),
                    ],
                    0,
                )
                for part in (1, 2)
            ]
            wide_q = spread_heads(load_quad(cur_own, cur_other, 0, g))
            wide_d = spread_heads(load_quad(datt_own, datt_other, 0, g))
            probs = probs_ref[0, g]
            dprobs = dot_nt(values, wide_d)
            near = jnp.where(prev, dprobs[:BLOCK], dprobs[BLOCK : 2 * BLOCK])
            folded = jnp.concatenate([near, dprobs[2 * BLOCK :]], 0)
            inner = jnp.sum(probs * folded, axis=0, keepdims=True)
            dscores = probs * (folded - inner) * HEAD ** (-0.5)
            full_p = unfold(probs[:BLOCK], probs[BLOCK:], prev)
            full_d = unfold(dscores[:BLOCK], dscores[BLOCK:], prev)
            dvals = dot_nn(full_p, wide_d)
            dkeys = dot_nn(full_d, wide_q)
            dq = gather_heads(dot_tn(full_d, keys))
            grads.append((dq, dkeys, dvals))
        for part in range(3):
            lanes = slice(part * HALF, (part + 1) * HALF)
            halves = join_quads([grad[part] for grad in grads])
            for side, out_ref in enumerate((out_own, out_other)):
                half = halves[side]
                if part == 0:
                    out_ref[:, lanes] = carry[side, :, lanes].astype(jnp.bfloat16)
                    carry[side, :, lanes] = half
                else:
                    out_ref[:, lanes] = (carry[side, :, lanes] + half[:BLOCK]).astype(jnp.bfloat16)
                    carry[side, :, lanes] = half[BLOCK : 2 * BLOCK]
                    picked = slice((part - 1) * HALF, part * HALF)
                    dpicks[side, rows, picked] = half[2 * BLOCK :].astype(jnp.bfloat16)

    @pl.when(i == blocks)
    def _():
        out_own[...] = carry[0].astype(jnp.bfloat16)
        out_other[...] = carry[1].astype(jnp.bfloat16)

    @pl.when(i > blocks)
    def _():
        ids = lax.broadcasted_iota(jnp.int32, (BLOCK, blocks * TOPK), 0) + (i - blocks - 1) * BLOCK
        one_hot = (ids == sel_ref[...]).astype(jnp.float32).astype(jnp.bfloat16)
        for side, out_ref in enumerate((out_own, out_other)):
            out_ref[:, :HALF] = jnp.zeros((BLOCK, HALF), jnp.bfloat16)
            out_ref[:, HALF:] = dot_nn(one_hot, dpicks[side]).astype(jnp.bfloat16)


def attend_back(mixed_own, mixed_other, sel_row, info, picks, probs, datt, blocks, pool_rows):
    width = HEADS * HEAD
    base = pool_rows // BLOCK

    def query_block(i):
        return jnp.minimum(i, blocks - 1)

    def out_block(i, f):
        return (jnp.where(i > blocks, i - blocks - 1, base + i), 0)

    mixed_specs = [
        pl.BlockSpec((BLOCK, 3 * HALF), lambda i, f: (base + query_block(i), 0)),
        pl.BlockSpec((BLOCK, 3 * HALF), lambda i, f: (base + query_block(i) + 1, 0)),
    ]
    rows = pool_rows + (blocks + 1) * BLOCK
    return pl.pallas_call(
        partial(attend_back_kernel, blocks),
        grid_spec=pltpu.PrefetchScalarGridSpec(
            num_scalar_prefetch=1,
            grid=(blocks + 1 + base,),
            in_specs=[pl.BlockSpec((1, blocks * TOPK), lambda i, f: (0, 0))]
            + mixed_specs * 2
            + [
                pl.BlockSpec((2, TOPK, 2 * HALF), lambda i, f: (0, query_block(i), 0)),
                pl.BlockSpec(
                    (1, HEADS // 4, FOLD, QUAD), lambda i, f: (query_block(i), 0, 0, 0)
                ),
                pl.BlockSpec((BLOCK, width), lambda i, f: (query_block(i), 0)),
            ],
            out_specs=[pl.BlockSpec((BLOCK, 3 * HALF), out_block)] * 2,
            scratch_shapes=[
                pltpu.VMEM((2, BLOCK, 3 * HALF), jnp.float32),
                pltpu.VMEM((2, blocks * TOPK, 2 * HALF), jnp.bfloat16),
            ],
        ),
        out_shape=[jax.ShapeDtypeStruct((rows, 3 * HALF), jnp.bfloat16)] * 2,
        compiler_params=pltpu.CompilerParams(vmem_limit_bytes=32 * 1024 * 1024),
        cost_estimate=pl.CostEstimate(
            flops=20_000_000_000, bytes_accessed=18_000_000, transcendentals=0
        ),
        name="attend_back",
    )(info, sel_row, *[mixed_own] * 2, *[mixed_other] * 2, picks, probs, datt)


def standardize(values):
    center = values - jnp.mean(values, axis=-1, keepdims=True)
    spread = jnp.mean(center * center, axis=-1, keepdims=True)
    scale = lax.rsqrt(spread + 1e-05)
    return center * scale, scale


def standardize_back(unit, scale, dunit):
    return scale * (
        dunit
        - jnp.mean(dunit, axis=-1, keepdims=True)
        - unit * jnp.mean(dunit * unit, axis=-1, keepdims=True)
    )


def shift_seq(value, distance):
    size = lax.axis_size("seq")
    route = [(i - distance, i) for i in range(size) if 0 <= i - distance < size]
    return lax.ppermute(value, "seq", route)


BOTH = ("seq", "batch")

def flip_route(axis_size, bit):
    return [(i, i ^ bit) for i in range(axis_size)]

def ring_route(size, stride, steps):
    return [(i, (i + stride * steps) % size) for i in range(size)]

def swap(value, axis, bit):
    return lax.ppermute(value, axis, flip_route(lax.axis_size(axis), bit))

def in_order(bit, own, other):
    return jnp.stack([jnp.where(bit == 0, own, other), jnp.where(bit == 0, other, own)])

def gather_seq(slab, cut):
    size = lax.axis_size("seq")
    at = lax.axis_index("seq")
    layers = size // 4
    z, y, x = at // 4, at // 2 % 2, at % 2
    got = [slab] + [lax.ppermute(slab, "seq", ring_route(size, 4, k)) for k in range(1, layers)]
    stack = jnp.stack(got)
    line = jnp.concatenate([lax.dynamic_slice_in_dim(stack, (z - k) % layers, 1, 0) for k in range(layers)], 0)
    first, second = line[:, :, :cut], line[:, :, cut:]
    first_x = swap(first, "seq", 1)
    second_y = swap(second, "seq", 2)
    first = in_order(x, first, first_x)
    second = in_order(y, second, second_y)
    first_y = swap(first, "seq", 2)
    second_x = swap(second, "seq", 1)
    first = in_order(y, first, first_y)
    second = in_order(x, second, second_x)
    rows = size * slab.shape[0]
    first = jnp.transpose(first, (2, 0, 1, 3, 4)).reshape(rows, cut)
    second = jnp.transpose(second, (2, 1, 0, 3, 4)).reshape(rows, slab.shape[1] - cut)
    return jnp.concatenate([first, second], 1)

def pick(value, index, axis):
    return lax.dynamic_index_in_dim(value, index, axis, keepdims=False)

def add(a, b):
    return (a.astype(jnp.float32) + b.astype(jnp.float32)).astype(jnp.bfloat16)

def scatter_seq(full, cut):
    size = lax.axis_size("seq")
    at = lax.axis_index("seq")
    layers = size // 4
    z, y, x = at // 4, at // 2 % 2, at % 2
    grid = full.reshape(layers, 2, 2, -1, full.shape[1])
    first, second = grid[..., :cut], grid[..., cut:]
    first_got = swap(pick(first, 1 - x, 2), "seq", 1)
    second_got = swap(pick(second, 1 - y, 1), "seq", 2)
    first = add(pick(first, x, 2), first_got)
    second = add(pick(second, y, 1), second_got)
    first_got = swap(pick(first, 1 - y, 1), "seq", 2)
    second_got = swap(pick(second, 1 - x, 1), "seq", 1)
    line = jnp.concatenate([add(pick(first, y, 1), first_got), add(pick(second, x, 1), second_got)], -1)
    total = pick(line, z, 0).astype(jnp.float32)
    for k in range(1, layers):
        got = lax.ppermute(pick(line, (z + k) % layers, 0), "seq", ring_route(size, 4, k))
        total = total + got.astype(jnp.float32)
    return total


def paired():
    return lax.axis_size("batch") == 2 and lax.axis_size("seq") % 4 == 0


def side_index():
    return lax.axis_index("batch") % 2


def halves_of(matrix, groups):
    rows, columns = matrix.shape
    parts = matrix.reshape(rows, groups, 2, columns // (2 * groups))
    return jnp.transpose(parts, (2, 0, 1, 3)).reshape(2, rows, columns // 2)


def whole_of(halves, groups):
    _, rows, columns = halves.shape
    parts = halves.reshape(2, rows, groups, columns // groups)
    return jnp.transpose(parts, (1, 2, 0, 3)).reshape(rows, 2 * columns)


def gather_slab(halves):
    side = side_index()
    mine, theirs = pick(halves, side, 0), pick(halves, 1 - side, 0)
    got = swap(theirs, "batch", 1)
    return in_order(side, mine, got).reshape(-1, halves.shape[2])


def gather_halves(halves, cut):
    if paired():
        own = gather_seq(gather_slab(halves), cut)
        return own, swap(own, "batch", 1)
    full = lax.all_gather(halves, BOTH, axis=1, tiled=True)
    return pick(full, side_index(), 0), pick(full, 1 - side_index(), 0)


def scatter_halves(own, other, cut):
    side = side_index()
    if paired():
        mixed = add(own, swap(other, "batch", 1))
        total = scatter_seq(mixed, cut)
        total = total.reshape(2, -1, total.shape[1])
        got = swap(pick(total, 1 - side, 0), "batch", 1)
        return in_order(side, pick(total, side, 0), got)
    full = in_order(side, own, other)
    return lax.psum_scatter(full, BOTH, scatter_dimension=1, tiled=True).astype(jnp.float32)


def everyone(rows):
    size = lax.axis_size("seq")
    return lax.all_to_all(jnp.broadcast_to(rows, (size,) + rows.shape), "seq", 0, 0)


def gather_vectors(vectors):
    return lax.all_gather(vectors, BOTH, axis=1, tiled=True).astype(jnp.float32)


def local(
    inputs, selection, cotangent, ln1_gain, ln1_bias, w_qkv, w_out, ln2_gain, ln2_bias, w_up, w_down
):
    bf16, f32 = jnp.bfloat16, jnp.float32
    tokens_low = inputs[0]
    chosen = selection[0]
    count, width = tokens_low.shape
    blocks = count // BLOCK
    size = lax.axis_size("seq")
    pool_rows = blocks * size
    at = lax.axis_index("seq")
    side = side_index()
    vectors = jnp.stack([ln1_gain, ln1_bias, ln2_gain, ln2_bias])

    own_qkv, other_qkv = gather_halves(halves_of(w_qkv, 3), 512)
    out_up = jnp.concatenate([halves_of(w_out, 1), halves_of(w_up, 1)], 2)
    own_ou, other_ou = gather_halves(out_up, 1024)
    mat_down = lax.all_gather(w_down, BOTH, axis=0, tiled=True)
    mat_out = whole_of(in_order(side, own_ou[:, : width // 2], other_ou[:, : width // 2]), 1)
    mat_up = whole_of(in_order(side, own_ou[:, width // 2 :], other_ou[:, width // 2 :]), 1)

    tokens = tokens_low.astype(f32)
    unit, unit_scale = standardize(tokens)
    unit_halo, _ = standardize(shift_seq(tokens_low[-BLOCK:], 1).astype(f32))
    pooled = jnp.mean(unit.reshape(blocks, BLOCK, width), axis=1).astype(bf16)
    if paired():
        chip = in_order(side, vectors, swap(vectors, "batch", 1))
        chip = jnp.transpose(chip, (1, 0, 2)).reshape(1, -1)
        span = chip.shape[1]
        chip = jnp.pad(chip, ((0, 7), (0, width - span)))
        got = everyone(jnp.concatenate([pooled, chip], 0))
        unit_pool = got[:, :blocks].reshape(pool_rows, width)
        vectors = got[:, blocks, :span].reshape(size, 4, span // 4)
        vectors = jnp.transpose(vectors, (1, 0, 2)).reshape(4, width).astype(f32)
    else:
        unit_pool = lax.all_gather(pooled, "seq", axis=0, tiled=True)
        vectors = lax.all_gather(vectors, BOTH, axis=1, tiled=True).astype(f32)
    gain_one, bias_one, gain_two, bias_two = vectors
    unit_ext = jnp.concatenate([unit_pool.astype(f32), unit_halo, unit], 0)
    normed = (unit_ext * gain_one + bias_one).astype(bf16)
    mixed_own = dot_nn(normed, own_qkv).astype(bf16)
    mixed_other = dot_nn(normed, other_qkv).astype(bf16)

    block_ids = at * blocks + jnp.arange(blocks, dtype=jnp.int32)
    flat = chosen.reshape(blocks * TOPK)
    far_bias = jnp.where(chosen < block_ids[:, None], 0.0, NEG).reshape(blocks * TOPK, 1)
    info = jnp.stack([(at == 0).astype(jnp.int32), side])
    attended, probs, picks = attend(
        mixed_own, mixed_other, flat[:, None], far_bias, info, blocks, pool_rows
    )

    after = tokens + dot_nn(attended, mat_out)
    unit_two, scale_two = standardize(after)
    normed_two = (unit_two * gain_two + bias_two).astype(bf16)
    hidden = dot_nn(normed_two, mat_up)
    active, gelu_back = jax.vjp(partial(jax.nn.gelu, approximate=True), hidden)
    active = active.astype(bf16)
    output = (after + dot_nn(active, mat_down)).astype(bf16)

    upstream = cotangent[0]
    dhidden = gelu_back(dot_nt(upstream, mat_down))[0].astype(bf16)
    grad_down = dot_tn(active, upstream).astype(bf16)
    grad_up = in_order(side, *jnp.split(dot_tn(normed_two, dhidden).astype(bf16), 2, axis=1))
    dnormed_two = dot_nt(dhidden, mat_up)
    grad_gain_two = jnp.sum(dnormed_two * unit_two, axis=0)
    grad_bias_two = jnp.sum(dnormed_two, axis=0)
    dafter = upstream.astype(f32) + standardize_back(unit_two, scale_two, dnormed_two * gain_two)
    dafter_low = dafter.astype(bf16)
    grad_out = in_order(side, *jnp.split(dot_tn(attended, dafter_low).astype(bf16), 2, axis=1))
    dattended = dot_nt(dafter_low, mat_out).astype(bf16)
    own_down = lax.psum_scatter(grad_down, BOTH, scatter_dimension=0, tiled=True).astype(f32)
    sum_up = scatter_halves(grad_up[0], grad_up[1], 768)

    dmixed_own, dmixed_other = attend_back(
        mixed_own, mixed_other, flat[None, :], info, picks, probs, dattended, blocks, pool_rows
    )
    grad_other = dot_tn(normed, dmixed_other).astype(bf16)
    grad_own = dot_tn(normed, dmixed_own).astype(bf16)
    dnormed = dot_nt(dmixed_own, own_qkv) + dot_nt(dmixed_other, other_qkv)
    grad_gain_one = jnp.sum(dnormed * unit_ext, axis=0)
    grad_bias_one = jnp.sum(dnormed, axis=0)
    vector_grads = jnp.stack([grad_gain_one, grad_bias_one, grad_gain_two, grad_bias_two])
    from_next = shift_seq(dnormed[pool_rows : pool_rows + BLOCK].astype(bf16), -1).astype(f32)
    own_qo = jnp.concatenate([grad_own, grad_out[0]], 1)
    other_qo = jnp.concatenate([grad_other, grad_out[1]], 1)
    sum_qo = scatter_halves(own_qo, other_qo, 768)
    dpool = dnormed[:pool_rows].astype(bf16)
    if paired():
        spread = jnp.transpose(vector_grads.reshape(4, size, -1), (1, 0, 2)).reshape(size, 1, -1)
        spread = jnp.pad(spread.astype(bf16), ((0, 0), (0, 7), (0, width - spread.shape[2])))
        send = jnp.concatenate([dpool.reshape(size, blocks, width), spread], 1)
        got = jnp.sum(lax.all_to_all(send, "seq", 0, 0).astype(f32), axis=0)
        from_pool = got[:blocks]
        chip = got[blocks, :span].reshape(4, 2, -1)
        vector_sums = pick(chip, side, 1) + swap(pick(chip, 1 - side, 1), "batch", 1)
    else:
        from_pool = lax.psum_scatter(dpool, "seq", scatter_dimension=0, tiled=True).astype(f32)
        vector_sums = lax.psum_scatter(vector_grads, BOTH, scatter_dimension=1, tiled=True)
    dtoken = (
        dnormed[pool_rows + BLOCK :]
        + jnp.repeat(from_pool * (1.0 / BLOCK), BLOCK, axis=0)
        + jnp.pad(from_next, ((count - BLOCK, 0), (0, 0)))
    )
    input_grad = dafter + standardize_back(unit, unit_scale, dtoken * gain_one)

    split = 3 * width // 2
    return (
        output[None],
        input_grad[None],
        vector_sums[0],
        vector_sums[1],
        whole_of(sum_qo[:, :, :split], 3),
        whole_of(sum_qo[:, :, split:], 1),
        vector_sums[2],
        vector_sums[3],
        whole_of(sum_up, 1),
        own_down,
    )


def solution(mesh):
    tokens = P("batch", "seq", None)
    vector = P(BOTH)
    matrix = P(BOTH, None)
    return jax.shard_map(
        local,
        mesh=mesh,
        in_specs=(
            tokens,
            tokens,
            tokens,
            vector,
            vector,
            matrix,
            matrix,
            vector,
            vector,
            matrix,
            matrix,
        ),
        out_specs=(
            tokens,
            tokens,
            vector,
            vector,
            matrix,
            matrix,
            vector,
            vector,
            matrix,
            matrix,
        ),
        check_vma=False,
    )
```

time: 631 us -> 438 us (0.69)
  waiting for transfers between devices: 336 us -> 89.7 us
  starting transfers between devices: 18.1 us -> 75 us
  blocking collectives: 40.5 us -> 0 us
  other arithmetic: 32.2 us -> 59.1 us
  local copies, waits for them, and re-layouts: 54 us -> 65.4 us
  matrix products: 98 us -> 90.8 us
    unnamed x8 -> x2, waiting for transfers between devices: 110 us -> 0.03 us
    ppermute x0 -> x38, waiting for transfers between devices: none -> 89.6 us  [the longest x26 44.5 us: swap(): return lax.ppermute(value, axis, flip_route(lax.axis_size(axis), bit))]
    reduce_scatter x2 -> x1, waiting for transfers between devices: 88.1 us -> 0.01 us  [local(): lax.psum_scatter(grad_down, BOTH, scatter_dimension=0, tiled=True)]
    all_gather x3 -> x0, waiting for transfers between devices: 83 us -> none  [the longest x1 60.1 us: local(): mat_up = lax.all_gather(w_up, BOTH, axis=0, tiled=True)]
    ppermute x0 -> x38, starting transfers between devices: none -> 55.8 us  [the longest x26 23.7 us: swap(): return lax.ppermute(value, axis, flip_route(lax.axis_size(axis), bit))]
    all_gather x1, waiting for transfers between devices: 54 us -> 0.02 us  [local(): mat_down = lax.all_gather(w_down, BOTH, axis=0, tiled=True)]
    all_gather x1 -> x0, blocking collectives: 40.5 us -> none  [local(): lax.all_gather(jnp.stack([ln1_gain, ln1_bias, ln2_gain, ln2_bias]), BOTH,...]
    another operation x1 -> x28, other arithmetic: 0.02 us -> 12.9 us  [the longest x24 11.8 us: in_order(): jnp.stack([jnp.where(bit == 0, own, other), jnp.where(bit == 0, other, ow...]
  transfers between devices with their start and end apart: 11 -> 44, of which waited for: 6 -> 14; matrix products, arithmetic and copies ran while one was open for 23% -> 47% of each run, Pallas kernels for 5% -> 8%
where the time goes in v2:
time: 438 us; the launch traced here: 430 us
  matrix products  90.8 us (21%)
  waiting for transfers between devices  89.7 us (20%)
  starting transfers between devices  75 us (17%)
  local copies, waits for them, and re-layouts  65.4 us (15%)
  other arithmetic  59.1 us (13%)
  Pallas kernels  33.7 us (8%)
  between operations  16.1 us (4%)
    ppermute x26, waiting for transfers between devices, swap(): return lax.ppermute(value, axis, flip_route(lax.axis_size(axis), bit))  44.5 us
    dot_general x5, matrix products, dot_nt(): lax.dot_general(a, b, (((1,), (1,)), ((), ())), preferred_element_type=jn...  37.7 us
    ppermute x6, waiting for transfers between devices, gather_seq(): lax.ppermute(slab, 'seq', ring_route(size, 4, k))  30.4 us
    dot_general x5, matrix products, dot_nn(): lax.dot_general(a, b, (((1,), (0,)), ((), ())), preferred_element_type=jn...  28.2 us
    unnamed x135, local copies, waits for them, and re-layouts  25.3 us
    dot_general x5, matrix products, dot_tn(): lax.dot_general(a, b, (((0,), (0,)), ((), ())), preferred_element_type=jn...  24.9 us
    ppermute x26, starting transfers between devices, swap(): return lax.ppermute(value, axis, flip_route(lax.axis_size(axis), bit))  23.7 us
    ppermute x6, starting transfers between devices, gather_seq(): lax.ppermute(slab, 'seq', ring_route(size, 4, k))  20.3 us
  transfers between devices with their start and end apart: 44, of which 14 were waited for; matrix products, arithmetic and copies ran while one was open for 47% of the time, Pallas kernels for 8%

profile of v2, /device:TPU:0, one launch (start us, length us, event | category | flops | bytes accessed | tf_op | source)
XLA Modules:
  0.0 429.8 jit_solution(14760992533399191462)
XLA Ops:
  28.4 6.0 %all-to-all-start = ((bf16[16,24,768]{2,1,0:T(8,128)(2,1)}), bf16[16,24,768]{2,1,0:T(8,128)(2,1)}, u32[]{:S(2)}, u32[]{:S(2)}) async-start(bf16[16,24,768]{2,1,0:T(8,128)(2,1)} %broadcast_in_dim.18), calls=%async_computation | async-start | bytes 1179648 | tf_op jit(solution)/shard_map/all_to_all | solution.py:433
  44.4 9.9 %collective-permute-done.5 = bf16[48,1152]{1,0:T(8,128)(2,1)S(1)} collective-permute-done((bf16[48,1152]{1,0:T(8,128)(2,1)S(1)}, bf16[48,1152]{1,0:T(8,128)(2,1)S(1)}, u32[]{:S(2)}, u32[]{:S(2)}) %collective-permute-start.5) | collective-permute-done | bytes 110624 | tf_op jit(solution)/shard_map/ppermute | solution.py:340
  54.3 11.5 %collective-permute-start.12 = (bf16[48,1920]{1,0:T(8,128)(2,1)S(1)}, bf16[48,1920]{1,0:T(8,128)(2,1)S(1)}, u32[]{:S(2)}, u32[]{:S(2)}) collective-permute-start(bf16[48,1920]{1,0:T(8,128)(2,1)S(1)} %bitcast.341), channel_id=1, source_target_pairs={{0,8},{2,10},{4,12},{6,14},{8,16},{10,18},{12,20},{14,22},{16,24},... | collective-permute-start | bytes 552968 | tf_op jit(solution)/shard_map/ppermute | solution.py:340
  65.8 9.4 %collective-permute-done.4 = bf16[48,1152]{1,0:T(8,128)(2,1)S(1)} collective-permute-done((bf16[48,1152]{1,0:T(8,128)(2,1)S(1)}, bf16[48,1152]{1,0:T(8,128)(2,1)S(1)}, u32[]{:S(2)}, u32[]{:S(2)}) %collective-permute-start.4) | collective-permute-done | bytes 110624 | tf_op jit(solution)/shard_map/ppermute | solution.py:340
  78.5 11.1 %collective-permute-done.13 = bf16[48,1920]{1,0:T(8,128)(2,1)S(1)} collective-permute-done((bf16[48,1920]{1,0:T(8,128)(2,1)S(1)}, bf16[48,1920]{1,0:T(8,128)(2,1)S(1)}, u32[]{:S(2)}, u32[]{:S(2)}) %collective-permute-start.13) | collective-permute-done | bytes 184352 | tf_op jit(solution)/shard_map/ppermute | solution.py:340
  94.6 6.3 %collective-permute-done.17 = bf16[4,48,896]{2,1,0:T(8,128)(2,1)S(1)} collective-permute-done((bf16[4,48,896]{2,1,0:T(8,128)(2,1)S(1)}, bf16[4,48,896]{2,1,0:T(8,128)(2,1)S(1)}, u32[]{:S(2)}, u32[]{:S(2)}) %collective-permute-start.17) | collective-permute-done | bytes 344096 | tf_op jit(solution)/shard_map/ppermute | solution.py:330
  109.5 4.7 %collective-permute-done.9 = bf16[2,4,48,640]{3,2,1,0:T(8,128)(2,1)S(1)} collective-permute-done((bf16[2,4,48,640]{3,2,1,0:T(8,128)(2,1)S(1)}, bf16[2,4,48,640]{3,2,1,0:T(8,128)(2,1)S(1)}, u32[]{:S(2)}, u32[]{:S(2)}) %collective-permute-start.9) | collective-permute-done | bytes 491552 | tf_op jit(solution)/shard_map/ppermute | solution.py:330
  119.0 7.8 %collective-permute-done.18 = bf16[2,4,48,896]{3,2,0,1:T(8,128)(2,1)} collective-permute-done((bf16[2,4,48,896]{3,2,0,1:T(8,128)(2,1)}, bf16[2,4,48,896]{3,2,0,1:T(8,128)(2,1)}, u32[]{:S(2)}, u32[]{:S(2)}) %collective-permute-start.18) | collective-permute-done | bytes 688160 | tf_op jit(solution)/shard_map/ppermute | solution.py:330
  135.3 6.5 %concatenate.39 = f32[1344,768]{0,1:T(8,128)} concatenate(f32[256,768]{0,1:T(8,128)} %copy.80, f32[64,768]{0,1:T(8,128)} %fusion.26, f32[1024,768]{0,1:T(8,128)} %fusion.9), dimensions={0} | concatenate | bytes 8257536 | tf_op jit(solution)/shard_map/concatenate | solution.py:478
  147.6 5.5 %convolution_convert_fusion.pool_other.prev_other.cur_other = bf16[1344,1152]{1,0:T(8,128)(2,1)S(1)} fusion(bf16[1344,768]{0,1:T(8,128)(2,1)S(1)} %add_convert_fusion.2, bf16[768,1152]{1,0:T(8,128)(2,1)} %collective-permute-done.10), kind=kOutput, calls=%fused_computation.10 | convolution fusion | flops 2379718656 | bytes 6930432 | tf_op jit(solution)/shard_map/dot_general | solution.py:20
  153.1 15.6 %attend.1 = (bf16[1024,768]{1,0:T(8,128)(2,1)S(1)}, f32[16,3,80,256]{3,2,1,0:T(8,128)S(1)}, bf16[2,256,768]{2,1,0:T(8,128)(2,1)S(1)}) custom-call(s32[2]{0:T(128)S(1)} %pad_add_fusion.info_ref, s32[256,1]{1,0:T(8,128)S(1)} %broadcast_in_dim_reshape_squeeze.8.sel_ref, f32[256,1]{1,0:T(8,128)S(1)} %compare_select_fusion.bias_ref, ...), custom_call_target="tpu_custom_call" | custom-call | flops 12000000000 | bytes 12000000 | tf_op jit(solution)/shard_map/attend/pallas_call | solution.py:143
  183.2 6.8 %copy.90 = bf16[768,1,2,1536]{0,3,2,1:T(8,128)(2,1)} copy(bf16[768,1,2,1536]{3,0,2,1:T(8,128)(2,1)} %maximum_bitcast_fusion) | data formatting | bytes 9437184 | tf_op jit(solution)/shard_map/transpose | solution.py:401
  193.4 5.5 %fusion.63 = f32[1024,3072]{1,0:T(8,128)S(1)} fusion(bf16[768,3072]{0,1:T(8,128)(2,1)S(1)} %bitcast.323, f32[1024,768]{0,1:T(8,128)S(1)} %get-tuple-element.126, f32[768]{0:T(1024)S(1)} %add.315, f32[768]{0:T(1024)S(1)} %mul.181, f32[1024]{0:T(1024)S(1)} %add_rsqrt_fusion, f32[1024]{0:T(1024)S(1)} %broadcast_multiply_fusion.4), kind=kOutput, calls=%fused_computation.249 | convolution fusion | flops 4835770368 | bytes 20461568 | tf_op jit(solution)/shard_map/dot_general | solution.py:20
  203.5 8.9 %convolution_convert_fusion.2 = bf16[3072,768]{1,0:T(8,128)(2,1)} fusion(bf16[1,1024,768]{2,1,0:T(8,128)(2,1)S(1)} %copy-done.37, f32[1024,3072]{1,0:T(8,128)S(1)} %fusion.63), kind=kOutput, calls=%fused_computation.12 | convolution fusion | flops 4862509056 | bytes 18874368 | tf_op jit(solution)/shard_map/dot_general | solution.py:28
  212.5 14.6 %fusion.6 = bf16[1024,3072]{1,0:T(8,128)(2,1)S(1)} fusion(f32[1024,3072]{1,0:T(8,128)} %copy-done.53, bf16[3072,768]{1,0:T(8,128)(2,1)} %all-gather.2.cloned.1.call-done, bf16[1,1024,768]{2,1,0:T(8,128)(2,1)S(1)} %copy-done.37), kind=kOutput, calls=%fused_computation.8 | convolution fusion | flops 4894752768 | bytes 25165824 | tf_op jit(solution)/shard_map/dot_general | solution.py:24
  227.1 11.4 %fusion.69 = (bf16[768]{0:T(1024)(128)(2,1)S(1)}, f32[1024,768]{1,0:T(8,128)}) fusion(bf16[1024,3072]{1,0:T(8,128)(2,1)S(1)} %fusion.6, bf16[768,3072]{0,1:T(8,128)(2,1)} %bitcast.320), kind=kOutput, calls=%fused_computation.254 | convolution fusion | flops 4832623616 | bytes 14157312 | tf_op jit(solution)/shard_map/dot_general | solution.py:24
  252.5 18.2 %attend_back.1 = (bf16[1344,1152]{1,0:T(8,128)(2,1)S(1)}, bf16[1344,1152]{1,0:T(8,128)(2,1)S(1)}) custom-call(s32[2]{0:T(128)S(1)} %pad_add_fusion.info_ref, s32[1,256]{1,0:T(1,128)S(1)} %broadcast_in_dim_reshape_squeeze.7.sel_ref, bf16[1344,1152]{1,0:T(8,128)(2,1)S(1)} %copy-done.4, bf16[1344,1152]{1,0:T(8,128)(2,1)S(1)} %copy-done.4, ...), custom_call_target="tpu_custom_call" | custom-call | flops 20000000000 | bytes 18000000 | tf_op jit(solution)/shard_map/attend_back/pallas_call | solution.py:271
  273.9 7.1 %multiply_reduce_fusion = (bf16[768]{0:T(1024)(128)(2,1)S(1)}, bf16[768]{0:T(1024)(128)(2,1)S(1)}, bf16[1344,768]{0,1:T(8,128)(2,1)S(1)}, f32[1344,768]{0,1:T(8,128)}) fusion(f32[1344,768]{0,1:T(8,128)S(1)} %bitcast.308, f32[1344,768]{0,1:T(8,128)S(1)} %fusion.62, bf16[1344,1152]{1,0:T(8,128)(2,1)S(1)} %get-tuple-element.19, ...), kind=kOutput, calls=%fused_computation.17 | convolution fusion | flops 2383329792 | bytes 19319808 | tf_op jit(solution)/shard_map/dot_general | solution.py:24
  282.5 11.5 %fusion.13 = bf16[1,1024,768]{1,2,0:T(8,128)(2,1)} fusion(f32[1024,768]{0,1:T(8,128)S(1)} %copy-done.15, bf16[3072,768]{1,0:T(8,128)(2,1)} %all-gather.2.cloned.1.call-done, f32[1024,3072]{1,0:T(8,128)} %copy-done.53), kind=kOutput, calls=%fused_computation.55 | convolution fusion | flops 4861722624 | bytes 22020096 | tf_op jit(solution)/shard_map/dot_general | solution.py:20
  302.1 7.4 %all-to-all-start.1 = ((bf16[16,24,768]{2,1,0:T(8,128)(2,1)}), bf16[16,24,768]{2,1,0:T(8,128)(2,1)}, u32[]{:S(2)}, u32[]{:S(2)}) async-start(bf16[16,24,768]{2,1,0:T(8,128)(2,1)} %fusion.21), calls=%async_computation.1 | async-start | bytes 1179648 | tf_op jit(solution)/shard_map/all_to_all | solution.py:531
  320.4 5.7 %convolution_convert_fusion.3 = bf16[768,3072]{1,0:T(8,128)(2,1)S(1)} fusion(bf16[1024,3072]{1,0:T(8,128)(2,1)S(1)} %bitcast.374, f32[1024,768]{0,1:T(8,128)S(1)} %copy-done.16, f32[768]{0:T(1024)S(1)} %add.315, f32[768]{0:T(1024)S(1)} %mul.181, f32[1024]{0:T(1024)S(1)} %add_rsqrt_fusion, f32[1024]{0:T(1024)S(1)} %broadcast_multiply_fusion.4), kind=kOutput, calls=%fused_computation.13 | convolution fusion | flops 4838129664 | bytes 14170112 | tf_op jit(solution)/shard_map/dot_general | solution.py:28
  361.8 8.8 %collective-permute-done.23 = bf16[4,2,48,768]{3,2,0,1:T(8,128)(2,1)S(1)} collective-permute-done((bf16[4,2,48,768]{3,2,0,1:T(8,128)(2,1)S(1)}, bf16[4,2,48,768]{3,2,0,1:T(8,128)(2,1)S(1)}, u32[]{:S(2)}, u32[]{:S(2)}) %collective-permute-start.23) | collective-permute-done | bytes 589856 | tf_op jit(solution)/shard_map/ppermute | solution.py:330
  374.6 8.6 %collective-permute-done.32 = bf16[4,2,48,768]{3,2,0,1:T(8,128)(2,1)S(1)} collective-permute-done((bf16[4,2,48,768]{3,2,0,1:T(8,128)(2,1)S(1)}, bf16[4,2,48,768]{3,2,0,1:T(8,128)(2,1)S(1)}, u32[]{:S(2)}, u32[]{:S(2)}) %collective-permute-start.32) | collective-permute-done | bytes 589856 | tf_op jit(solution)/shard_map/ppermute | solution.py:330
  404.5 10.2 %collective-permute-done.28 = bf16[48,1536]{1,0:T(8,128)(2,1)S(1)} collective-permute-done((bf16[48,1536]{1,0:T(8,128)(2,1)S(1)}, bf16[48,1536]{1,0:T(8,128)(2,1)S(1)}, u32[]{:S(2)}, u32[]{:S(2)}) %collective-permute-start.28) | collective-permute-done | bytes 147488 | tf_op jit(solution)/shard_map/ppermute | solution.py:379
  (381 shorter events, 194.8 us)
Async XLA Ops:
  7.2 205.3 %all-gather.2.cloned.1.call-start = ((), (), s32[]{:S(2)}) async-start(), calls=%async_computation.3 | async-start | bytes 4866048 | tf_op jit(solution)/shard_map/all_gather | solution.py:457
  10.4 31.8 %collective-permute-start.1 = (bf16[64,768]{0,1:T(8,128)(2,1)S(1)}, bf16[64,768]{0,1:T(8,128)(2,1)S(1)}, u32[]{:S(2)}, u32[]{:S(2)}) collective-permute-start(bf16[64,768]{0,1:T(8,128)(2,1)S(1)} %slice_bitcast_fusion), channel_id=1, source_target_pairs={{0,2},{2,4},{4,6},{6,8},{8,10},{10,12},{12,14},{14,16},{16,18},{18... | collective-permute-start | bytes 294920 | tf_op jit(solution)/shard_map/ppermute | solution.py:318
  15.1 19.4 %collective-permute-start.2 = (bf16[24,1152]{1,0:T(8,128)(2,1)S(1)}, bf16[24,1152]{1,0:T(8,128)(2,1)S(1)}, u32[]{:S(2)}, u32[]{:S(2)}) collective-permute-start(bf16[24,1152]{1,0:T(8,128)(2,1)S(1)} %dynamic-slice_bitcast_fusion.8), channel_id=1, source_target_pairs={{0,1},{1,0},{2,3},{3,2},{4,5},{5,4},{6,7},{7,6},{8,9},{9,8},{10,11... | collective-permute-start | bytes 165896 | tf_op jit(solution)/shard_map/ppermute | solution.py:330
  16.0 23.4 %collective-permute-start.11 = (bf16[24,1920]{1,0:T(8,128)(2,1)S(1)}, bf16[24,1920]{1,0:T(8,128)(2,1)S(1)}, u32[]{:S(2)}, u32[]{:S(2)}) collective-permute-start(bf16[24,1920]{1,0:T(8,128)(2,1)S(1)} %bitcast.361), channel_id=1, source_target_pairs={{0,1},{1,0},{2,3},{3,2},{4,5},{5,4},{6,7},{7,6},{8,9},{9,8},{10,11... | collective-permute-start | bytes 276488 | tf_op jit(solution)/shard_map/ppermute | solution.py:330
  28.4 87.6 %all-to-all-start = ((bf16[16,24,768]{2,1,0:T(8,128)(2,1)}), bf16[16,24,768]{2,1,0:T(8,128)(2,1)}, u32[]{:S(2)}, u32[]{:S(2)}) async-start(bf16[16,24,768]{2,1,0:T(8,128)(2,1)} %broadcast_in_dim.18), calls=%async_computation | async-start | bytes 1179648 | tf_op jit(solution)/shard_map/all_to_all | solution.py:433
  34.4 315.5 %reduce-scatter.2.cloned.1.call-start = ((), (), s32[]{:S(2)}) async-start(), calls=%async_computation.4 | async-start | bytes 4866048 | tf_op jit(solution)/shard_map/reduce_scatter | solution.py:510
  34.5 19.7 %collective-permute-start.5 = (bf16[48,1152]{1,0:T(8,128)(2,1)S(1)}, bf16[48,1152]{1,0:T(8,128)(2,1)S(1)}, u32[]{:S(2)}, u32[]{:S(2)}) collective-permute-start(bf16[48,1152]{1,0:T(8,128)(2,1)S(1)} %bitcast.347), channel_id=1, source_target_pairs={{0,24},{2,26},{4,28},{6,30},{8,0},{10,2},{12,4},{14,6},{16,8},{18,... | collective-permute-start | bytes 331784 | tf_op jit(solution)/shard_map/ppermute | solution.py:340
  38.3 37.0 %collective-permute-start.4 = (bf16[48,1152]{1,0:T(8,128)(2,1)S(1)}, bf16[48,1152]{1,0:T(8,128)(2,1)S(1)}, u32[]{:S(2)}, u32[]{:S(2)}) collective-permute-start(bf16[48,1152]{1,0:T(8,128)(2,1)S(1)} %bitcast.348), channel_id=1, source_target_pairs={{0,16},{2,18},{4,20},{6,22},{8,24},{10,26},{12,28},{14,30},{16,0},... | collective-permute-start | bytes 331784 | tf_op jit(solution)/shard_map/ppermute | solution.py:340
  38.3 37.0 %collective-permute-start.3 = (bf16[48,1152]{1,0:T(8,128)(2,1)S(1)}, bf16[48,1152]{1,0:T(8,128)(2,1)S(1)}, u32[]{:S(2)}, u32[]{:S(2)}) collective-permute-start(bf16[48,1152]{1,0:T(8,128)(2,1)S(1)} %bitcast.349), channel_id=1, source_target_pairs={{0,8},{2,10},{4,12},{6,14},{8,16},{10,18},{12,20},{14,22},{16,24},... | collective-permute-start | bytes 331784 | tf_op jit(solution)/shard_map/ppermute | solution.py:340
  39.5 39.0 %collective-permute-start.14 = (bf16[48,1920]{1,0:T(8,128)(2,1)S(1)}, bf16[48,1920]{1,0:T(8,128)(2,1)S(1)}, u32[]{:S(2)}, u32[]{:S(2)}) collective-permute-start(bf16[48,1920]{1,0:T(8,128)(2,1)S(1)} %bitcast.339), channel_id=1, source_target_pairs={{0,24},{2,26},{4,28},{6,30},{8,0},{10,2},{12,4},{14,6},{16,8},{18,... | collective-permute-start | bytes 552968 | tf_op jit(solution)/shard_map/ppermute | solution.py:340
  42.2 47.4 %collective-permute-start.13 = (bf16[48,1920]{1,0:T(8,128)(2,1)S(1)}, bf16[48,1920]{1,0:T(8,128)(2,1)S(1)}, u32[]{:S(2)}, u32[]{:S(2)}) collective-permute-start(bf16[48,1920]{1,0:T(8,128)(2,1)S(1)} %bitcast.340), channel_id=1, source_target_pairs={{0,16},{2,18},{4,20},{6,22},{8,24},{10,26},{12,28},{14,30},{16,0},... | collective-permute-start | bytes 552968 | tf_op jit(solution)/shard_map/ppermute | solution.py:340
  54.3 35.3 %collective-permute-start.12 = (bf16[48,1920]{1,0:T(8,128)(2,1)S(1)}, bf16[48,1920]{1,0:T(8,128)(2,1)S(1)}, u32[]{:S(2)}, u32[]{:S(2)}) collective-permute-start(bf16[48,1920]{1,0:T(8,128)(2,1)S(1)} %bitcast.341), channel_id=1, source_target_pairs={{0,8},{2,10},{4,12},{6,14},{8,16},{10,18},{12,20},{14,22},{16,24},... | collective-permute-start | bytes 552968 | tf_op jit(solution)/shard_map/ppermute | solution.py:340
  94.0 20.2 %collective-permute-start.9 = (bf16[2,4,48,640]{3,2,1,0:T(8,128)(2,1)S(1)}, bf16[2,4,48,640]{3,2,1,0:T(8,128)(2,1)S(1)}, u32[]{:S(2)}, u32[]{:S(2)}) collective-permute-start(bf16[2,4,48,640]{3,2,1,0:T(8,128)(2,1)S(1)} %pad_maximum_fusion.9), channel_id=1, source_target_pairs={{0,2},{2,0},{4,6},{6,4},{8,10},{10,8},{12,14},{14,12},{16,18},{18,... | collective-permute-start | bytes 1474568 | tf_op jit(solution)/shard_map/ppermute | solution.py:330
  102.1 24.8 %collective-permute-start.18 = (bf16[2,4,48,896]{3,2,0,1:T(8,128)(2,1)}, bf16[2,4,48,896]{3,2,0,1:T(8,128)(2,1)}, u32[]{:S(2)}, u32[]{:S(2)}) collective-permute-start(bf16[2,4,48,896]{3,2,0,1:T(8,128)(2,1)} %pad_maximum_fusion.8), channel_id=1, source_target_pairs={{0,2},{2,0},{4,6},{6,4},{8,10},{10,8},{12,14},{14,12},{16,18},{18,... | collective-permute-start | bytes 2064392 | tf_op jit(solution)/shard_map/ppermute | solution.py:330
  104.7 23.7 %collective-permute-start.16 = (bf16[2,4,48,1024]{3,2,1,0:T(8,128)(2,1)}, bf16[2,4,48,1024]{3,2,1,0:T(8,128)(2,1)}, u32[]{:S(2)}, u32[]{:S(2)}) collective-permute-start(bf16[2,4,48,1024]{3,2,1,0:T(8,128)(2,1)} %pad_maximum_fusion.5), channel_id=1, source_target_pairs={{0,4},{2,6},{4,0},{6,2},{8,12},{10,14},{12,8},{14,10},{16,20},{18,... | collective-permute-start | bytes 2359304 | tf_op jit(solution)/shard_map/ppermute | solution.py:330
  116.0 31.5 %collective-permute-start.10 = (bf16[768,1152]{1,0:T(8,128)(2,1)}, bf16[768,1152]{1,0:T(8,128)(2,1)}, u32[]{:S(2)}, u32[]{:S(2)}) collective-permute-start(bf16[768,1152]{1,0:T(8,128)(2,1)} %pad_maximum_fusion.2), channel_id=1, source_target_pairs={{0,1},{1,0},{2,3},{3,2},{4,5},{5,4},{6,7},{7,6},{8,9},{9,8},{10,11... | collective-permute-start | bytes 5308424 | tf_op jit(solution)/shard_map/ppermute | solution.py:330
  132.6 38.9 %collective-permute-start.19 = (bf16[768,1920]{1,0:T(8,128)(2,1)}, bf16[768,1920]{1,0:T(8,128)(2,1)}, u32[]{:S(2)}, u32[]{:S(2)}) collective-permute-start(bf16[768,1920]{1,0:T(8,128)(2,1)} %pad_maximum_fusion), channel_id=1, source_target_pairs={{0,1},{1,0},{2,3},{3,2},{4,5},{5,4},{6,7},{7,6},{8,9},{9,8},{10,11... | collective-permute-start | bytes 8847368 | tf_op jit(solution)/shard_map/ppermute | solution.py:330
  296.5 42.1 %collective-permute-start.20 = (bf16[64,768]{0,1:T(8,128)(2,1)}, bf16[64,768]{0,1:T(8,128)(2,1)}, u32[]{:S(2)}, u32[]{:S(2)}) collective-permute-start(bf16[64,768]{0,1:T(8,128)(2,1)} %slice.126), channel_id=1, source_target_pairs={{2,0},{4,2},{6,4},{8,6},{10,8},{12,10},{14,12},{16,14},{18,16},{20... | collective-permute-start | bytes 294920 | tf_op jit(solution)/shard_map/ppermute | solution.py:318
  302.1 28.9 %all-to-all-start.1 = ((bf16[16,24,768]{2,1,0:T(8,128)(2,1)}), bf16[16,24,768]{2,1,0:T(8,128)(2,1)}, u32[]{:S(2)}, u32[]{:S(2)}) async-start(bf16[16,24,768]{2,1,0:T(8,128)(2,1)} %fusion.21), calls=%async_computation.1 | async-start | bytes 1179648 | tf_op jit(solution)/shard_map/all_to_all | solution.py:531
  319.4 32.2 %collective-permute-start.22 = (bf16[768,1536]{1,0:T(8,128)(2,1)}, bf16[768,1536]{1,0:T(8,128)(2,1)}, u32[]{:S(2)}, u32[]{:S(2)}) collective-permute-start(bf16[768,1536]{1,0:T(8,128)(2,1)} %pad_maximum_fusion.1), channel_id=1, source_target_pairs={{0,1},{1,0},{2,3},{3,2},{4,5},{5,4},{6,7},{7,6},{8,9},{9,8},{10,11... | collective-permute-start | bytes 7077896 | tf_op jit(solution)/shard_map/ppermute | solution.py:330
  330.9 27.1 %collective-permute-start.31 = (bf16[768,1536]{1,0:T(8,128)(2,1)}, bf16[768,1536]{1,0:T(8,128)(2,1)}, u32[]{:S(2)}, u32[]{:S(2)}) collective-permute-start(bf16[768,1536]{1,0:T(8,128)(2,1)} %broadcast_select_fusion), channel_id=1, source_target_pairs={{0,1},{1,0},{2,3},{3,2},{4,5},{5,4},{6,7},{7,6},{8,9},{9,8},{10,11... | collective-permute-start | bytes 7077896 | tf_op jit(solution)/shard_map/ppermute | solution.py:330
  361.1 22.2 %collective-permute-start.32 = (bf16[4,2,48,768]{3,2,0,1:T(8,128)(2,1)S(1)}, bf16[4,2,48,768]{3,2,0,1:T(8,128)(2,1)S(1)}, u32[]{:S(2)}, u32[]{:S(2)}) collective-permute-start(bf16[4,2,48,768]{3,2,0,1:T(8,128)(2,1)S(1)} %bitcast.344), channel_id=1, source_target_pairs={{0,2},{2,0},{4,6},{6,4},{8,10},{10,8},{12,14},{14,12},{16,18},{18,... | collective-permute-start | bytes 1769480 | tf_op jit(solution)/shard_map/ppermute | solution.py:330
  361.7 23.8 %collective-permute-start.34 = (bf16[4,2,48,768]{3,2,1,0:T(8,128)(2,1)S(1)}, bf16[4,2,48,768]{3,2,1,0:T(8,128)(2,1)S(1)}, u32[]{:S(2)}, u32[]{:S(2)}) collective-permute-start(bf16[4,2,48,768]{3,2,1,0:T(8,128)(2,1)S(1)} %dynamic-slice_bitcast_fusion), channel_id=1, source_target_pairs={{0,4},{2,6},{4,0},{6,2},{8,12},{10,14},{12,8},{14,10},{16,20},{18,... | collective-permute-start | bytes 1769480 | tf_op jit(solution)/shard_map/ppermute | solution.py:330
  370.8 21.0 %collective-permute-start.24 = (bf16[4,48,768]{2,1,0:T(8,128)(2,1)S(1)}, bf16[4,48,768]{2,1,0:T(8,128)(2,1)S(1)}, u32[]{:S(2)}, u32[]{:S(2)}) collective-permute-start(bf16[4,48,768]{2,1,0:T(8,128)(2,1)S(1)} %dynamic-slice_bitcast_fusion.5), channel_id=1, source_target_pairs={{0,4},{2,6},{4,0},{6,2},{8,12},{10,14},{12,8},{14,10},{16,20},{18,... | collective-permute-start | bytes 884744 | tf_op jit(solution)/shard_map/ppermute | solution.py:330
  (83 other events, 874.9 us)
Sparse Core Ops, SparseCore 0:
  16.5 81.5 all-gather.1
  212.6 108.3 reduce-scatter.1

commit v3 on v2

--- a/solution.py
+++ b/solution.py
@@ -134,11 +134,11 @@
 
 def attend(mixed_own, mixed_other, sel_col, bias_col, info, blocks, pool_rows):
     width = HEADS * HEAD
-    base = pool_rows // BLOCK
+    halo = blocks + pool_rows // BLOCK
     mixed_specs = [
-        pl.BlockSpec((pool_rows, 3 * HALF), lambda c, f: (0, 0)),
-        pl.BlockSpec((BLOCK, 3 * HALF), lambda c, f: (base + c, 0)),
-        pl.BlockSpec((BLOCK, 3 * HALF), lambda c, f: (base + c + 1, 0)),
+        pl.BlockSpec((pool_rows, 3 * HALF), lambda c, f: (blocks * BLOCK // pool_rows, 0)),
+        pl.BlockSpec((BLOCK, 3 * HALF), lambda c, f: (jnp.where(c == 0, halo, c - 1), 0)),
+        pl.BlockSpec((BLOCK, 3 * HALF), lambda c, f: (c, 0)),
     ]
     return pl.pallas_call(
         attend_kernel,
@@ -260,12 +260,16 @@
     def query_block(i):
         return jnp.minimum(i, blocks - 1)
 
+    def before_block(i, f):
+        return (jnp.where(i == 0, blocks + base, query_block(i) - 1), 0)
+
     def out_block(i, f):
-        return (jnp.where(i > blocks, i - blocks - 1, base + i), 0)
+        row = jnp.where(i == 0, blocks + base, i - 1)
+        return (jnp.where(i > blocks, i - 1, row), 0)
 
     mixed_specs = [
-        pl.BlockSpec((BLOCK, 3 * HALF), lambda i, f: (base + query_block(i), 0)),
-        pl.BlockSpec((BLOCK, 3 * HALF), lambda i, f: (base + query_block(i) + 1, 0)),
+        pl.BlockSpec((BLOCK, 3 * HALF), before_block),
+        pl.BlockSpec((BLOCK, 3 * HALF), lambda i, f: (query_block(i), 0)),
     ]
     rows = pool_rows + (blocks + 1) * BLOCK
     return pl.pallas_call(
@@ -312,6 +316,478 @@
     )
 
 
+ROWS = 256
+CHUNK = 512
+MIB = 1024 * 1024
+
+
+def params(mib):
+    return pltpu.CompilerParams(vmem_limit_bytes=mib * MIB)
+
+
+def shape(rows, columns, dtype=jnp.bfloat16):
+    return jax.ShapeDtypeStruct((rows, columns), dtype)
+
+
+def cost(flops, moved):
+    return pl.CostEstimate(flops=flops, bytes_accessed=moved, transcendentals=0)
+
+
+def lanes_at(index, size):
+    return pl.ds(pl.multiple_of(index * size, 128), size)
+
+
+def pool_kernel(tokens_ref, out_ref):
+    for b in range(out_ref.shape[0]):
+        unit, _ = standardize(tokens_ref[b * BLOCK : (b + 1) * BLOCK].astype(jnp.float32))
+        out_ref[b : b + 1] = jnp.mean(unit, axis=0, keepdims=True)
+
+
+def pool(tokens):
+    rows, width = tokens.shape
+    return pl.pallas_call(
+        pool_kernel,
+        out_shape=shape(rows // BLOCK, width, jnp.float32),
+        compiler_params=params(16),
+        cost_estimate=cost(2_000_000_000, 6_000_000),
+        name="pool",
+    )(tokens)
+
+
+def project_kernel(
+    tokens_ref, pool_ref, halo_ref, vec_ref, own_ref, other_ref, normed_ref, unit_ref, m_own, m_other
+):
+    j = pl.program_id(0)
+
+    @pl.when(j == 0)
+    def _():
+        gain, bias = vec_ref[0:1], vec_ref[1:2]
+        start = 0
+        for ref in (tokens_ref, pool_ref, halo_ref):
+            for r in range(0, ref.shape[0], BLOCK):
+                unit = ref[r : r + BLOCK].astype(jnp.float32)
+                if ref is not pool_ref:
+                    unit, _ = standardize(unit)
+                rows = slice(start, start + BLOCK)
+                unit_ref[rows] = unit.astype(jnp.bfloat16)
+                normed_ref[rows] = (unit * gain + bias).astype(jnp.bfloat16)
+                start += BLOCK
+
+    @pl.when(j < 3)
+    def _():
+        m_own[...] = dot_nn(normed_ref[...], own_ref[...]).astype(jnp.bfloat16)
+
+    @pl.when(j >= 3)
+    def _():
+        m_other[...] = dot_nn(normed_ref[...], other_ref[...]).astype(jnp.bfloat16)
+
+
+def project(tokens, unit_pool, halo, vectors, own, other):
+    width = tokens.shape[1]
+    total = tokens.shape[0] + unit_pool.shape[0] + halo.shape[0]
+
+    def first(j):
+        return (0, jnp.minimum(j, 2))
+
+    def second(j):
+        return (0, jnp.maximum(j - 3, 0))
+
+    whole = lambda j: (0, 0)
+    return pl.pallas_call(
+        project_kernel,
+        grid=(6,),
+        in_specs=[
+            pl.BlockSpec(tokens.shape, whole),
+            pl.BlockSpec(unit_pool.shape, whole),
+            pl.BlockSpec(halo.shape, whole),
+            pl.BlockSpec(vectors.shape, whole),
+            pl.BlockSpec((width, HALF), first),
+            pl.BlockSpec((width, HALF), second),
+        ],
+        out_specs=[
+            pl.BlockSpec((total, width), whole),
+            pl.BlockSpec((total, width), whole),
+            pl.BlockSpec((total, HALF), first),
+            pl.BlockSpec((total, HALF), second),
+        ],
+        out_shape=[
+            shape(total, width),
+            shape(total, width),
+            shape(total, 3 * HALF),
+            shape(total, 3 * HALF),
+        ],
+        compiler_params=params(40),
+        cost_estimate=cost(6_000_000_000, 12_000_000),
+        name="project",
+    )(tokens, unit_pool, halo, vectors, own, other)
+
+
+def after_kernel(info_ref, att_ref, own_ref, other_ref, tokens_ref, vec_ref, after_ref, normed_ref):
+    core = info_ref[1]
+    half = own_ref.shape[1]
+    after_ref[:, lanes_at(core, half)] = dot_nn(att_ref[...], own_ref[...])
+    after_ref[:, lanes_at(1 - core, half)] = dot_nn(att_ref[...], other_ref[...])
+    after = tokens_ref[...].astype(jnp.float32) + after_ref[...]
+    after_ref[...] = after
+    unit, _ = standardize(after)
+    normed_ref[...] = (unit * vec_ref[2:3] + vec_ref[3:4]).astype(jnp.bfloat16)
+
+
+def out_columns(own):
+    width = own.shape[0]
+    half = width // 2
+    return pl.BlockSpec((width, half), lambda i, f: (0, own.shape[1] // half - 1))
+
+
+def after_attention(attended, own, other, tokens, vectors, info):
+    count, width = tokens.shape
+    row = pl.BlockSpec((ROWS, width), lambda i, f: (i, 0))
+    return pl.pallas_call(
+        after_kernel,
+        grid_spec=pltpu.PrefetchScalarGridSpec(
+            num_scalar_prefetch=1,
+            grid=(count // ROWS,),
+            in_specs=[
+                row,
+                out_columns(own),
+                out_columns(other),
+                row,
+                pl.BlockSpec(vectors.shape, lambda i, f: (0, 0)),
+            ],
+            out_specs=[row, row],
+        ),
+        out_shape=[shape(count, width, jnp.float32), shape(count, width)],
+        compiler_params=params(24),
+        cost_estimate=cost(2_000_000_000, 10_000_000),
+        name="after_attention",
+    )(info, attended, own, other, tokens, vectors)
+
+
+def up_kernel(
+    info_ref, n2_ref, dy_ref, own_ref, other_ref, active_ref, slope_ref, gd_own, gd_other, grad_ref
+):
+    j = pl.program_id(0)
+    core = info_ref[1]
+    side = gd_own.shape[1]
+    half = pl.num_programs(0) // 2
+    weight = jnp.where(j < half, own_ref[...], other_ref[...])
+    root = (2.0 / 3.141592653589793) ** 0.5
+    for r in range(0, n2_ref.shape[0], ROWS):
+        rows = slice(r, r + ROWS)
+        u = dot_nn(n2_ref[rows], weight)
+        square = u * u
+        t = jnp.tanh(root * u * (1.0 + 0.044715 * square))
+        upper = 0.5 * (1.0 + t)
+        active_ref[rows] = (u * upper).astype(jnp.bfloat16)
+        bend = 0.5 * u * (1.0 - t * t) * (root * (1.0 + 3.0 * 0.044715 * square))
+        slope_ref[rows] = (upper + bend).astype(jnp.bfloat16)
+    grad_ref[...] = dot_tn(active_ref[...], dy_ref[...]).astype(jnp.bfloat16)
+    gd_own[...] = grad_ref[:, lanes_at(core, side)]
+    gd_other[...] = grad_ref[:, lanes_at(1 - core, side)]
+
+
+def ff_maps(hidden):
+    steps = hidden // CHUNK
+    half = steps // 2
+    own = lambda j, f: (0, jnp.minimum(j, half - 1))
+    other = lambda j, f: (0, jnp.maximum(j - half, 0))
+    place = lambda j, f: lax.rem(f[1] * half + j, steps)
+    return steps, own, other, place
+
+
+def up_project(normed_two, upstream, own, other, info, hidden):
+    count, width = normed_two.shape
+    steps, first, second, place = ff_maps(hidden)
+    whole = pl.BlockSpec((count, width), lambda j, f: (0, 0))
+    columns = pl.BlockSpec((count, CHUNK), lambda j, f: (0, place(j, f)))
+    rows = pl.BlockSpec((CHUNK, width // 2), lambda j, f: (place(j, f), 0))
+    return pl.pallas_call(
+        up_kernel,
+        grid_spec=pltpu.PrefetchScalarGridSpec(
+            num_scalar_prefetch=1,
+            grid=(steps,),
+            in_specs=[
+                whole,
+                whole,
+                pl.BlockSpec((width, CHUNK), first),
+                pl.BlockSpec((width, CHUNK), second),
+            ],
+            out_specs=[
+                columns,
+                columns,
+                rows,
+                rows,
+            ],
+            scratch_shapes=[pltpu.VMEM((CHUNK, width), jnp.bfloat16)],
+        ),
+        out_shape=[
+            shape(count, hidden),
+            shape(count, hidden),
+            shape(hidden, width // 2),
+            shape(hidden, width // 2),
+        ],
+        compiler_params=params(40),
+        cost_estimate=cost(14_000_000_000, 25_000_000),
+        name="up_project",
+    )(info, normed_two, upstream, own, other)
+
+
+def down_kernel(
+    info_ref,
+    n2_ref,
+    dy_ref,
+    slope_ref,
+    down_ref,
+    own_ref,
+    other_ref,
+    dn2_ref,
+    g_own,
+    g_other,
+    dh_ref,
+):
+    j = pl.program_id(0)
+    half = pl.num_programs(0) // 2
+    weight = jnp.where(j < half, own_ref[...], other_ref[...])
+
+    @pl.when(j == 0)
+    def _():
+        dn2_ref[...] = jnp.zeros_like(dn2_ref)
+
+    for r in range(0, n2_ref.shape[0], ROWS):
+        rows = slice(r, r + ROWS)
+        dactive = dot_nt(dy_ref[rows], down_ref[...])
+        dh = (dactive * slope_ref[rows].astype(jnp.float32)).astype(jnp.bfloat16)
+        dh_ref[rows] = dh
+        dn2_ref[rows] += dot_nt(dh, weight)
+    grad = dot_tn(n2_ref[...], dh_ref[...]).astype(jnp.bfloat16)
+
+    @pl.when(j < half)
+    def _():
+        g_own[...] = grad
+
+    @pl.when(j >= half)
+    def _():
+        g_other[...] = grad
+
+
+def down_back(normed_two, upstream, slope, mat_down, own, other, info, hidden):
+    count, width = normed_two.shape
+    steps, first, second, place = ff_maps(hidden)
+    whole = pl.BlockSpec((count, width), lambda j, f: (0, 0))
+    return pl.pallas_call(
+        down_kernel,
+        grid_spec=pltpu.PrefetchScalarGridSpec(
+            num_scalar_prefetch=1,
+            grid=(steps,),
+            in_specs=[
+                whole,
+                whole,
+                pl.BlockSpec((count, CHUNK), lambda j, f: (0, place(j, f))),
+                pl.BlockSpec((CHUNK, width), lambda j, f: (place(j, f), 0)),
+                pl.BlockSpec((width, CHUNK), first),
+                pl.BlockSpec((width, CHUNK), second),
+            ],
+            out_specs=[
+                whole,
+                pl.BlockSpec((width, CHUNK), first),
+                pl.BlockSpec((width, CHUNK), second),
+            ],
+            scratch_shapes=[pltpu.VMEM((count, CHUNK), jnp.bfloat16)],
+        ),
+        out_shape=[
+            shape(count, width, jnp.float32),
+            shape(width, hidden // 2),
+            shape(width, hidden // 2),
+        ],
+        compiler_params=params(40),
+        cost_estimate=cost(20_000_000_000, 25_000_000),
+        name="down_back",
+    )(info, normed_two, upstream, slope, mat_down, own, other)
+
+
+def after_back_kernel(
+    info_ref,
+    after_ref,
+    dn2_ref,
+    dy_ref,
+    att_ref,
+    vec_ref,
+    own_ref,
+    other_ref,
+    dafter_ref,
+    datt_ref,
+    go_own,
+    go_other,
+    sums_ref,
+    acc,
+    low,
+):
+    i = pl.program_id(0)
+    core = info_ref[1]
+    half = own_ref.shape[1]
+
+    @pl.when(i == 0)
+    def _():
+        sums_ref[...] = jnp.zeros_like(sums_ref)
+        acc[...] = jnp.zeros_like(acc)
+
+    unit, scale = standardize(after_ref[...])
+    dn2 = dn2_ref[...]
+    sums_ref[0:1] += jnp.sum(dn2 * unit, axis=0, keepdims=True)
+    sums_ref[1:2] += jnp.sum(dn2, axis=0, keepdims=True)
+    dafter = dy_ref[...].astype(jnp.float32) + standardize_back(unit, scale, dn2 * vec_ref[2:3])
+    dafter_ref[...] = dafter
+    low[...] = dafter.astype(jnp.bfloat16)
+    datt = dot_nt(low[:, lanes_at(core, half)], own_ref[...])
+    datt += dot_nt(low[:, lanes_at(1 - core, half)], other_ref[...])
+    datt_ref[...] = datt.astype(jnp.bfloat16)
+    acc[...] += dot_tn(att_ref[...], low[...])
+
+    @pl.when(i == pl.num_programs(0) - 1)
+    def _():
+        go_own[...] = acc[:, lanes_at(core, half)].astype(jnp.bfloat16)
+        go_other[...] = acc[:, lanes_at(1 - core, half)].astype(jnp.bfloat16)
+
+
+def after_back(after, dn2, upstream, attended, vectors, own, other, info):
+    count, width = after.shape
+    row = pl.BlockSpec((ROWS, width), lambda i, f: (i, 0))
+    return pl.pallas_call(
+        after_back_kernel,
+        grid_spec=pltpu.PrefetchScalarGridSpec(
+            num_scalar_prefetch=1,
+            grid=(count // ROWS,),
+            in_specs=[
+                row,
+                row,
+                row,
+                row,
+                pl.BlockSpec(vectors.shape, lambda i, f: (0, 0)),
+                out_columns(own),
+                out_columns(other),
+            ],
+            out_specs=[
+                row,
+                row,
+                pl.BlockSpec((width, width // 2), lambda i, f: (0, 0)),
+                pl.BlockSpec((width, width // 2), lambda i, f: (0, 0)),
+                pl.BlockSpec((8, width), lambda i, f: (0, 0)),
+            ],
+            scratch_shapes=[
+                pltpu.VMEM((width, width), jnp.float32),
+                pltpu.VMEM((ROWS, width), jnp.bfloat16),
+            ],
+        ),
+        out_shape=[
+            shape(count, width, jnp.float32),
+            shape(count, width),
+            shape(width, width // 2),
+            shape(width, width // 2),
+            shape(8, width, jnp.float32),
+        ],
+        compiler_params=params(32),
+        cost_estimate=cost(4_000_000_000, 16_000_000),
+        name="after_back",
+    )(info, after, dn2, upstream, attended, vectors, own, other)
+
+
+def project_back_kernel(dm_own, dm_other, own_ref, other_ref, unit_ref, dn_ref, sums_ref):
+    @pl.when(pl.program_id(0) == 0)
+    def _():
+        sums_ref[...] = jnp.zeros_like(sums_ref)
+
+    dn = dot_nt(dm_own[...], own_ref[...]) + dot_nt(dm_other[...], other_ref[...])
+    dn_ref[...] = dn
+    sums_ref[0:1] += jnp.sum(dn * unit_ref[...].astype(jnp.float32), axis=0, keepdims=True)
+    sums_ref[1:2] += jnp.sum(dn, axis=0, keepdims=True)
+
+
+def project_back(dm_own, dm_other, own, other, unit):
+    total, width = unit.shape
+    groups = total // BLOCK
+    rows = BLOCK * max(n for n in range(1, 8) if groups % n == 0)
+    row = lambda i: (i, 0)
+    whole = pl.BlockSpec((width, 3 * HALF), lambda i: (0, 0))
+    return pl.pallas_call(
+        project_back_kernel,
+        grid=(total // rows,),
+        in_specs=[
+            pl.BlockSpec((rows, 3 * HALF), row),
+            pl.BlockSpec((rows, 3 * HALF), row),
+            whole,
+            whole,
+            pl.BlockSpec((rows, width), row),
+        ],
+        out_specs=[pl.BlockSpec((rows, width), row), pl.BlockSpec((8, width), lambda i: (0, 0))],
+        out_shape=[shape(total, width, jnp.float32), shape(8, width, jnp.float32)],
+        compiler_params=params(32),
+        cost_estimate=cost(6_000_000_000, 16_000_000),
+        name="project_back",
+    )(dm_own, dm_other, own, other, unit)
+
+
+def input_kernel(tokens_ref, dn_ref, dafter_ref, pool_ref, next_ref, vec_ref, out_ref):
+    i = pl.program_id(0)
+    gain = vec_ref[0:1]
+    per = tokens_ref.shape[0] // BLOCK
+    last = (i == pl.num_programs(0) - 1).astype(jnp.float32)
+    for b in range(per):
+        rows = slice(b * BLOCK, (b + 1) * BLOCK)
+        unit, scale = standardize(tokens_ref[rows].astype(jnp.float32))
+        dn = dn_ref[rows] + pool_ref[pl.ds(i * per + b, 1)] * (1.0 / BLOCK)
+        if b == per - 1:
+            dn += next_ref[...].astype(jnp.float32) * last
+        out_ref[rows] = dafter_ref[rows] + standardize_back(unit, scale, dn * gain)
+
+
+def input_back(tokens, dnormed, dafter, from_pool, from_next, vectors):
+    count, width = tokens.shape
+    row = pl.BlockSpec((ROWS, width), lambda i: (i, 0))
+    whole = lambda i: (0, 0)
+    return pl.pallas_call(
+        input_kernel,
+        grid=(count // ROWS,),
+        in_specs=[
+            row,
+            row,
+            row,
+            pl.BlockSpec(from_pool.shape, whole),
+            pl.BlockSpec(from_next.shape, whole),
+            pl.BlockSpec(vectors.shape, whole),
+        ],
+        out_specs=row,
+        out_shape=shape(count, width, jnp.float32),
+        compiler_params=params(24),
+        cost_estimate=cost(3_000_000_000, 12_000_000),
+        name="input_back",
+    )(tokens, dnormed, dafter, from_pool, from_next, vectors)
+
+
+def output_kernel(after_ref, active_ref, down_ref, out_ref):
+    value = after_ref[...] + dot_nn(active_ref[...], down_ref[...])
+    out_ref[...] = value.astype(jnp.bfloat16)
+
+
+def layer_output(after, active, mat_down):
+    count, width = after.shape
+    hidden = active.shape[1]
+    row = lambda i: (i, 0)
+    return pl.pallas_call(
+        output_kernel,
+        grid=(count // ROWS,),
+        in_specs=[
+            pl.BlockSpec((ROWS, width), row),
+            pl.BlockSpec((ROWS, hidden), row),
+            pl.BlockSpec((hidden, width), lambda i: (0, 0)),
+        ],
+        out_specs=pl.BlockSpec((ROWS, width), row),
+        out_shape=shape(count, width),
+        compiler_params=params(32),
+        cost_estimate=cost(6_000_000_000, 16_000_000),
+        name="layer_output",
+    )(after, active, mat_down)
+
+
 def shift_seq(value, distance):
     size = lax.axis_size("seq")
     route = [(i - distance, i) for i in range(size) if 0 <= i - distance < size]
@@ -320,65 +796,122 @@
 
 BOTH = ("seq", "batch")
 
-def flip_route(axis_size, bit):
-    return [(i, i ^ bit) for i in range(axis_size)]
+
+def follows(value, *earlier):
+    return lax.optimization_barrier((value, earlier))[0]
+
+
+def flip_route(size, bit):
+    return [(i, i ^ bit) for i in range(size)]
+
 
 def ring_route(size, stride, steps):
     return [(i, (i + stride * steps) % size) for i in range(size)]
 
+
 def swap(value, axis, bit):
     return lax.ppermute(value, axis, flip_route(lax.axis_size(axis), bit))
 
+
 def in_order(bit, own, other):
     return jnp.stack([jnp.where(bit == 0, own, other), jnp.where(bit == 0, other, own)])
 
-def gather_seq(slab, cut):
-    size = lax.axis_size("seq")
-    at = lax.axis_index("seq")
-    layers = size // 4
-    z, y, x = at // 4, at // 2 % 2, at % 2
-    got = [slab] + [lax.ppermute(slab, "seq", ring_route(size, 4, k)) for k in range(1, layers)]
-    stack = jnp.stack(got)
-    line = jnp.concatenate([lax.dynamic_slice_in_dim(stack, (z - k) % layers, 1, 0) for k in range(layers)], 0)
-    first, second = line[:, :, :cut], line[:, :, cut:]
-    first_x = swap(first, "seq", 1)
-    second_y = swap(second, "seq", 2)
-    first = in_order(x, first, first_x)
-    second = in_order(y, second, second_y)
-    first_y = swap(first, "seq", 2)
-    second_x = swap(second, "seq", 1)
-    first = in_order(y, first, first_y)
-    second = in_order(x, second, second_x)
-    rows = size * slab.shape[0]
-    first = jnp.transpose(first, (2, 0, 1, 3, 4)).reshape(rows, cut)
-    second = jnp.transpose(second, (2, 1, 0, 3, 4)).reshape(rows, slab.shape[1] - cut)
-    return jnp.concatenate([first, second], 1)
 
 def pick(value, index, axis):
     return lax.dynamic_index_in_dim(value, index, axis, keepdims=False)
 
+
 def add(a, b):
     return (a.astype(jnp.float32) + b.astype(jnp.float32)).astype(jnp.bfloat16)
 
-def scatter_seq(full, cut):
+
+def place():
+    at = lax.axis_index("seq")
+    return at // 4, at // 2 % 2, at % 2
+
+
+def send_line(slab):
     size = lax.axis_size("seq")
-    at = lax.axis_index("seq")
+    return [lax.ppermute(slab, "seq", ring_route(size, 4, k)) for k in range(1, size // 4)]
+
+
+def join_line(slab, got):
+    z = place()[0]
+    stack = jnp.stack([slab] + got)
+    layers = stack.shape[0]
+    parts = [lax.dynamic_slice_in_dim(stack, (z - k) % layers, 1, 0) for k in range(layers)]
+    return jnp.concatenate(parts, 0)
+
+
+def send_near(line, cut):
+    first, second = line[:, :, :cut], line[:, :, cut:]
+    return first, second, swap(first, "seq", 1), swap(second, "seq", 2)
+
+
+def join_near(first, second, first_got, second_got):
+    _, y, x = place()
+    return in_order(x, first, first_got), in_order(y, second, second_got)
+
+
+def send_far(first, second):
+    return swap(first, "seq", 2), swap(second, "seq", 1)
+
+
+def join_far(first, second, first_got, second_got):
+    _, y, x = place()
+    first = jnp.transpose(in_order(y, first, first_got), (2, 0, 1, 3, 4))
+    second = jnp.transpose(in_order(x, second, second_got), (2, 1, 0, 3, 4))
+    rows = first.shape[3] * lax.axis_size("seq")
+    return first.reshape(rows, -1), second.reshape(rows, -1)
+
+
+def split_grid(full, cut, axis=4):
+    grid = full.reshape(lax.axis_size("seq") // 4, 2, 2, -1, full.shape[1])
+    return jnp.split(grid, [cut], axis)
+
+
+def drop_near(first, second):
+    _, y, x = place()
+    return pick(first, 1 - x, 2), pick(second, 1 - y, 1)
+
+
+def keep_near(first, second, first_got, second_got):
+    _, y, x = place()
+    return add(pick(first, x, 2), first_got), add(pick(second, y, 1), second_got)
+
+
+def drop_far(first, second):
+    _, y, x = place()
+    return pick(first, 1 - y, 1), pick(second, 1 - x, 1)
+
+
+def keep_far(first, second, first_got, second_got, axis=2):
+    _, y, x = place()
+    parts = [add(pick(first, y, 1), first_got), add(pick(second, x, 1), second_got)]
+    return jnp.concatenate(parts, axis)
+
+
+def swap_near(dropped):
+    return swap(dropped[0], "seq", 1), swap(dropped[1], "seq", 2)
+
+
+def swap_far(dropped):
+    return swap(dropped[0], "seq", 2), swap(dropped[1], "seq", 1)
+
+
+def scatter_line(line):
+    z = place()[0]
+    size = lax.axis_size("seq")
     layers = size // 4
-    z, y, x = at // 4, at // 2 % 2, at % 2
-    grid = full.reshape(layers, 2, 2, -1, full.shape[1])
-    first, second = grid[..., :cut], grid[..., cut:]
-    first_got = swap(pick(first, 1 - x, 2), "seq", 1)
-    second_got = swap(pick(second, 1 - y, 1), "seq", 2)
-    first = add(pick(first, x, 2), first_got)
-    second = add(pick(second, y, 1), second_got)
-    first_got = swap(pick(first, 1 - y, 1), "seq", 2)
-    second_got = swap(pick(second, 1 - x, 1), "seq", 1)
-    line = jnp.concatenate([add(pick(first, y, 1), first_got), add(pick(second, x, 1), second_got)], -1)
-    total = pick(line, z, 0).astype(jnp.float32)
-    for k in range(1, layers):
-        got = lax.ppermute(pick(line, (z + k) % layers, 0), "seq", ring_route(size, 4, k))
-        total = total + got.astype(jnp.float32)
-    return total
+    got = [
+        lax.ppermute(pick(line, (z + k) % layers, 0), "seq", ring_route(size, 4, k))
+        for k in range(1, layers)
+    ]
+    return pick(line, z, 0), got
+
+
+def sum_line(own, got):
+    return sum((g.astype(jnp.float32) for g in got), own.astype(jnp.float32))
 
 
 def paired():
@@ -401,84 +934,82 @@
     return jnp.transpose(parts, (1, 2, 0, 3)).reshape(rows, 2 * columns)
 
 
-def gather_slab(halves):
+def rows_of_side(total):
     side = side_index()
-    mine, theirs = pick(halves, side, 0), pick(halves, 1 - side, 0)
-    got = swap(theirs, "batch", 1)
-    return in_order(side, mine, got).reshape(-1, halves.shape[2])
-
-
-def gather_halves(halves, cut):
-    if paired():
-        own = gather_seq(gather_slab(halves), cut)
-        return own, swap(own, "batch", 1)
-    full = lax.all_gather(halves, BOTH, axis=1, tiled=True)
-    return pick(full, side_index(), 0), pick(full, 1 - side_index(), 0)
-
-
-def scatter_halves(own, other, cut):
-    side = side_index()
-    if paired():
-        mixed = add(own, swap(other, "batch", 1))
-        total = scatter_seq(mixed, cut)
-        total = total.reshape(2, -1, total.shape[1])
-        got = swap(pick(total, 1 - side, 0), "batch", 1)
-        return in_order(side, pick(total, side, 0), got)
-    full = in_order(side, own, other)
-    return lax.psum_scatter(full, BOTH, scatter_dimension=1, tiled=True).astype(jnp.float32)
-
-
-def everyone(rows):
-    size = lax.axis_size("seq")
-    return lax.all_to_all(jnp.broadcast_to(rows, (size,) + rows.shape), "seq", 0, 0)
-
-
-def gather_vectors(vectors):
-    return lax.all_gather(vectors, BOTH, axis=1, tiled=True).astype(jnp.float32)
+    total = total.reshape(2, -1, total.shape[1])
+    got = swap(pick(total, 1 - side, 0), "batch", 1)
+    return in_order(side, pick(total, side, 0), got)
 
 
 def local(
     inputs, selection, cotangent, ln1_gain, ln1_bias, w_qkv, w_out, ln2_gain, ln2_bias, w_up, w_down
 ):
     bf16, f32 = jnp.bfloat16, jnp.float32
-    tokens_low = inputs[0]
+    tokens = inputs[0]
     chosen = selection[0]
-    count, width = tokens_low.shape
+    upstream = cotangent[0]
+    count, width = tokens.shape
+    hidden = w_up.shape[1]
     blocks = count // BLOCK
     size = lax.axis_size("seq")
     pool_rows = blocks * size
     at = lax.axis_index("seq")
     side = side_index()
+    fast = paired()
+
+    half_qkv = halves_of(w_qkv, 3)
+    half_uo = jnp.concatenate([halves_of(w_up, 1), halves_of(w_out, 1)], 2)
     vectors = jnp.stack([ln1_gain, ln1_bias, ln2_gain, ln2_bias])
-
-    own_qkv, other_qkv = gather_halves(halves_of(w_qkv, 3), 512)
-    out_up = jnp.concatenate([halves_of(w_out, 1), halves_of(w_up, 1)], 2)
-    own_ou, other_ou = gather_halves(out_up, 1024)
+    if fast:
+        columns = jnp.pad(vectors.T, ((0, 0), (0, 124)))
+        columns = jnp.broadcast_to(columns, (2,) + columns.shape)
+        bundle = jnp.concatenate([columns, half_qkv, half_uo], 2)
+        got = swap(pick(bundle, 1 - side, 0), "batch", 1)
+        slab = in_order(side, pick(bundle, side, 0), got).reshape(-1, bundle.shape[2])
+        third = width // 3
+        per = slab.shape[0] // 3
+        pooled = pool(tokens).astype(bf16).reshape(per, 3, third)
+        pooled = jnp.transpose(pooled, (1, 0, 2)).reshape(-1, third)
+        front = third + 128
+        edge = 128 + half_qkv.shape[2]
+        slab_q = jnp.concatenate([pooled, slab[:, :edge]], 1)
+        slab_u = slab[:, edge:]
+        line_got = send_line(slab_q)
+        halo = shift_seq(follows(tokens[-BLOCK:], slab_q), 1)
+        line_got_u = send_line(follows(slab_u, halo))
+        line_q = join_line(slab_q, line_got)
+        near = send_near(line_q, 768)
+        wide_q = join_near(*near)
+        far = send_far(*wide_q)
+        line_u = join_line(slab_u, follows(line_got_u, wide_q))
+        near_u = send_near(line_u, 1024)
+        first, second = join_far(*wide_q, *far)
+        own_qkv = jnp.concatenate([first[:, front:], second], 1)
+        other_qkv = swap(own_qkv, "batch", 1)
+        unit_pool = jnp.transpose(first[:, :third].reshape(size, 3, per, third), (0, 2, 1, 3))
+        unit_pool = unit_pool.reshape(pool_rows, width)
+        vectors = first[:, third : third + 4].T.astype(f32)
+        wide_u = join_near(*follows(near_u, own_qkv))
+        far_u = send_far(*wide_u)
+        other_qkv = follows(other_qkv, wide_u)
+    else:
+        gathered = lax.all_gather(half_qkv, BOTH, axis=1, tiled=True)
+        own_qkv, other_qkv = pick(gathered, side, 0), pick(gathered, 1 - side, 0)
+        gathered = lax.all_gather(half_uo, BOTH, axis=1, tiled=True)
+        own_uo, other_uo = pick(gathered, side, 0), pick(gathered, 1 - side, 0)
+        halo = shift_seq(tokens[-BLOCK:], 1)
+        unit_pool = lax.all_gather(pool(tokens).astype(bf16), "seq", axis=0, tiled=True)
+        vectors = lax.all_gather(vectors, BOTH, axis=1, tiled=True).astype(f32)
     mat_down = lax.all_gather(w_down, BOTH, axis=0, tiled=True)
-    mat_out = whole_of(in_order(side, own_ou[:, : width // 2], other_ou[:, : width // 2]), 1)
-    mat_up = whole_of(in_order(side, own_ou[:, width // 2 :], other_ou[:, width // 2 :]), 1)
-
-    tokens = tokens_low.astype(f32)
-    unit, unit_scale = standardize(tokens)
-    unit_halo, _ = standardize(shift_seq(tokens_low[-BLOCK:], 1).astype(f32))
-    pooled = jnp.mean(unit.reshape(blocks, BLOCK, width), axis=1).astype(bf16)
-    if paired():
-        chip = in_order(side, vectors, swap(vectors, "batch", 1))
-        chip = jnp.transpose(chip, (1, 0, 2)).reshape(1, -1)
-        span = chip.shape[1]
-        chip = jnp.pad(chip, ((0, 7), (0, width - span)))
-        got = everyone(jnp.concatenate([pooled, chip], 0))
-        unit_pool = got[:, :blocks].reshape(pool_rows, width)
-        vectors = got[:, blocks, :span].reshape(size, 4, span // 4)
-        vectors = jnp.transpose(vectors, (1, 0, 2)).reshape(4, width).astype(f32)
-    else:
-        unit_pool = lax.all_gather(pooled, "seq", axis=0, tiled=True)
-        vectors = lax.all_gather(vectors, BOTH, axis=1, tiled=True).astype(f32)
-    gain_one, bias_one, gain_two, bias_two = vectors
-    unit_ext = jnp.concatenate([unit_pool.astype(f32), unit_halo, unit], 0)
-    normed = (unit_ext * gain_one + bias_one).astype(bf16)
-    mixed_own = dot_nn(normed, own_qkv).astype(bf16)
-    mixed_other = dot_nn(normed, other_qkv).astype(bf16)
+    vectors = jnp.pad(vectors, ((0, 4), (0, 0)))
+
+    normed, unit, mixed_own, mixed_other = project(
+        tokens, unit_pool, halo, vectors, own_qkv, other_qkv
+    )
+    if fast:
+        own_uo = jnp.concatenate(join_far(*wide_u, *follows(far_u, mixed_own)), 1)
+        other_uo = swap(own_uo, "batch", 1)
+        mixed_own = follows(mixed_own, own_uo)
 
     block_ids = at * blocks + jnp.arange(blocks, dtype=jnp.int32)
     flat = chosen.reshape(blocks * TOPK)
@@ -487,73 +1018,113 @@
     attended, probs, picks = attend(
         mixed_own, mixed_other, flat[:, None], far_bias, info, blocks, pool_rows
     )
-
-    after = tokens + dot_nn(attended, mat_out)
-    unit_two, scale_two = standardize(after)
-    normed_two = (unit_two * gain_two + bias_two).astype(bf16)
-    hidden = dot_nn(normed_two, mat_up)
-    active, gelu_back = jax.vjp(partial(jax.nn.gelu, approximate=True), hidden)
-    active = active.astype(bf16)
-    output = (after + dot_nn(active, mat_down)).astype(bf16)
-
-    upstream = cotangent[0]
-    dhidden = gelu_back(dot_nt(upstream, mat_down))[0].astype(bf16)
-    grad_down = dot_tn(active, upstream).astype(bf16)
-    grad_up = in_order(side, *jnp.split(dot_tn(normed_two, dhidden).astype(bf16), 2, axis=1))
-    dnormed_two = dot_nt(dhidden, mat_up)
-    grad_gain_two = jnp.sum(dnormed_two * unit_two, axis=0)
-    grad_bias_two = jnp.sum(dnormed_two, axis=0)
-    dafter = upstream.astype(f32) + standardize_back(unit_two, scale_two, dnormed_two * gain_two)
-    dafter_low = dafter.astype(bf16)
-    grad_out = in_order(side, *jnp.split(dot_tn(attended, dafter_low).astype(bf16), 2, axis=1))
-    dattended = dot_nt(dafter_low, mat_out).astype(bf16)
-    own_down = lax.psum_scatter(grad_down, BOTH, scatter_dimension=0, tiled=True).astype(f32)
-    sum_up = scatter_halves(grad_up[0], grad_up[1], 768)
+    after, normed_two = after_attention(attended, own_uo, other_uo, tokens, vectors, info)
+    active, slope, down_own, down_other = up_project(
+        normed_two, upstream, own_uo, other_uo, info, hidden
+    )
+    if fast:
+        down_got = swap(down_other, "batch", 1)
+        slope = follows(slope, down_other)
+    dn2, up_own, up_other = down_back(
+        normed_two, upstream, slope, mat_down, own_uo, other_uo, info, hidden
+    )
+    if fast:
+        up_got = swap(up_other, "batch", 1)
+        grid_d = split_grid(add(down_own, follows(down_got, dn2)), hidden // size // 2, 3)
+        drop_d = drop_near(*grid_d)
+        near_d = swap_near(drop_d)
+        dn2 = follows(dn2, drop_d)
+    dafter, dattended, out_own, out_other, sums_two = after_back(
+        after, dn2, upstream, attended, vectors, own_uo, other_uo, info
+    )
+    if fast:
+        out_got = swap(out_other, "batch", 1)
+        kept_d = keep_near(*grid_d, *follows(near_d, dattended))
+        drop_d = drop_far(*kept_d)
+        far_d = swap_far(drop_d)
+        up_sum = add(up_own, follows(up_got, dattended))
+        out_sum = add(out_own, follows(out_got, drop_d))
+        grid_u = split_grid(jnp.concatenate([up_sum, out_sum], 1), 1024)
+        drop_u = drop_near(*grid_u)
+        near_u = swap_near(drop_u)
+        dattended = follows(dattended, drop_u)
 
     dmixed_own, dmixed_other = attend_back(
         mixed_own, mixed_other, flat[None, :], info, picks, probs, dattended, blocks, pool_rows
     )
+    if fast:
+        line_d = keep_far(*kept_d, *follows(far_d, dmixed_own), axis=1)
+        line_d, got_d = scatter_line(line_d)
+        kept_u = keep_near(*grid_u, *follows(near_u, dmixed_own))
+        drop_u = drop_far(*kept_u)
+        far_u = swap_far(drop_u)
+        dmixed_other, dmixed_own = follows((dmixed_other, dmixed_own), drop_u, line_d)
     grad_other = dot_tn(normed, dmixed_other).astype(bf16)
+    if fast:
+        grad_got = swap(grad_other, "batch", 1)
+        dmixed_own = follows(dmixed_own, grad_other)
     grad_own = dot_tn(normed, dmixed_own).astype(bf16)
-    dnormed = dot_nt(dmixed_own, own_qkv) + dot_nt(dmixed_other, other_qkv)
-    grad_gain_one = jnp.sum(dnormed * unit_ext, axis=0)
-    grad_bias_one = jnp.sum(dnormed, axis=0)
-    vector_grads = jnp.stack([grad_gain_one, grad_bias_one, grad_gain_two, grad_bias_two])
-    from_next = shift_seq(dnormed[pool_rows : pool_rows + BLOCK].astype(bf16), -1).astype(f32)
-    own_qo = jnp.concatenate([grad_own, grad_out[0]], 1)
-    other_qo = jnp.concatenate([grad_other, grad_out[1]], 1)
-    sum_qo = scatter_halves(own_qo, other_qo, 768)
-    dpool = dnormed[:pool_rows].astype(bf16)
-    if paired():
+    if fast:
+        grid_q = split_grid(add(grad_own, grad_got), 512)
+        drop_q = drop_near(*grid_q)
+        near_q = swap_near(drop_q)
+        line_u = keep_far(*kept_u, *follows(far_u, drop_q))
+        line_u, got_u = scatter_line(line_u)
+        dmixed_own = follows(dmixed_own, line_u)
+    dnormed, sums_one = project_back(dmixed_own, dmixed_other, own_qkv, other_qkv, unit)
+    vector_grads = jnp.concatenate([sums_one[:2], sums_two[:2]], 0)
+    from_next = shift_seq(dnormed[count + pool_rows :].astype(bf16), -1)
+    dpool = dnormed[count : count + pool_rows].astype(bf16)
+    if fast:
+        kept_q = keep_near(*grid_q, *follows(near_q, dnormed))
+        drop_q = drop_far(*kept_q)
+        far_q = swap_far(drop_q)
         spread = jnp.transpose(vector_grads.reshape(4, size, -1), (1, 0, 2)).reshape(size, 1, -1)
-        spread = jnp.pad(spread.astype(bf16), ((0, 0), (0, 7), (0, width - spread.shape[2])))
+        span = spread.shape[2]
+        spread = jnp.pad(spread.astype(bf16), ((0, 0), (0, 7), (0, width - span)))
         send = jnp.concatenate([dpool.reshape(size, blocks, width), spread], 1)
-        got = jnp.sum(lax.all_to_all(send, "seq", 0, 0).astype(f32), axis=0)
+        pool_got = lax.all_to_all(send, "seq", 0, 0)
+        sum_down = rows_of_side(sum_line(line_d, follows(got_d, drop_q)))
+        output = layer_output(follows(after, drop_q, send), active, mat_down)
+        line_q = keep_far(*kept_q, *follows(far_q, output))
+        line_q, got_q = scatter_line(line_q)
+        got = jnp.sum(follows(pool_got, line_q).astype(f32), axis=0)
         from_pool = got[:blocks]
         chip = got[blocks, :span].reshape(4, 2, -1)
         vector_sums = pick(chip, side, 1) + swap(pick(chip, 1 - side, 1), "batch", 1)
+        sum_uo = rows_of_side(sum_line(line_u, follows(got_u, line_q)))
     else:
         from_pool = lax.psum_scatter(dpool, "seq", scatter_dimension=0, tiled=True).astype(f32)
         vector_sums = lax.psum_scatter(vector_grads, BOTH, scatter_dimension=1, tiled=True)
-    dtoken = (
-        dnormed[pool_rows + BLOCK :]
-        + jnp.repeat(from_pool * (1.0 / BLOCK), BLOCK, axis=0)
-        + jnp.pad(from_next, ((count - BLOCK, 0), (0, 0)))
-    )
-    input_grad = dafter + standardize_back(unit, unit_scale, dtoken * gain_one)
-
-    split = 3 * width // 2
+        output = layer_output(after, active, mat_down)
+    input_grad = input_back(tokens, dnormed, dafter, from_pool, from_next, vectors)
+    if fast:
+        sum_qkv = rows_of_side(sum_line(line_q, follows(got_q, input_grad)))
+    else:
+
+        def scatter(own, other):
+            full = in_order(side, own, other)
+            sums = lax.psum_scatter(full, BOTH, scatter_dimension=1, tiled=True)
+            return sums.astype(f32)
+
+        sum_uo = scatter(
+            jnp.concatenate([up_own, out_own], 1), jnp.concatenate([up_other, out_other], 1)
+        )
+        sum_qkv = scatter(grad_own, grad_other)
+        sum_down = scatter(down_own, down_other)
+
+    split = hidden // 2
     return (
         output[None],
         input_grad[None],
         vector_sums[0],
         vector_sums[1],
-        whole_of(sum_qo[:, :, :split], 3),
-        whole_of(sum_qo[:, :, split:], 1),
+        whole_of(sum_qkv, 3),
+        whole_of(sum_uo[:, :, split:], 1),
         vector_sums[2],
         vector_sums[3],
-        whole_of(sum_up, 1),
-        own_down,
+        whole_of(sum_uo[:, :, :split], 1),
+        whole_of(sum_down, 1),
     )
 
 

time: 438 us -> 348 us (0.79)
  Pallas kernels: 33.7 us -> 122 us
  matrix products: 90.8 us -> 6.46 us
  waiting for transfers between devices: 89.7 us -> 43.4 us
  other arithmetic: 59.1 us -> 29.7 us
  local copies, waits for them, and re-layouts: 65.4 us -> 56.3 us
  starting transfers between devices: 75 us -> 69.2 us
    pallas_call x0 -> x9, Pallas kernels: none -> 88.3 us  [the longest x1 24.1 us: down_back(): pl.pallas_call(down_kernel, grid_spec=pltpu.PrefetchScalarGridSpec(num_sc...]
    dot_general x10 -> x0, matrix products: 65.8 us -> none  [the longest x5 37.7 us: dot_nt(): lax.dot_general(a, b, (((1,), (1,)), ((), ())), preferred_element_type=jn...]
    ppermute x12 -> x15, waiting for transfers between devices: 45.1 us -> 19.6 us  [the longest x6 17.8 us: send_line(): lax.ppermute(slab, 'seq', ring_route(size, 4, k))]
    ppermute x26 -> x31, waiting for transfers between devices: 44.5 us -> 23.8 us  [swap(): return lax.ppermute(value, axis, flip_route(lax.axis_size(axis), bit))]
    dot_general x5 -> x2, matrix products: 24.9 us -> 6.46 us  [dot_tn(): lax.dot_general(a, b, (((0,), (0,)), ((), ())), preferred_element_type=jn...]
    unnamed x135 -> x119, local copies, waits for them, and re-layouts: 25.3 us -> 43.2 us
    reduce_sum x9 -> x1, other arithmetic: 12.5 us -> 0.08 us  [local(): got = jnp.sum(follows(pool_got, line_q).astype(f32), axis=0)]
    transpose x8 -> x6, local copies, waits for them, and re-layouts: 9.88 us -> 0.72 us  [the longest x1 0.27 us: local(): jnp.transpose(first[:, :third].reshape(size, 3, per, third), (0, 2, 1, 3))]
  transfers between devices with their start and end apart: 44 -> 50, of which waited for: 14 -> 12; matrix products, arithmetic and copies ran while one was open for 47% -> 13% of each run, Pallas kernels for 8% -> 36%
where the time goes in v3:
time: 348 us; the launch traced here: 343 us
  Pallas kernels  122 us (35%)
  starting transfers between devices  69.2 us (20%)
  local copies, waits for them, and re-layouts  56.3 us (16%)
  waiting for transfers between devices  43.4 us (12%)
  other arithmetic  29.7 us (9%)
  between operations  15.6 us (4%)
  matrix products  6.46 us (2%)
    unnamed x119, local copies, waits for them, and re-layouts  43.2 us
    ppermute x31, starting transfers between devices, swap(): return lax.ppermute(value, axis, flip_route(lax.axis_size(axis), bit))  25.9 us
    pallas_call x1, Pallas kernels, down_back(): pl.pallas_call(down_kernel, grid_spec=pltpu.PrefetchScalarGridSpec(num_sc...  24.1 us
    ppermute x31, waiting for transfers between devices, swap(): return lax.ppermute(value, axis, flip_route(lax.axis_size(axis), bit))  23.8 us
    ppermute x9, starting transfers between devices, scatter_line(): lax.ppermute(pick(line, (z + k) % layers, 0), 'seq', ring_route(size, 4, k))  21.6 us
    pallas_call x1, Pallas kernels, up_project(): pl.pallas_call(up_kernel, grid_spec=pltpu.PrefetchScalarGridSpec(num_scal...  19.8 us
    pallas_call x1, Pallas kernels, attend_back(): pl.pallas_call(partial(attend_back_kernel, blocks), grid_spec=pltpu.Prefe...  18.5 us
    ppermute x6, waiting for transfers between devices, send_line(): lax.ppermute(slab, 'seq', ring_route(size, 4, k))  17.8 us
  transfers between devices with their start and end apart: 50, of which 12 were waited for; matrix products, arithmetic and copies ran while one was open for 13% of the time, Pallas kernels for 36%

profile of v3, /device:TPU:0, one launch (start us, length us, event | category | flops | bytes accessed | tf_op | source)
XLA Modules:
  0.0 343.2 jit_solution(15850698679454505862)
XLA Ops:
  21.5 2.9 collective-permute-done.1
  24.3 6.0 %collective-permute-done.2 = bf16[48,1536]{1,0:T(8,128)(2,1)S(1)} collective-permute-done((bf16[48,1536]{1,0:T(8,128)(2,1)S(1)}, bf16[48,1536]{1,0:T(8,128)(2,1)S(1)}, u32[]{:S(2)}, u32[]{:S(2)}) %collective-permute-start.2) | collective-permute-done | bytes 147488 | tf_op jit(solution)/shard_map/ppermute | solution.py:835
  36.1 4.4 %collective-permute-done.4 = bf16[4,48,768]{2,1,0:T(8,128)(2,1)S(1)} collective-permute-done((bf16[4,48,768]{2,1,0:T(8,128)(2,1)S(1)}, bf16[4,48,768]{2,1,0:T(8,128)(2,1)S(1)}, u32[]{:S(2)}, u32[]{:S(2)}) %collective-permute-start.4) | collective-permute-done | bytes 294944 | tf_op jit(solution)/shard_map/ppermute | solution.py:813
  48.1 3.7 %collective-permute-start.10 = (bf16[48,1920]{1,0:T(8,128)(2,1)}, bf16[48,1920]{1,0:T(8,128)(2,1)S(1)}, u32[]{:S(2)}, u32[]{:S(2)}) collective-permute-start(bf16[48,1920]{1,0:T(8,128)(2,1)} %get-tuple-element.82), channel_id=1, source_target_pairs={{0,8},{2,10},{4,12},{6,14},{8,16},{10,18},{12,20},{14,22},{16,24},... | collective-permute-start | bytes 552968 | tf_op jit(solution)/shard_map/ppermute | solution.py:835
  54.3 4.0 %collective-permute-done.10 = bf16[48,1920]{1,0:T(8,128)(2,1)S(1)} collective-permute-done((bf16[48,1920]{1,0:T(8,128)(2,1)}, bf16[48,1920]{1,0:T(8,128)(2,1)S(1)}, u32[]{:S(2)}, u32[]{:S(2)}) %collective-permute-start.10) | collective-permute-done | bytes 184352 | tf_op jit(solution)/shard_map/ppermute | solution.py:835
  58.3 5.0 %collective-permute-done.11 = bf16[48,1920]{1,0:T(8,128)(2,1)S(1)} collective-permute-done((bf16[48,1920]{1,0:T(8,128)(2,1)}, bf16[48,1920]{1,0:T(8,128)(2,1)S(1)}, u32[]{:S(2)}, u32[]{:S(2)}) %collective-permute-start.11) | collective-permute-done | bytes 184352 | tf_op jit(solution)/shard_map/ppermute | solution.py:835
  69.4 9.7 %collective-permute-done.14 = bf16[4,48,896]{2,1,0:T(8,128)(2,1)S(1)} collective-permute-done((bf16[4,48,896]{2,1,0:T(8,128)(2,1)S(1)}, bf16[4,48,896]{2,1,0:T(8,128)(2,1)S(1)}, u32[]{:S(2)}, u32[]{:S(2)}) %collective-permute-start.14) | collective-permute-done | bytes 344096 | tf_op jit(solution)/shard_map/ppermute | solution.py:813
  87.0 11.9 %project.1 = (bf16[1344,768]{1,0:T(8,128)(2,1)S(1)}, bf16[1344,768]{1,0:T(8,128)(2,1)S(1)}, bf16[1344,1152]{1,0:T(8,128)(2,1)S(1)}, bf16[1344,1152]{1,0:T(8,128)(2,1)}) custom-call(bf16[1024,768]{1,0:T(8,128)(2,1)S(1)} %bitcast.266, bf16[256,768]{1,0:T(8,128)(2,1)S(1)} %bitcast.272, bf16[64,768]{1,0:T(8,128)(2,1)S(1)} %collective-permute-done.6.halo_ref, ...), custom_call_target="tpu_custom_call" | custom-call | flops 6000000000 | bytes 12000000 | tf_op jit(solution)/shard_map/project/pallas_call | solution.py:396
  110.4 15.6 %attend.1 = (bf16[1024,768]{1,0:T(8,128)(2,1)S(1)}, f32[16,3,80,256]{3,2,1,0:T(8,128)S(1)}, bf16[2,256,768]{2,1,0:T(8,128)(2,1)S(1)}) custom-call(s32[2]{0:T(128)S(1)} %pad_add_fusion.info_ref, s32[256,1]{1,0:T(8,128)S(1)} %broadcast_in_dim_reshape_squeeze.8.sel_ref, f32[256,1]{1,0:T(8,128)S(1)} %compare_select_fusion.bias_ref, ...), custom_call_target="tpu_custom_call" | custom-call | flops 12000000000 | bytes 12000000 | tf_op jit(solution)/shard_map/attend/pallas_call | solution.py:143
  128.0 5.9 %after_attention.1 = (f32[1024,768]{1,0:T(8,128)S(1)}, bf16[1024,768]{1,0:T(8,128)(2,1)S(1)}) custom-call(s32[2]{0:T(128)S(1)} %pad_add_fusion.info_ref, bf16[1024,768]{1,0:T(8,128)(2,1)S(1)} %get-tuple-element.96.att_ref, bf16[768,1920]{1,0:T(8,128)(2,1)S(1)} %pad_maximum_fusion.own_ref, bf16[768,1920]{1,0:T(8,128)(2,1)} %collective-permute-done.17.other_ref, ...), custom_call_target="tpu_custom_call" | custom-call | flops 2000000000 | bytes 10000000 | tf_op jit(solution)/shard_map/after_attention/pallas_call | solution.py:445
  135.6 19.8 %up_project.1 = (bf16[1024,3072]{1,0:T(8,128)(2,1)}, bf16[1024,3072]{1,0:T(8,128)(2,1)}, bf16[3072,384]{1,0:T(8,128)(2,1)S(1)}, bf16[3072,384]{1,0:T(8,128)(2,1)}) custom-call(s32[2]{0:T(128)S(1)} %pad_add_fusion.info_ref, bf16[1024,768]{1,0:T(8,128)(2,1)S(1)} %get-tuple-element.101.n2_ref, bf16[1024,768]{1,0:T(8,128)(2,1)S(1)} %bitcast.269, ...), custom_call_target="tpu_custom_call" | custom-call | flops 14000000000 | bytes 25000000 | tf_op jit(solution)/shard_map/up_project/pallas_call | solution.py:504
  159.9 24.1 %down_back.1 = (f32[1024,768]{1,0:T(8,128)}, bf16[768,1536]{1,0:T(8,128)(2,1)S(1)}, bf16[768,1536]{1,0:T(8,128)(2,1)}) custom-call(s32[2]{0:T(128)S(1)} %pad_add_fusion.info_ref, bf16[1024,768]{1,0:T(8,128)(2,1)S(1)} %copy-done.25, bf16[1024,768]{1,0:T(8,128)(2,1)S(1)} %bitcast.270, bf16[1024,3072]{1,0:T(8,128)(2,1)} %get-tuple-element.104.slope_ref, ...), custom_call_target="tpu_custom_call" | custom-call | flops 20000000000 | bytes 25000000 | tf_op jit(solution)/shard_map/down_back/pallas_call | solution.py:577
  199.2 8.1 %after_back.1 = (f32[1024,768]{1,0:T(8,128)S(1)}, bf16[1024,768]{1,0:T(8,128)(2,1)S(1)}, bf16[768,384]{1,0:T(8,128)(2,1)S(1)}, bf16[768,384]{1,0:T(8,128)(2,1)S(1)}, f32[8,768]{1,0:T(8,128)S(1)}) custom-call(s32[2]{0:T(128)S(1)} %pad_add_fusion.info_ref, f32[1024,768]{1,0:T(8,128)S(1)} %copy-done.8, f32[1024,768]{1,0:T(8,128)S(1)} %copy-done.10, ...), custom_call_target="tpu_custom_call" | custom-call | flops 4000000000 | bytes 16000000 | tf_op jit(solution)/shard_map/after_back/pallas_call | solution.py:655
  219.9 18.5 %attend_back.1 = (bf16[1344,1152]{1,0:T(8,128)(2,1)S(1)}, bf16[1344,1152]{1,0:T(8,128)(2,1)S(1)}) custom-call(s32[2]{0:T(128)S(1)} %pad_add_fusion.info_ref, s32[1,256]{1,0:T(1,128)S(1)} %broadcast_in_dim_reshape_squeeze.7.sel_ref, bf16[1344,1152]{1,0:T(8,128)(2,1)S(1)} %copy-done.33, bf16[1344,1152]{1,0:T(8,128)(2,1)S(1)} %copy-done.33, ...), custom_call_target="tpu_custom_call" | custom-call | flops 20000000000 | bytes 18000000 | tf_op jit(solution)/shard_map/attend_back/pallas_call | solution.py:275
  241.2 3.2 convolution_convert_fusion.1
  244.5 5.5 %collective-permute-start.44 = (bf16[192,384]{1,0:T(8,128)(2,1)}, bf16[192,384]{1,0:T(8,128)(2,1)}, u32[]{:S(2)}, u32[]{:S(2)}) collective-permute-start(bf16[192,384]{1,0:T(8,128)(2,1)} %get-tuple-element.184), channel_id=1, source_target_pairs={{0,8},{2,10},{4,12},{6,14},{8,16},{10,18},{12,20},{14,22},{16,24},... | collective-permute-start | bytes 442376 | tf_op jit(solution)/shard_map/ppermute | solution.py:907
  250.0 4.3 %collective-permute-start.45 = (bf16[192,384]{1,0:T(8,128)(2,1)}, bf16[192,384]{1,0:T(8,128)(2,1)}, u32[]{:S(2)}, u32[]{:S(2)}) collective-permute-start(bf16[192,384]{1,0:T(8,128)(2,1)} %get-tuple-element.185), channel_id=1, source_target_pairs={{0,16},{2,18},{4,20},{6,22},{8,24},{10,26},{12,28},{14,30},{16,0},... | collective-permute-start | bytes 442376 | tf_op jit(solution)/shard_map/ppermute | solution.py:907
  256.2 3.2 convolution_convert_fusion
  265.5 6.1 %collective-permute-done.30 = bf16[4,48,1024]{2,1,0:T(8,128)(2,1)S(1)} collective-permute-done((bf16[4,48,1024]{2,1,0:T(8,128)(2,1)S(1)}, bf16[4,48,1024]{2,1,0:T(8,128)(2,1)S(1)}, u32[]{:S(2)}, u32[]{:S(2)}) %collective-permute-start.30) | collective-permute-done | bytes 393248 | tf_op jit(solution)/shard_map/ppermute | solution.py:813
  273.2 7.5 %project_back.1 = (f32[1344,768]{1,0:T(8,128)S(1)}, f32[8,768]{1,0:T(8,128)S(1)}) custom-call(bf16[1344,1152]{1,0:T(8,128)(2,1)S(1)} %get-tuple-element.130.dm_own, bf16[1344,1152]{1,0:T(8,128)(2,1)S(1)} %get-tuple-element.126.dm_other, bf16[768,1152]{1,0:T(8,128)(2,1)S(1)} %copy-done.18, bf16[768,1152]{1,0:T(8,128)(2,1)} %collective-permute-done.9.other_ref, ...), custom_call_target="tpu_custom_call" | custom-call | flops 6000000000 | bytes 16000000 | tf_op jit(solution)/shard_map/project_back/pallas_call | solution.py:711
  284.5 5.0 %all-to-all-start = ((bf16[16,24,768]{2,1,0:T(8,128)(2,1)}), bf16[16,24,768]{2,1,0:T(8,128)(2,1)S(1)}, u32[]{:S(2)}, u32[]{:S(2)}) async-start(bf16[16,24,768]{2,1,0:T(8,128)(2,1)} %fusion.9), calls=%async_computation | async-start | bytes 1179648 | tf_op jit(solution)/shard_map/all_to_all | solution.py:1086
  304.7 6.5 %layer_output.1 = bf16[1024,768]{1,0:T(8,128)(2,1)} custom-call(f32[1024,768]{1,0:T(8,128)S(1)} %copy-done.9, bf16[1024,3072]{1,0:T(8,128)(2,1)S(1)} %copy-done.28, bf16[3072,768]{1,0:T(8,128)(2,1)S(1)} %copy-done.23), custom_call_target="tpu_custom_call" | custom-call | flops 6000000000 | bytes 16000000 | tf_op jit(solution)/shard_map/layer_output/pallas_call | solution.py:775
  317.2 3.7 %collective-permute-start.36 = (bf16[48,1152]{1,0:T(8,128)(2,1)S(1)}, bf16[48,1152]{1,0:T(8,128)(2,1)S(1)}, u32[]{:S(2)}, u32[]{:S(2)}) collective-permute-start(bf16[48,1152]{1,0:T(8,128)(2,1)S(1)} %get-tuple-element.202), channel_id=1, source_target_pairs={{0,8},{2,10},{4,12},{6,14},{8,16},{10,18},{12,20},{14,22},{16,24},... | collective-permute-start | bytes 331784 | tf_op jit(solution)/shard_map/ppermute | solution.py:907
  329.6 3.4 input_back.1
  (344 shorter events, 139.8 us)
Async XLA Ops:
  7.2 149.9 %all-gather.2.cloned.1.call-start = ((), (), s32[]{:S(2)}) async-start(), calls=%async_computation.1 | async-start | bytes 4866048 | tf_op jit(solution)/shard_map/all_gather | solution.py:1003
  43.9 20.4 %collective-permute-start.5 = (bf16[2,4,48,768]{3,2,1,0:T(8,128)(2,1)}, bf16[2,4,48,768]{3,2,1,0:T(8,128)(2,1)}, u32[]{:S(2)}, u32[]{:S(2)}) collective-permute-start(bf16[2,4,48,768]{3,2,1,0:T(8,128)(2,1)} %pad_maximum_fusion.9), channel_id=1, source_target_pairs={{0,4},{2,6},{4,0},{6,2},{8,12},{10,14},{12,8},{14,10},{16,20},{18,... | collective-permute-start | bytes 1769480 | tf_op jit(solution)/shard_map/ppermute | solution.py:813
  47.4 17.0 %collective-permute-start.8 = (bf16[2,4,48,768]{3,2,1,0:T(8,128)(2,1)}, bf16[2,4,48,768]{3,2,1,0:T(8,128)(2,1)}, u32[]{:S(2)}, u32[]{:S(2)}) collective-permute-start(bf16[2,4,48,768]{3,2,1,0:T(8,128)(2,1)} %pad_maximum_fusion.10), channel_id=1, source_target_pairs={{0,2},{2,0},{4,6},{6,4},{8,10},{10,8},{12,14},{14,12},{16,18},{18,... | collective-permute-start | bytes 1769480 | tf_op jit(solution)/shard_map/ppermute | solution.py:813
  66.4 19.5 %collective-permute-start.9 = (bf16[768,1152]{1,0:T(8,128)(2,1)S(1)}, bf16[768,1152]{1,0:T(8,128)(2,1)}, u32[]{:S(2)}, u32[]{:S(2)}) collective-permute-start(bf16[768,1152]{1,0:T(8,128)(2,1)S(1)} %pad_maximum_fusion.2.own_ref), channel_id=1, source_target_pairs={{0,1},{1,0},{2,3},{3,2},{4,5},{5,4},{6,7},{7,6},{8,9},{9,8},{10,11... | collective-permute-start | bytes 5308424 | tf_op jit(solution)/shard_map/ppermute | solution.py:813
  80.2 20.8 %collective-permute-start.15 = (bf16[2,4,48,1024]{3,2,1,0:T(8,128)(2,1)}, bf16[2,4,48,1024]{3,2,1,0:T(8,128)(2,1)}, u32[]{:S(2)}, u32[]{:S(2)}) collective-permute-start(bf16[2,4,48,1024]{3,2,1,0:T(8,128)(2,1)} %pad_maximum_fusion.3), channel_id=1, source_target_pairs={{0,4},{2,6},{4,0},{6,2},{8,12},{10,14},{12,8},{14,10},{16,20},{18,... | collective-permute-start | bytes 2359304 | tf_op jit(solution)/shard_map/ppermute | solution.py:813
  81.9 19.2 %collective-permute-start.16 = (bf16[2,4,48,896]{3,2,1,0:T(8,128)(2,1)}, bf16[2,4,48,896]{3,2,1,0:T(8,128)(2,1)}, u32[]{:S(2)}, u32[]{:S(2)}) collective-permute-start(bf16[2,4,48,896]{3,2,1,0:T(8,128)(2,1)} %pad_maximum_fusion.6), channel_id=1, source_target_pairs={{0,2},{2,0},{4,6},{6,4},{8,10},{10,8},{12,14},{14,12},{16,18},{18,... | collective-permute-start | bytes 2064392 | tf_op jit(solution)/shard_map/ppermute | solution.py:813
  105.9 22.0 %collective-permute-start.17 = (bf16[768,1920]{1,0:T(8,128)(2,1)S(1)}, bf16[768,1920]{1,0:T(8,128)(2,1)}, u32[]{:S(2)}, u32[]{:S(2)}) collective-permute-start(bf16[768,1920]{1,0:T(8,128)(2,1)S(1)} %pad_maximum_fusion.own_ref), channel_id=1, source_target_pairs={{0,1},{1,0},{2,3},{3,2},{4,5},{5,4},{6,7},{7,6},{8,9},{9,8},{10,11... | collective-permute-start | bytes 8847368 | tf_op jit(solution)/shard_map/ppermute | solution.py:813
  156.8 27.2 %collective-permute-start.18 = (bf16[3072,384]{1,0:T(8,128)(2,1)}, bf16[3072,384]{1,0:T(8,128)(2,1)}, u32[]{:S(2)}, u32[]{:S(2)}) collective-permute-start(bf16[3072,384]{1,0:T(8,128)(2,1)} %get-tuple-element.103), channel_id=1, source_target_pairs={{0,1},{1,0},{2,3},{3,2},{4,5},{5,4},{6,7},{7,6},{8,9},{9,8},{10,11... | collective-permute-start | bytes 7077896 | tf_op jit(solution)/shard_map/ppermute | solution.py:813
  184.0 29.4 %collective-permute-start.19 = (bf16[768,1536]{1,0:T(8,128)(2,1)}, bf16[768,1536]{1,0:T(8,128)(2,1)}, u32[]{:S(2)}, u32[]{:S(2)}) collective-permute-start(bf16[768,1536]{1,0:T(8,128)(2,1)} %get-tuple-element.111), channel_id=1, source_target_pairs={{0,1},{1,0},{2,3},{3,2},{4,5},{5,4},{6,7},{7,6},{8,9},{9,8},{10,11... | collective-permute-start | bytes 7077896 | tf_op jit(solution)/shard_map/ppermute | solution.py:813
  190.5 17.0 %collective-permute-start.22 = (bf16[4,2,96,384]{3,2,1,0:T(8,128)(2,1)}, bf16[4,2,96,384]{3,2,1,0:T(8,128)(2,1)}, u32[]{:S(2)}, u32[]{:S(2)}) collective-permute-start(bf16[4,2,96,384]{3,2,1,0:T(8,128)(2,1)} %dynamic-slice_bitcast_fusion.2), channel_id=1, source_target_pairs={{0,4},{2,6},{4,0},{6,2},{8,12},{10,14},{12,8},{14,10},{16,20},{18,... | collective-permute-start | bytes 1769480 | tf_op jit(solution)/shard_map/ppermute | solution.py:813
  209.6 28.8 %collective-permute-start.26 = (bf16[4,96,384]{2,1,0:T(8,128)(2,1)S(1)}, bf16[4,96,384]{2,1,0:T(8,128)(2,1)S(1)}, u32[]{:S(2)}, u32[]{:S(2)}) collective-permute-start(bf16[4,96,384]{2,1,0:T(8,128)(2,1)S(1)} %dynamic-slice_bitcast_fusion.6), channel_id=1, source_target_pairs={{0,2},{2,0},{4,6},{6,4},{8,10},{10,8},{12,14},{14,12},{16,18},{18,... | collective-permute-start | bytes 884744 | tf_op jit(solution)/shard_map/ppermute | solution.py:813
  212.6 25.8 %collective-permute-start.25 = (bf16[4,96,384]{2,1,0:T(8,128)(2,1)S(1)}, bf16[4,96,384]{2,1,0:T(8,128)(2,1)S(1)}, u32[]{:S(2)}, u32[]{:S(2)}) collective-permute-start(bf16[4,96,384]{2,1,0:T(8,128)(2,1)S(1)} %dynamic-slice_bitcast_fusion.7), channel_id=1, source_target_pairs={{0,4},{2,6},{4,0},{6,2},{8,12},{10,14},{12,8},{14,10},{16,20},{18,... | collective-permute-start | bytes 884744 | tf_op jit(solution)/shard_map/ppermute | solution.py:813
  216.4 23.0 %collective-permute-start.24 = (bf16[4,2,48,896]{3,2,1,0:T(8,128)(2,1)S(1)}, bf16[4,2,48,896]{3,2,1,0:T(8,128)(2,1)S(1)}, u32[]{:S(2)}, u32[]{:S(2)}) collective-permute-start(bf16[4,2,48,896]{3,2,1,0:T(8,128)(2,1)S(1)} %dynamic-slice_bitcast_fusion.1), channel_id=1, source_target_pairs={{0,4},{2,6},{4,0},{6,2},{8,12},{10,14},{12,8},{14,10},{16,20},{18,... | collective-permute-start | bytes 2064392 | tf_op jit(solution)/shard_map/ppermute | solution.py:813
  218.0 21.5 %collective-permute-start.23 = (bf16[4,2,48,1024]{3,2,1,0:T(8,128)(2,1)S(1)}, bf16[4,2,48,1024]{3,2,1,0:T(8,128)(2,1)S(1)}, u32[]{:S(2)}, u32[]{:S(2)}) collective-permute-start(bf16[4,2,48,1024]{3,2,1,0:T(8,128)(2,1)S(1)} %dynamic-slice_bitcast_fusion), channel_id=1, source_target_pairs={{0,2},{2,0},{4,6},{6,4},{8,10},{10,8},{12,14},{14,12},{16,18},{18,... | collective-permute-start | bytes 2359304 | tf_op jit(solution)/shard_map/ppermute | solution.py:813
  244.5 50.6 %collective-permute-start.44 = (bf16[192,384]{1,0:T(8,128)(2,1)}, bf16[192,384]{1,0:T(8,128)(2,1)}, u32[]{:S(2)}, u32[]{:S(2)}) collective-permute-start(bf16[192,384]{1,0:T(8,128)(2,1)} %get-tuple-element.184), channel_id=1, source_target_pairs={{0,8},{2,10},{4,12},{6,14},{8,16},{10,18},{12,20},{14,22},{16,24},... | collective-permute-start | bytes 442376 | tf_op jit(solution)/shard_map/ppermute | solution.py:907
  250.0 46.6 %collective-permute-start.45 = (bf16[192,384]{1,0:T(8,128)(2,1)}, bf16[192,384]{1,0:T(8,128)(2,1)}, u32[]{:S(2)}, u32[]{:S(2)}) collective-permute-start(bf16[192,384]{1,0:T(8,128)(2,1)} %get-tuple-element.185), channel_id=1, source_target_pairs={{0,16},{2,18},{4,20},{6,22},{8,24},{10,26},{12,28},{14,30},{16,0},... | collective-permute-start | bytes 442376 | tf_op jit(solution)/shard_map/ppermute | solution.py:907
  254.2 43.9 %collective-permute-start.46 = (bf16[192,384]{1,0:T(8,128)(2,1)}, bf16[192,384]{1,0:T(8,128)(2,1)}, u32[]{:S(2)}, u32[]{:S(2)}) collective-permute-start(bf16[192,384]{1,0:T(8,128)(2,1)} %get-tuple-element.182), channel_id=1, source_target_pairs={{0,24},{2,26},{4,28},{6,30},{8,0},{10,2},{12,4},{14,6},{16,8},{18,... | collective-permute-start | bytes 442376 | tf_op jit(solution)/shard_map/ppermute | solution.py:907
  264.3 27.1 %collective-permute-start.29 = (bf16[4,2,48,640]{3,2,1,0:T(8,128)(2,1)S(1)}, bf16[4,2,48,640]{3,2,1,0:T(8,128)(2,1)S(1)}, u32[]{:S(2)}, u32[]{:S(2)}) collective-permute-start(bf16[4,2,48,640]{3,2,1,0:T(8,128)(2,1)S(1)} %dynamic-slice_bitcast_fusion.3), channel_id=1, source_target_pairs={{0,4},{2,6},{4,0},{6,2},{8,12},{10,14},{12,8},{14,10},{16,20},{18,... | collective-permute-start | bytes 1474568 | tf_op jit(solution)/shard_map/ppermute | solution.py:813
  271.6 17.8 %collective-permute-start.28 = (bf16[4,2,48,512]{3,2,0,1:T(8,128)(2,1)}, bf16[4,2,48,512]{3,2,0,1:T(8,128)(2,1)}, u32[]{:S(2)}, u32[]{:S(2)}) collective-permute-start(bf16[4,2,48,512]{3,2,0,1:T(8,128)(2,1)} %bitcast.261), channel_id=1, source_target_pairs={{0,2},{2,0},{4,6},{6,4},{8,10},{10,8},{12,14},{14,12},{16,18},{18,... | collective-permute-start | bytes 1179656 | tf_op jit(solution)/shard_map/ppermute | solution.py:813
  284.5 40.9 %all-to-all-start = ((bf16[16,24,768]{2,1,0:T(8,128)(2,1)}), bf16[16,24,768]{2,1,0:T(8,128)(2,1)S(1)}, u32[]{:S(2)}, u32[]{:S(2)}) async-start(bf16[16,24,768]{2,1,0:T(8,128)(2,1)} %fusion.9), calls=%async_computation | async-start | bytes 1179648 | tf_op jit(solution)/shard_map/all_to_all | solution.py:1086
  289.4 24.5 %collective-permute-start.40 = (bf16[48,1920]{1,0:T(8,128)(2,1)}, bf16[48,1920]{1,0:T(8,128)(2,1)S(1)}, u32[]{:S(2)}, u32[]{:S(2)}) collective-permute-start(bf16[48,1920]{1,0:T(8,128)(2,1)} %get-tuple-element.174), channel_id=1, source_target_pairs={{0,8},{2,10},{4,12},{6,14},{8,16},{10,18},{12,20},{14,22},{16,24},... | collective-permute-start | bytes 552968 | tf_op jit(solution)/shard_map/ppermute | solution.py:907
  291.4 24.2 %collective-permute-start.41 = (bf16[48,1920]{1,0:T(8,128)(2,1)}, bf16[48,1920]{1,0:T(8,128)(2,1)S(1)}, u32[]{:S(2)}, u32[]{:S(2)}) collective-permute-start(bf16[48,1920]{1,0:T(8,128)(2,1)} %get-tuple-element.175), channel_id=1, source_target_pairs={{0,16},{2,18},{4,20},{6,22},{8,24},{10,26},{12,28},{14,30},{16,0},... | collective-permute-start | bytes 552968 | tf_op jit(solution)/shard_map/ppermute | solution.py:907
  295.1 20.6 %collective-permute-start.42 = (bf16[48,1920]{1,0:T(8,128)(2,1)S(1)}, bf16[48,1920]{1,0:T(8,128)(2,1)S(1)}, u32[]{:S(2)}, u32[]{:S(2)}) collective-permute-start(bf16[48,1920]{1,0:T(8,128)(2,1)S(1)} %get-tuple-element.172), channel_id=1, source_target_pairs={{0,24},{2,26},{4,28},{6,30},{8,0},{10,2},{12,4},{14,6},{16,8},{18,... | collective-permute-start | bytes 552968 | tf_op jit(solution)/shard_map/ppermute | solution.py:907
  296.6 17.0 %collective-permute-start.33 = (bf16[4,48,640]{2,1,0:T(8,128)(2,1)S(1)}, bf16[4,48,640]{2,1,0:T(8,128)(2,1)S(1)}, u32[]{:S(2)}, u32[]{:S(2)}) collective-permute-start(bf16[4,48,640]{2,1,0:T(8,128)(2,1)S(1)} %dynamic-slice_bitcast_fusion.8), channel_id=1, source_target_pairs={{0,2},{2,0},{4,6},{6,4},{8,10},{10,8},{12,14},{14,12},{16,18},{18,... | collective-permute-start | bytes 737288 | tf_op jit(solution)/shard_map/ppermute | solution.py:813
  (81 other events, 513.9 us)
Sparse Core Ops, SparseCore 0:
  54.5 64.6 all-gather.1

commit v4 on v3

v4 whole, which is shorter than its diff:
```python
from functools import partial

import jax
import jax.numpy as jnp
from jax import lax
from jax.experimental import pallas as pl
from jax.experimental.pallas import tpu as pltpu
from jax.sharding import PartitionSpec as P

HEADS = 12
HEAD = 64
BLOCK = 64
TOPK = 16
QUAD = 4 * HEAD
FOLD = BLOCK + TOPK
NEG = -1e30


def dot_nn(a, b):
    return lax.dot_general(a, b, (((1,), (0,)), ((), ())), preferred_element_type=jnp.float32)


def dot_nt(a, b):
    return lax.dot_general(a, b, (((1,), (1,)), ((), ())), preferred_element_type=jnp.float32)


def dot_tn(a, b):
    return lax.dot_general(a, b, (((0,), (0,)), ((), ())), preferred_element_type=jnp.float32)


def spread_heads(rows):
    lane = lax.broadcasted_iota(jnp.int32, rows.shape, 1) // HEAD
    zero = jnp.zeros_like(rows)
    return jnp.concatenate([jnp.where(lane == h, rows, zero) for h in range(4)], 0)


def gather_heads(full):
    lane = lax.broadcasted_iota(jnp.int32, (BLOCK, QUAD), 1) // HEAD
    out = full[:BLOCK]
    for h in range(1, 4):
        out = jnp.where(lane == h, full[h * BLOCK : (h + 1) * BLOCK], out)
    return out


def prev_side():
    k = lax.broadcasted_iota(jnp.int32, (BLOCK, QUAD), 0)
    q = lax.broadcasted_iota(jnp.int32, (BLOCK, QUAD), 1) % BLOCK
    return k > q


def unfold(near, far, prev):
    zero = jnp.zeros_like(near)
    both = [jnp.where(prev, near, zero), jnp.where(prev, zero, near), far]
    return jnp.concatenate(both, 0).astype(jnp.bfloat16)


HALF = HEADS // 2 * HEAD
PAIR = 2 * BLOCK


def load_quad(own_ref, other_ref, rows, part, g):
    at = part * HALF
    if g == 0:
        return own_ref[rows, at : at + QUAD]
    if g == 1:
        return jnp.concatenate(
            [own_ref[rows, at + QUAD : at + HALF], other_ref[rows, at : at + HALF - QUAD]], 1
        )
    return other_ref[rows, at + HALF - QUAD : at + HALF]


def join_quads(quads):
    own = jnp.concatenate([quads[0], quads[1][:, : HALF - QUAD]], 1)
    other = jnp.concatenate([quads[1][:, HALF - QUAD :], quads[2]], 1)
    return own, other


CHAINS = [(b, g) for b in range(2) for g in range(HEADS // 4)]


def load_keys(prev, cur, picks, part, b, g):
    every = slice(None)
    before = load_quad(*prev, every, part, g) if b == 0 else load_quad(*cur, slice(0, BLOCK), part, g)
    here = load_quad(*cur, slice(b * BLOCK, (b + 1) * BLOCK), part, g)
    picked = load_quad(*picks, slice(b * TOPK, (b + 1) * TOPK), part - 1, g)
    return jnp.concatenate([before, here, picked], 0)


def attend_kernel(
    info_ref,
    sel_ref,
    bias_ref,
    pool_own,
    prev_own,
    cur_own,
    pool_other,
    prev_other,
    cur_other,
    att_ref,
    probs_ref,
    picks_ref,
):
    c = pl.program_id(0)
    core = info_ref[1]

    @pl.when(c == 0)
    def _():
        pool_rows = pool_own.shape[0]
        ids = lax.broadcasted_iota(jnp.int32, (sel_ref.shape[0], pool_rows), 1)
        one_hot = (ids == sel_ref[...]).astype(jnp.float32).astype(jnp.bfloat16)
        picks_ref[0] = dot_nn(one_hot, pool_own[:, HALF:]).astype(jnp.bfloat16)
        picks_ref[1] = dot_nn(one_hot, pool_other[:, HALF:]).astype(jnp.bfloat16)

    side = prev_side()
    edge = jnp.where((c == 0) & (info_ref[0] == 1), NEG, 0.0)
    rows = pl.ds(pl.multiple_of(c * 2 * TOPK, 2 * TOPK), 2 * TOPK)
    prev, cur = (prev_own, prev_other), (cur_own, cur_other)
    picks = (picks_ref.at[0, rows], picks_ref.at[1, rows])
    scored, values, fulls, outs = [], [], [], []
    for b, g in CHAINS:
        keys = load_keys(prev, cur, picks, 1, b, g)
        values.append(load_keys(prev, cur, picks, 2, b, g))
        wide_q = spread_heads(load_quad(*cur, slice(b * BLOCK, (b + 1) * BLOCK), 0, g))
        scored.append(dot_nt(keys, wide_q))
    for n, (b, g) in enumerate(CHAINS):
        scores = scored[n] * HEAD ** (-0.5)
        before = scores[:BLOCK] + edge if b == 0 else scores[:BLOCK]
        near = jnp.where(side, before, scores[BLOCK : 2 * BLOCK])
        far = scores[2 * BLOCK :] + bias_ref[b * TOPK : (b + 1) * TOPK]
        folded = jnp.concatenate([near, far], 0)
        top = jnp.max(folded, axis=0, keepdims=True)
        weights = jnp.exp(folded - top)
        probs = weights * (1.0 / jnp.sum(weights, axis=0, keepdims=True))
        probs_ref[b, g] = probs
        fulls.append(unfold(probs[:BLOCK], probs[BLOCK:], side))
    for n, (b, g) in enumerate(CHAINS):
        outs.append(gather_heads(dot_tn(fulls[n], values[n])).astype(jnp.bfloat16))
    for b in range(2):
        own, other = join_quads(outs[b * (HEADS // 4) : (b + 1) * (HEADS // 4)])
        here = slice(b * BLOCK, (b + 1) * BLOCK)
        att_ref[here, pl.ds(pl.multiple_of(core * HALF, 128), HALF)] = own
        att_ref[here, pl.ds(pl.multiple_of((1 - core) * HALF, 128), HALF)] = other


def attend(mixed_own, mixed_other, sel_col, bias_col, info, blocks, pool_rows):
    width = HEADS * HEAD
    halo = mixed_own.shape[0] // BLOCK - 1
    mixed_specs = [
        pl.BlockSpec((pool_rows, 3 * HALF), lambda c, f: (blocks * BLOCK // pool_rows, 0)),
        pl.BlockSpec((BLOCK, 3 * HALF), lambda c, f: (jnp.where(c == 0, halo, 2 * c - 1), 0)),
        pl.BlockSpec((PAIR, 3 * HALF), lambda c, f: (c, 0)),
    ]
    return pl.pallas_call(
        attend_kernel,
        grid_spec=pltpu.PrefetchScalarGridSpec(
            num_scalar_prefetch=1,
            grid=(blocks // 2,),
            in_specs=[
                pl.BlockSpec((blocks * TOPK, 1), lambda c, f: (0, 0)),
                pl.BlockSpec((2 * TOPK, 1), lambda c, f: (c, 0)),
            ]
            + mixed_specs * 2,
            out_specs=[
                pl.BlockSpec((PAIR, width), lambda c, f: (c, 0)),
                pl.BlockSpec((2, HEADS // 4, FOLD, QUAD), lambda c, f: (c, 0, 0, 0)),
                pl.BlockSpec((2, blocks * TOPK, 2 * HALF), lambda c, f: (0, 0, 0)),
            ],
        ),
        out_shape=[
            jax.ShapeDtypeStruct((blocks * BLOCK, width), jnp.bfloat16),
            jax.ShapeDtypeStruct((blocks, HEADS // 4, FOLD, QUAD), jnp.float32),
            jax.ShapeDtypeStruct((2, blocks * TOPK, 2 * HALF), jnp.bfloat16),
        ],
        compiler_params=pltpu.CompilerParams(vmem_limit_bytes=32 * 1024 * 1024),
        cost_estimate=pl.CostEstimate(
            flops=12_000_000_000, bytes_accessed=12_000_000, transcendentals=1_000_000
        ),
        name="attend",
    )(info, sel_col, bias_col, *[mixed_own] * 3, *[mixed_other] * 3)


def attend_back_kernel(
    pairs,
    info_ref,
    sel_ref,
    prev_own,
    cur_own,
    prev_other,
    cur_other,
    picks_ref,
    probs_ref,
    datt_ref,
    out_own,
    out_other,
    carry,
    dpicks,
):
    i = pl.program_id(0)
    core = info_ref[1]
    outs = (out_own, out_other)

    @pl.when(i == 0)
    def _():
        carry[...] = jnp.zeros_like(carry)

    @pl.when(i < pairs)
    def _():
        side = prev_side()
        datt = (
            datt_ref.at[:, pl.ds(pl.multiple_of(core * HALF, 128), HALF)],
            datt_ref.at[:, pl.ds(pl.multiple_of((1 - core) * HALF, 128), HALF)],
        )
        prev, cur = (prev_own, prev_other), (cur_own, cur_other)
        picks = (picks_ref.at[0], picks_ref.at[1])
        wide_qs, wide_ds, firsts, full_ps, full_ds = [], [], [], [], []
        for b, g in CHAINS:
            here = slice(b * BLOCK, (b + 1) * BLOCK)
            wide_qs.append(spread_heads(load_quad(*cur, here, 0, g)))
            wide_ds.append(spread_heads(load_quad(*datt, here, 0, g)))
            firsts.append(dot_nt(load_keys(prev, cur, picks, 2, b, g), wide_ds[-1]))
        for n, (b, g) in enumerate(CHAINS):
            probs, dprobs = probs_ref[b, g], firsts[n]
            near = jnp.where(side, dprobs[:BLOCK], dprobs[BLOCK : 2 * BLOCK])
            folded = jnp.concatenate([near, dprobs[2 * BLOCK :]], 0)
            inner = jnp.sum(probs * folded, axis=0, keepdims=True)
            dscores = probs * (folded - inner) * HEAD ** (-0.5)
            full_ps.append(unfold(probs[:BLOCK], probs[BLOCK:], side))
            full_ds.append(unfold(dscores[:BLOCK], dscores[BLOCK:], side))
        grads = []
        for n, (b, g) in enumerate(CHAINS):
            dvals = dot_nn(full_ps[n], wide_ds[n])
            dkeys = dot_nn(full_ds[n], wide_qs[n])
            dq = gather_heads(dot_tn(full_ds[n], load_keys(prev, cur, picks, 1, b, g)))
            grads.append((dq, dkeys, dvals))
        for part in range(3):
            lanes = slice(part * HALF, (part + 1) * HALF)
            a = join_quads([grad[part] for grad in grads[: HEADS // 4]])
            b = join_quads([grad[part] for grad in grads[HEADS // 4 :]])
            for s, out_ref in enumerate(outs):
                if part == 0:
                    out_ref[:, lanes] = carry[s, :, lanes].astype(jnp.bfloat16)
                    carry[s, :BLOCK, lanes] = a[s]
                    carry[s, BLOCK:, lanes] = b[s]
                else:
                    out_ref[:BLOCK, lanes] = carry[s, :BLOCK, lanes].astype(jnp.bfloat16)
                    low = carry[s, BLOCK:, lanes] + a[s][:BLOCK]
                    out_ref[BLOCK:, lanes] = low.astype(jnp.bfloat16)
                    carry[s, :BLOCK, lanes] = a[s][BLOCK : 2 * BLOCK] + b[s][:BLOCK]
                    carry[s, BLOCK:, lanes] = b[s][BLOCK : 2 * BLOCK]
                    both = jnp.concatenate([a[s][2 * BLOCK :], b[s][2 * BLOCK :]], 0)
                    rows = pl.ds(pl.multiple_of(i * 2 * TOPK, 2 * TOPK), 2 * TOPK)
                    picked = slice((part - 1) * HALF, part * HALF)
                    dpicks[s, rows, picked] = both.astype(jnp.bfloat16)

    @pl.when(i == pairs)
    def _():
        out_own[...] = carry[0].astype(jnp.bfloat16)
        out_other[...] = carry[1].astype(jnp.bfloat16)

    @pl.when(i > pairs)
    def _():
        ids = lax.broadcasted_iota(jnp.int32, (PAIR, 2 * pairs * TOPK), 0) + (i - pairs - 1) * PAIR
        one_hot = (ids == sel_ref[...]).astype(jnp.float32).astype(jnp.bfloat16)
        for s, out_ref in enumerate(outs):
            out_ref[:, :HALF] = jnp.zeros((PAIR, HALF), jnp.bfloat16)
            out_ref[:, HALF:] = dot_nn(one_hot, dpicks[s]).astype(jnp.bfloat16)


def attend_back(mixed_own, mixed_other, sel_row, info, picks, probs, datt, blocks, pool_rows):
    width = HEADS * HEAD
    pairs = blocks // 2
    total = mixed_own.shape[0]
    halo = total // BLOCK - 1

    def pair(i):
        return jnp.minimum(i, pairs - 1)

    def before_block(i, f):
        return (jnp.where(i == 0, halo, 2 * pair(i) - 1), 0)

    def out_block(i, f):
        return (jnp.where(i == 0, total // PAIR - 1, i - 1), 0)

    mixed_specs = [
        pl.BlockSpec((BLOCK, 3 * HALF), before_block),
        pl.BlockSpec((PAIR, 3 * HALF), lambda i, f: (pair(i), 0)),
    ]
    return pl.pallas_call(
        partial(attend_back_kernel, pairs),
        grid_spec=pltpu.PrefetchScalarGridSpec(
            num_scalar_prefetch=1,
            grid=(pairs + 1 + pool_rows // PAIR,),
            in_specs=[pl.BlockSpec((1, blocks * TOPK), lambda i, f: (0, 0))]
            + mixed_specs * 2
            + [
                pl.BlockSpec((2, 2 * TOPK, 2 * HALF), lambda i, f: (0, pair(i), 0)),
                pl.BlockSpec((2, HEADS // 4, FOLD, QUAD), lambda i, f: (pair(i), 0, 0, 0)),
                pl.BlockSpec((PAIR, width), lambda i, f: (pair(i), 0)),
            ],
            out_specs=[pl.BlockSpec((PAIR, 3 * HALF), out_block)] * 2,
            scratch_shapes=[
                pltpu.VMEM((2, PAIR, 3 * HALF), jnp.float32),
                pltpu.VMEM((2, blocks * TOPK, 2 * HALF), jnp.bfloat16),
            ],
        ),
        out_shape=[jax.ShapeDtypeStruct((total, 3 * HALF), jnp.bfloat16)] * 2,
        compiler_params=pltpu.CompilerParams(vmem_limit_bytes=32 * 1024 * 1024),
        cost_estimate=pl.CostEstimate(
            flops=20_000_000_000, bytes_accessed=18_000_000, transcendentals=0
        ),
        name="attend_back",
    )(info, sel_row, *[mixed_own] * 2, *[mixed_other] * 2, picks, probs, datt)


def standardize(values):
    center = values - jnp.mean(values, axis=-1, keepdims=True)
    spread = jnp.mean(center * center, axis=-1, keepdims=True)
    scale = lax.rsqrt(spread + 1e-05)
    return center * scale, scale


def standardize_back(unit, scale, dunit):
    return scale * (
        dunit
        - jnp.mean(dunit, axis=-1, keepdims=True)
        - unit * jnp.mean(dunit * unit, axis=-1, keepdims=True)
    )


ROWS = 256
CHUNK = 768
GROUP = 48
MIB = 1024 * 1024


def params(mib):
    return pltpu.CompilerParams(vmem_limit_bytes=mib * MIB)


def shape(rows, columns, dtype=jnp.bfloat16):
    return jax.ShapeDtypeStruct((rows, columns), dtype)


def cost(flops, moved):
    return pl.CostEstimate(flops=flops, bytes_accessed=moved, transcendentals=0)


def lanes_at(index, size):
    return pl.ds(pl.multiple_of(index * size, 128), size)


def pool_kernel(tokens_ref, unit_ref, out_ref):
    for b in range(out_ref.shape[0]):
        rows = slice(b * BLOCK, (b + 1) * BLOCK)
        unit, _ = standardize(tokens_ref[rows].astype(jnp.float32))
        unit_ref[rows] = unit
        out_ref[b : b + 1] = jnp.mean(unit, axis=0, keepdims=True)


def pool(tokens):
    rows, width = tokens.shape
    return pl.pallas_call(
        pool_kernel,
        out_shape=[shape(rows, width, jnp.float32), shape(rows // BLOCK, width, jnp.float32)],
        compiler_params=params(24),
        cost_estimate=cost(2_000_000_000, 6_000_000),
        name="pool",
    )(tokens)


def normal_kernel(own_ref, pool_ref, halo_ref, vec_ref, normed_ref, unit_ref):
    gain, bias = vec_ref[0:1], vec_ref[1:2]
    start = 0
    for ref in (own_ref, pool_ref, halo_ref):
        for r in range(0, ref.shape[0], BLOCK):
            unit = ref[r : r + BLOCK].astype(jnp.float32)
            if ref is halo_ref:
                unit, _ = standardize(unit)
                rows = slice(start, start + BLOCK)
                unit_ref[rows] = jnp.zeros(unit.shape, jnp.bfloat16)
                normed_ref[rows] = jnp.zeros(unit.shape, jnp.bfloat16)
                start += BLOCK
            rows = slice(start, start + BLOCK)
            unit_ref[rows] = unit.astype(jnp.bfloat16)
            normed_ref[rows] = (unit * gain + bias).astype(jnp.bfloat16)
            start += BLOCK


def normal(unit_own, unit_pool, halo, vectors):
    width = unit_own.shape[1]
    total = unit_own.shape[0] + unit_pool.shape[0] + 2 * halo.shape[0]
    return pl.pallas_call(
        normal_kernel,
        out_shape=[shape(total, width), shape(total, width)],
        compiler_params=params(24),
        cost_estimate=cost(2_000_000_000, 10_000_000),
        name="normal",
    )(unit_own, unit_pool, halo, vectors)


def mlp_kernel(
    info_ref,
    att_ref,
    tokens_ref,
    dy_ref,
    vec_ref,
    out_own,
    out_other,
    up_own,
    up_other,
    down_ref,
    output_ref,
    dafter_ref,
    datt_ref,
    gd_own,
    gd_other,
    gu_own,
    gu_other,
    sums_ref,
    after_ref,
    n2_ref,
    active_ref,
    dh_ref,
    dn2_ref,
    total_ref,
    grad_ref,
    acc,
    low,
):
    i = pl.program_id(0)
    core = info_ref[1]
    side = out_own.shape[1]
    count, width = n2_ref.shape
    row_steps = count // ROWS
    steps = pl.num_programs(0) - 2 * row_steps
    half = steps // 2
    j = i - row_steps

    @pl.when(i < row_steps)
    def _():
        rows = pl.ds(pl.multiple_of(i * ROWS, ROWS), ROWS)
        after_ref[rows, lanes_at(core, side)] = dot_nn(att_ref[rows], out_own[...])
        after_ref[rows, lanes_at(1 - core, side)] = dot_nn(att_ref[rows], out_other[...])
        after = tokens_ref[...].astype(jnp.float32) + after_ref[rows]
        after_ref[rows] = after
        unit, _ = standardize(after)
        n2_ref[rows] = (unit * vec_ref[2:3] + vec_ref[3:4]).astype(jnp.bfloat16)
        dn2_ref[rows] = jnp.zeros((ROWS, width), jnp.float32)
        total_ref[rows] = after

    @pl.when((j >= 0) & (j < steps))
    def _():
        weight = jnp.where(j < half, up_own[...], up_other[...])
        down = down_ref[...]
        root = (2.0 / 3.141592653589793) ** 0.5

        def first(r):
            rows = slice(r, r + ROWS)
            return rows, dot_nn(n2_ref[rows], weight), dot_nt(dy_ref[rows], down)

        def second(rows, u, dactive):
            square = u * u
            t = jnp.tanh(u * (root + (0.044715 * root) * square))
            upper = 0.5 + 0.5 * t
            active = u * upper
            bend = active * ((1.0 - t) * (root + (3.0 * 0.044715 * root) * square))
            active = active.astype(jnp.bfloat16)
            dh = (dactive * (upper + bend)).astype(jnp.bfloat16)
            active_ref[rows] = active
            dh_ref[rows] = dh
            dn2_ref[rows] += dot_nt(dh, weight)
            total_ref[rows] += dot_nn(active, down)

        waiting = first(0)
        for r in range(ROWS, count, ROWS):
            coming = first(r)
            second(*waiting)
            waiting = coming
        second(*waiting)
        grad_ref[...] = dot_tn(active_ref[...], dy_ref[...]).astype(jnp.bfloat16)
        per = gd_own.shape[1] // side
        for s in range(gd_own.shape[0] // GROUP):
            for g in range(per):
                rows = slice((s * per + g) * GROUP, (s * per + g + 1) * GROUP)
                to = (slice(s * GROUP, (s + 1) * GROUP), slice(g * side, (g + 1) * side))
                gd_own[to] = grad_ref[rows, lanes_at(core, side)]
                gd_other[to] = grad_ref[rows, lanes_at(1 - core, side)]
        grad = dot_tn(n2_ref[...], dh_ref[...]).astype(jnp.bfloat16)

        @pl.when(j < half)
        def _():
            gu_own[:, lanes_at(j, CHUNK)] = grad

        @pl.when(j >= half)
        def _():
            gu_other[:, lanes_at(j - half, CHUNK)] = grad

    @pl.when(j == steps)
    def _():
        sums_ref[...] = jnp.zeros_like(sums_ref)
        acc[...] = jnp.zeros_like(acc)

    @pl.when(j >= steps)
    def _():
        rows = pl.ds(pl.multiple_of((j - steps) * ROWS, ROWS), ROWS)
        output_ref[...] = total_ref[rows].astype(jnp.bfloat16)
        unit, scale = standardize(after_ref[rows])
        dn2 = dn2_ref[rows]
        sums_ref[0:1] += jnp.sum(dn2 * unit, axis=0, keepdims=True)
        sums_ref[1:2] += jnp.sum(dn2, axis=0, keepdims=True)
        dafter = dy_ref[rows].astype(jnp.float32)
        dafter += standardize_back(unit, scale, dn2 * vec_ref[2:3])
        dafter_ref[...] = dafter
        low[...] = dafter.astype(jnp.bfloat16)
        datt = dot_nt(low[:, lanes_at(core, side)], out_own[...])
        datt += dot_nt(low[:, lanes_at(1 - core, side)], out_other[...])
        datt_ref[...] = datt.astype(jnp.bfloat16)
        acc[...] += dot_tn(att_ref[rows], low[...])

    @pl.when(i == pl.num_programs(0) - 1)
    def _():
        at = gu_own.shape[1] - side
        gu_own[:, at:] = acc[:, lanes_at(core, side)].astype(jnp.bfloat16)
        gu_other[:, at:] = acc[:, lanes_at(1 - core, side)].astype(jnp.bfloat16)


def ff_maps(hidden, before):
    steps = hidden // CHUNK
    half = steps // 2
    step = lambda i: jnp.clip(i - before, 0, steps - 1)
    own = lambda i, f: (0, jnp.minimum(step(i), half - 1))
    other = lambda i, f: (0, jnp.maximum(step(i) - half, 0))
    place = lambda i, f: lax.rem(f[1] * half + step(i), steps)
    return steps, own, other, place


def out_columns(own):
    width = own.shape[0]
    half = width // 2
    return pl.BlockSpec((width, half), lambda i, f: (0, own.shape[1] // half - 1))


def mlp(attended, tokens, upstream, vectors, own, other, mat_down, info):
    count, width = tokens.shape
    hidden = mat_down.shape[0]
    row_steps = count // ROWS
    steps, first, second, place = ff_maps(hidden, row_steps)
    whole = lambda i, f: (0, 0)
    once = pl.Buffered(1)
    full = pl.BlockSpec((count, width), whole, pipeline_mode=once)
    grads = pl.BlockSpec(own.shape, whole, pipeline_mode=once)
    low_grads = pl.BlockSpec((CHUNK // 4, 2 * width), lambda i, f: (place(i, f), 0))
    row = pl.BlockSpec((ROWS, width), lambda i, f: (jnp.maximum(i - row_steps - steps, 0), 0))
    f32 = jnp.float32
    return pl.pallas_call(
        mlp_kernel,
        grid_spec=pltpu.PrefetchScalarGridSpec(
            num_scalar_prefetch=1,
            grid=(2 * row_steps + steps,),
            in_specs=[
                full,
                pl.BlockSpec((ROWS, width), lambda i, f: (jnp.minimum(i, row_steps - 1), 0)),
                full,
                pl.BlockSpec(vectors.shape, whole),
                out_columns(own),
                out_columns(other),
                pl.BlockSpec((width, CHUNK), first),
                pl.BlockSpec((width, CHUNK), second),
                pl.BlockSpec((CHUNK, width), lambda i, f: (place(i, f), 0)),
            ],
            out_specs=[
                row,
                row,
                row,
                low_grads,
                low_grads,
                grads,
                grads,
                pl.BlockSpec((8, width), whole),
            ],
            scratch_shapes=[
                pltpu.VMEM((count, width), f32),
                pltpu.VMEM((count, width), jnp.bfloat16),
                pltpu.VMEM((count, CHUNK), jnp.bfloat16),
                pltpu.VMEM((count, CHUNK), jnp.bfloat16),
                pltpu.VMEM((count, width), f32),
                pltpu.VMEM((count, width), f32),
                pltpu.VMEM((CHUNK, width), jnp.bfloat16),
                pltpu.VMEM((width, width), f32),
                pltpu.VMEM((ROWS, width), jnp.bfloat16),
            ],
        ),
        out_shape=[
            shape(count, width),
            shape(count, width, f32),
            shape(count, width),
            shape(hidden // 4, 2 * width),
            shape(hidden // 4, 2 * width),
            shape(*own.shape),
            shape(*own.shape),
            shape(8, width, f32),
        ],
        compiler_params=params(58),
        cost_estimate=cost(40_000_000_000, 30_000_000),
        name="mlp",
    )(info, attended, tokens, upstream, vectors, own, other, own, other, mat_down)


def project_back_kernel(dm_own, dm_other, own_ref, other_ref, unit_ref, dn_ref, sums_ref):
    @pl.when(pl.program_id(0) == 0)
    def _():
        sums_ref[...] = jnp.zeros_like(sums_ref)

    dn = dot_nt(dm_own[...], own_ref[...]) + dot_nt(dm_other[...], other_ref[...])
    dn_ref[...] = dn
    sums_ref[0:1] += jnp.sum(dn * unit_ref[...].astype(jnp.float32), axis=0, keepdims=True)
    sums_ref[1:2] += jnp.sum(dn, axis=0, keepdims=True)


def project_back(dm_own, dm_other, own, other, unit):
    total, width = unit.shape
    rows = total // 4
    row = lambda i: (i, 0)
    whole = pl.BlockSpec((width, 3 * HALF), lambda i: (0, 0))
    return pl.pallas_call(
        project_back_kernel,
        grid=(total // rows,),
        in_specs=[
            pl.BlockSpec((rows, 3 * HALF), row),
            pl.BlockSpec((rows, 3 * HALF), row),
            whole,
            whole,
            pl.BlockSpec((rows, width), row),
        ],
        out_specs=[pl.BlockSpec((rows, width), row), pl.BlockSpec((8, width), lambda i: (0, 0))],
        out_shape=[shape(total, width, jnp.float32), shape(8, width, jnp.float32)],
        compiler_params=params(32),
        cost_estimate=cost(6_000_000_000, 16_000_000),
        name="project_back",
    )(dm_own, dm_other, own, other, unit)


def input_kernel(tokens_ref, dn_ref, dafter_ref, pool_ref, next_ref, vec_ref, out_ref):
    i = pl.program_id(0)
    gain = vec_ref[0:1]
    per = tokens_ref.shape[0] // BLOCK
    last = (i == pl.num_programs(0) - 1).astype(jnp.float32)
    for b in range(per):
        rows = slice(b * BLOCK, (b + 1) * BLOCK)
        unit, scale = standardize(tokens_ref[rows].astype(jnp.float32))
        dn = dn_ref[rows] + pool_ref[pl.ds(i * per + b, 1)] * (1.0 / BLOCK)
        if b == per - 1:
            dn += next_ref[...].astype(jnp.float32) * last
        out_ref[rows] = dafter_ref[rows] + standardize_back(unit, scale, dn * gain)


def input_back(tokens, dnormed, dafter, from_pool, from_next, vectors):
    count, width = tokens.shape
    row = pl.BlockSpec((ROWS, width), lambda i: (i, 0))
    whole = lambda i: (0, 0)
    return pl.pallas_call(
        input_kernel,
        grid=(count // ROWS,),
        in_specs=[
            row,
            row,
            row,
            pl.BlockSpec(from_pool.shape, whole),
            pl.BlockSpec(from_next.shape, whole),
            pl.BlockSpec(vectors.shape, whole),
        ],
        out_specs=row,
        out_shape=shape(count, width, jnp.float32),
        compiler_params=params(24),
        cost_estimate=cost(3_000_000_000, 12_000_000),
        name="input_back",
    )(tokens, dnormed, dafter, from_pool, from_next, vectors)


def shift_seq(value, distance):
    size = lax.axis_size("seq")
    route = [(i - distance, i) for i in range(size) if 0 <= i - distance < size]
    return lax.ppermute(value, "seq", route)


BOTH = ("seq", "batch")


def follows(value, *earlier):
    return lax.optimization_barrier((value, earlier))[0]


def flip_route(size, bit):
    return [(i, i ^ bit) for i in range(size)]


def ring_route(size, stride, steps):
    return [(i, (i + stride * steps) % size) for i in range(size)]


def swap(value, axis, bit):
    return lax.ppermute(value, axis, flip_route(lax.axis_size(axis), bit))


def in_order(bit, own, other):
    return jnp.stack([jnp.where(bit == 0, own, other), jnp.where(bit == 0, other, own)])


def pick(value, index, axis):
    return lax.dynamic_index_in_dim(value, index, axis, keepdims=False)


def add(a, b):
    return (a.astype(jnp.float32) + b.astype(jnp.float32)).astype(jnp.bfloat16)


def place():
    at = lax.axis_index("seq")
    return at // 4, at // 2 % 2, at % 2


def send_line(slab):
    size = lax.axis_size("seq")
    return [lax.ppermute(slab, "seq", ring_route(size, 4, k)) for k in range(1, size // 4)]


def join_line(slab, got):
    z = place()[0]
    stack = jnp.stack([slab] + got)
    layers = stack.shape[0]
    parts = [lax.dynamic_slice_in_dim(stack, (z - k) % layers, 1, 0) for k in range(layers)]
    return jnp.concatenate(parts, 0)


def send_near(line, cut):
    first, second = line[:, :, :cut], line[:, :, cut:]
    return first, second, swap(first, "seq", 1), swap(second, "seq", 2)


def join_near(first, second, first_got, second_got):
    _, y, x = place()
    return in_order(x, first, first_got), in_order(y, second, second_got)


def send_far(first, second):
    return swap(first, "seq", 2), swap(second, "seq", 1)


def join_far(first, second, first_got, second_got):
    _, y, x = place()
    first = jnp.transpose(in_order(y, first, first_got), (2, 0, 1, 3, 4))
    second = jnp.transpose(in_order(x, second, second_got), (2, 1, 0, 3, 4))
    rows = first.shape[3] * lax.axis_size("seq")
    return first.reshape(rows, -1), second.reshape(rows, -1)


def split_grid(full, cut, axis=4):
    grid = full.reshape(lax.axis_size("seq") // 4, 2, 2, -1, full.shape[1])
    return jnp.split(grid, [cut], axis)


def drop_near(first, second):
    _, y, x = place()
    return pick(first, 1 - x, 2), pick(second, 1 - y, 1)


def keep_near(first, second, first_got, second_got):
    _, y, x = place()
    return add(pick(first, x, 2), first_got), add(pick(second, y, 1), second_got)


def drop_far(first, second):
    _, y, x = place()
    return pick(first, 1 - y, 1), pick(second, 1 - x, 1)


def keep_far(first, second, first_got, second_got, axis=2):
    _, y, x = place()
    parts = [add(pick(first, y, 1), first_got), add(pick(second, x, 1), second_got)]
    return jnp.concatenate(parts, axis)


def swap_near(dropped):
    return swap(dropped[0], "seq", 1), swap(dropped[1], "seq", 2)


def swap_far(dropped):
    return swap(dropped[0], "seq", 2), swap(dropped[1], "seq", 1)


def scatter_line(line):
    z = place()[0]
    size = lax.axis_size("seq")
    layers = size // 4
    got = [
        lax.ppermute(pick(line, (z + k) % layers, 0), "seq", ring_route(size, 4, k))
        for k in range(1, layers)
    ]
    return pick(line, z, 0), got


def sum_line(own, got):
    return sum((g.astype(jnp.float32) for g in got), own.astype(jnp.float32))


def paired():
    return lax.axis_size("batch") == 2 and lax.axis_size("seq") % 4 == 0


def side_index():
    return lax.axis_index("batch") % 2


def halves_of(matrix, groups):
    rows, columns = matrix.shape
    parts = matrix.reshape(rows, groups, 2, columns // (2 * groups))
    return jnp.transpose(parts, (2, 0, 1, 3)).reshape(2, rows, columns // 2)


def whole_of(halves, groups):
    _, rows, columns = halves.shape
    parts = halves.reshape(2, rows, groups, columns // groups)
    return jnp.transpose(parts, (1, 2, 0, 3)).reshape(rows, 2 * columns)


def rows_of_side(total):
    side = side_index()
    total = total.reshape(2, -1, total.shape[1])
    got = swap(pick(total, 1 - side, 0), "batch", 1)
    return in_order(side, pick(total, side, 0), got)


def local(
    inputs, selection, cotangent, ln1_gain, ln1_bias, w_qkv, w_out, ln2_gain, ln2_bias, w_up, w_down
):
    bf16, f32 = jnp.bfloat16, jnp.float32
    tokens = inputs[0]
    chosen = selection[0]
    upstream = cotangent[0]
    count, width = tokens.shape
    hidden = w_up.shape[1]
    blocks = count // BLOCK
    size = lax.axis_size("seq")
    pool_rows = blocks * size
    at = lax.axis_index("seq")
    side = side_index()
    fast = paired()

    half_qkv = halves_of(w_qkv, 3)
    half_uo = jnp.concatenate([halves_of(w_up, 1), halves_of(w_out, 1)], 2)
    vectors = jnp.stack([ln1_gain, ln1_bias, ln2_gain, ln2_bias])
    if fast:
        columns = jnp.pad(vectors.T, ((0, 0), (0, 124)))
        columns = jnp.broadcast_to(columns, (2,) + columns.shape)
        bundle = jnp.concatenate([columns, half_qkv, half_uo], 2)
        got = swap(pick(bundle, 1 - side, 0), "batch", 1)
        slab = in_order(side, pick(bundle, side, 0), got).reshape(-1, bundle.shape[2])
        third = width // 3
        per = slab.shape[0] // 3
        unit_own, pooled = pool(tokens)
        pooled = jnp.transpose(pooled.astype(bf16).reshape(per, 3, third), (1, 0, 2))
        pooled = pooled.reshape(-1, third)
        front = third + 128
        edge = 128 + half_qkv.shape[2]
        slab_q = jnp.concatenate([pooled, slab[:, :edge]], 1)
        slab_u = slab[:, edge:]
        line_got = send_line(slab_q)
        halo = shift_seq(follows(tokens[-BLOCK:], slab), 1)
        line_got_u = send_line(slab_u)
        line_q = join_line(slab_q, follows(line_got, halo))
        near = send_near(line_q, 768)
        wide_q = join_near(*near)
        far = send_far(*wide_q)
        line_u = join_line(slab_u, follows(line_got_u, wide_q))
        near_u = send_near(line_u, 1024)
        first, second = join_far(*wide_q, *follows(far, near_u[0], near_u[1]))
        own_qkv = jnp.concatenate([first[:, front:], second], 1)
        other_qkv = swap(own_qkv, "batch", 1)
        unit_pool = jnp.transpose(first[:, :third].reshape(size, 3, per, third), (0, 2, 1, 3))
        unit_pool = unit_pool.reshape(pool_rows, width)
        vectors = first[:, third : third + 4].T.astype(f32)
    else:
        gathered = lax.all_gather(half_qkv, BOTH, axis=1, tiled=True)
        own_qkv, other_qkv = pick(gathered, side, 0), pick(gathered, 1 - side, 0)
        gathered = lax.all_gather(half_uo, BOTH, axis=1, tiled=True)
        own_uo, other_uo = pick(gathered, side, 0), pick(gathered, 1 - side, 0)
        halo = shift_seq(tokens[-BLOCK:], 1)
        unit_own, pooled = pool(tokens)
        unit_pool = lax.all_gather(pooled.astype(bf16), "seq", axis=0, tiled=True)
        vectors = lax.all_gather(vectors, BOTH, axis=1, tiled=True).astype(f32)
    mat_down = lax.all_gather(w_down, BOTH, axis=0, tiled=True)
    vectors = jnp.pad(vectors, ((0, 4), (0, 0)))

    normed, unit = normal(unit_own, unit_pool, halo, vectors)
    mixed_own = dot_nn(normed, own_qkv).astype(bf16)
    mixed_other = dot_nn(normed, other_qkv).astype(bf16)
    if fast:
        wide_u = join_near(*follows(near_u, mixed_other))
        far_u = send_far(*wide_u)
        mixed_own = follows(mixed_own, wide_u)

    block_ids = at * blocks + jnp.arange(blocks, dtype=jnp.int32)
    flat = chosen.reshape(blocks * TOPK)
    far_bias = jnp.where(chosen < block_ids[:, None], 0.0, NEG).reshape(blocks * TOPK, 1)
    info = jnp.stack([(at == 0).astype(jnp.int32), side])
    attended, probs, picks = attend(
        mixed_own, mixed_other, flat[:, None], far_bias, info, blocks, pool_rows
    )
    if fast:
        own_uo = jnp.concatenate(join_far(*wide_u, *follows(far_u, attended)), 1)
        other_uo = swap(own_uo, "batch", 1)
    output, dafter, dattended, down_own, down_other, uo_own, uo_other, sums_two = mlp(
        attended, tokens, upstream, vectors, own_uo, other_uo, mat_down, info
    )
    if fast:
        down_got = swap(down_other, "batch", 1)
        uo_got = swap(uo_other, "batch", 1)
        grid_d = split_grid(add(down_own, down_got), width)
        drop_d = drop_near(*grid_d)
        near_d = swap_near(drop_d)
        grid_u = split_grid(add(uo_own, follows(uo_got, drop_d)), 1024)
        drop_u = drop_near(*grid_u)
        near_u = swap_near(drop_u)
        dattended = follows(dattended, drop_u)

    dmixed_own, dmixed_other = attend_back(
        mixed_own, mixed_other, flat[None, :], info, picks, probs, dattended, blocks, pool_rows
    )
    if fast:
        kept_d = keep_near(*grid_d, *follows(near_d, dmixed_own))
        drop_d = drop_far(*kept_d)
        far_d = swap_far(drop_d)
        dmixed_other = follows(dmixed_other, drop_d)
    grad_other = dot_tn(normed, dmixed_other).astype(bf16)
    if fast:
        grad_got = swap(grad_other, "batch", 1)
        kept_u = keep_near(*grid_u, *follows(near_u, grad_other))
        drop_u = drop_far(*kept_u)
        far_u = swap_far(drop_u)
        dmixed_own = follows(dmixed_own, drop_u)
    grad_own = dot_tn(normed, dmixed_own).astype(bf16)
    if fast:
        grid_q = split_grid(add(grad_own, grad_got), 512)
        drop_q = drop_near(*grid_q)
        near_q = swap_near(drop_q)
        line_d = keep_far(*kept_d, *follows(far_d, drop_q))
        line_d, got_d = scatter_line(line_d)
        dmixed_own = follows(dmixed_own, line_d)
    dnormed, sums_one = project_back(dmixed_own, dmixed_other, own_qkv, other_qkv, unit)
    vector_grads = jnp.concatenate([sums_one[:2], sums_two[:2]], 0)
    from_next = shift_seq(dnormed[-BLOCK:].astype(bf16), -1)
    dpool = dnormed[count : count + pool_rows].astype(bf16)
    if fast:
        kept_q = keep_near(*grid_q, *follows(near_q, dnormed))
        drop_q = drop_far(*kept_q)
        far_q = swap_far(drop_q)
        spread = jnp.transpose(vector_grads.reshape(4, size, -1), (1, 0, 2)).reshape(size, 1, -1)
        span = spread.shape[2]
        spread = jnp.pad(spread.astype(bf16), ((0, 0), (0, 7), (0, width - span)))
        send = jnp.concatenate([dpool.reshape(size, blocks, width), spread], 1)
        pool_got = lax.all_to_all(send, "seq", 0, 0)
        line_u = keep_far(*kept_u, *follows(far_u, drop_q))
        line_u, got_u = scatter_line(line_u)
        line_q = keep_far(*kept_q, *follows(far_q, send, line_u))
        line_q, got_q = scatter_line(line_q)
        sum_down = sum_line(line_d, follows(got_d, line_q)).reshape(GROUP, 2, -1)
        sum_down = rows_of_side(jnp.transpose(sum_down, (1, 0, 2)).reshape(2 * GROUP, -1))
        sum_down = sum_down.reshape(2, GROUP, 2, -1)
        sum_down = jnp.transpose(sum_down, (2, 1, 0, 3)).reshape(-1, width)
        got = jnp.sum(follows(pool_got, line_q).astype(f32), axis=0)
        from_pool = got[:blocks]
        chip = got[blocks, :span].reshape(4, 2, -1)
        vector_sums = pick(chip, side, 1) + swap(pick(chip, 1 - side, 1), "batch", 1)
        sum_uo = rows_of_side(sum_line(line_u, follows(got_u, line_q)))
    else:
        from_pool = lax.psum_scatter(dpool, "seq", scatter_dimension=0, tiled=True).astype(f32)
        vector_sums = lax.psum_scatter(vector_grads, BOTH, scatter_dimension=1, tiled=True)
    input_grad = input_back(tokens, dnormed, dafter, from_pool, from_next, vectors)
    if fast:
        sum_qkv = rows_of_side(sum_line(line_q, follows(got_q, input_grad)))
    else:

        def scatter(own, other):
            full = in_order(side, own, other)
            sums = lax.psum_scatter(full, BOTH, scatter_dimension=1, tiled=True)
            return sums.astype(f32)

        sum_uo = scatter(uo_own, uo_other)
        sum_qkv = scatter(grad_own, grad_other)
        full = jnp.stack([down_own, down_other]).reshape(2, -1, GROUP, 4, width // 2)
        full = jnp.transpose(full, (1, 3, 2, 0, 4)).reshape(hidden, 2, width // 2)
        full = in_order(side, full[:, 0], full[:, 1])
        full = jnp.transpose(full, (1, 0, 2)).reshape(hidden, width)
        sum_down = lax.psum_scatter(full, BOTH, scatter_dimension=0, tiled=True).astype(f32)

    split = hidden // 2
    return (
        output[None],
        input_grad[None],
        vector_sums[0],
        vector_sums[1],
        whole_of(sum_qkv, 3),
        whole_of(sum_uo[:, :, split:], 1),
        vector_sums[2],
        vector_sums[3],
        whole_of(sum_uo[:, :, :split], 1),
        sum_down,
    )


def solution(mesh):
    tokens = P("batch", "seq", None)
    vector = P(BOTH)
    matrix = P(BOTH, None)
    return jax.shard_map(
        local,
        mesh=mesh,
        in_specs=(
            tokens,
            tokens,
            tokens,
            vector,
            vector,
            matrix,
            matrix,
            vector,
            vector,
            matrix,
            matrix,
        ),
        out_specs=(
            tokens,
            tokens,
            vector,
            vector,
            matrix,
            matrix,
            vector,
            vector,
            matrix,
            matrix,
        ),
        check_vma=False,
    )
```

time: 348 us -> 318 us (0.914)
  Pallas kernels: 122 us -> 82.3 us
  local copies, waits for them, and re-layouts: 56.3 us -> 42 us
  waiting for transfers between devices: 43.4 us -> 57.1 us
  matrix products: 6.46 us -> 16.5 us
    pallas_call x8 -> x4, Pallas kernels: 96 us -> 63.2 us  [the longest x1 51.9 us: mlp(): pl.pallas_call(mlp_kernel, grid_spec=pltpu.PrefetchScalarGridSpec(num_sca...]
    unnamed x119 -> x100, local copies, waits for them, and re-layouts: 43.2 us -> 22.2 us
    ppermute x9, waiting for transfers between devices: 1.75 us -> 14.8 us  [scatter_line(): lax.ppermute(pick(line, (z + k) % layers, 0), 'seq', ring_route(size, 4, k))]
    dot_general x0 -> x2, matrix products: none -> 8.93 us  [dot_nn(): lax.dot_general(a, b, (((1,), (0,)), ((), ())), preferred_element_type=jn...]
    pallas_call x1, Pallas kernels: 15.6 us -> 7.55 us  [attend(): pl.pallas_call(attend_kernel, grid_spec=pltpu.PrefetchScalarGridSpec(num_...]
    ppermute x6, waiting for transfers between devices: 17.8 us -> 10.8 us  [send_line(): lax.ppermute(slab, 'seq', ring_route(size, 4, k))]
    another operation x16 -> x14, other arithmetic: 10.3 us -> 3.64 us  [in_order(): jnp.stack([jnp.where(bit == 0, own, other), jnp.where(bit == 0, other, ow...]
    ppermute x31 -> x30, waiting for transfers between devices: 23.8 us -> 29.4 us  [swap(): return lax.ppermute(value, axis, flip_route(lax.axis_size(axis), bit))]
  transfers between devices with their start and end apart: 50 -> 49, of which waited for: 12 -> 15; matrix products, arithmetic and copies ran while one was open for 13% -> 20% of each run, Pallas kernels for 36% -> 10%
where the time goes in v4:
time: 318 us; the launch traced here: 313 us
  Pallas kernels  82.3 us (26%)
  starting transfers between devices  70.8 us (22%)
  waiting for transfers between devices  57.1 us (18%)
  local copies, waits for them, and re-layouts  42 us (13%)
  other arithmetic  28.7 us (9%)
  matrix products  16.5 us (5%)
  between operations  15.8 us (5%)
    pallas_call x1, Pallas kernels, mlp(): pl.pallas_call(mlp_kernel, grid_spec=pltpu.PrefetchScalarGridSpec(num_sca...  51.9 us
    ppermute x30, waiting for transfers between devices, swap(): return lax.ppermute(value, axis, flip_route(lax.axis_size(axis), bit))  29.4 us
    ppermute x30, starting transfers between devices, swap(): return lax.ppermute(value, axis, flip_route(lax.axis_size(axis), bit))  26 us
    unnamed x100, local copies, waits for them, and re-layouts  22.2 us
    ppermute x9, starting transfers between devices, scatter_line(): lax.ppermute(pick(line, (z + k) % layers, 0), 'seq', ring_route(size, 4, k))  16.5 us
    convert_element_type x15, other arithmetic, add(): return (a.astype(jnp.float32) + b.astype(jnp.float32)).astype(jnp.bfloat16)  16.2 us
    ppermute x6, starting transfers between devices, send_line(): lax.ppermute(slab, 'seq', ring_route(size, 4, k))  15.2 us
    ppermute x9, waiting for transfers between devices, scatter_line(): lax.ppermute(pick(line, (z + k) % layers, 0), 'seq', ring_route(size, 4, k))  14.8 us
  transfers between devices with their start and end apart: 49, of which 15 were waited for; matrix products, arithmetic and copies ran while one was open for 20% of the time, Pallas kernels for 10%

profile of v4, /device:TPU:0, one launch (start us, length us, event | category | flops | bytes accessed | tf_op | source)
XLA Modules:
  0.0 313.2 jit_solution(15484901005201080305)
XLA Ops:
  22.3 3.4 %collective-permute-start.4 = (bf16[64,768]{1,0:T(8,128)(2,1)S(1)}, bf16[64,768]{1,0:T(8,128)(2,1)S(1)}, u32[]{:S(2)}, u32[]{:S(2)}) collective-permute-start(bf16[64,768]{1,0:T(8,128)(2,1)S(1)} %slice_bitcast_fusion), channel_id=1, source_target_pairs={{0,2},{2,4},{4,6},{6,8},{8,10},{10,12},{12,14},{14,16},{16,18},{18... | collective-permute-start | bytes 294920 | tf_op jit(solution)/shard_map/ppermute | solution.py:683
  27.9 3.4 %collective-permute-done.2 = bf16[48,1536]{1,0:T(8,128)(2,1)S(1)} collective-permute-done((bf16[48,1536]{1,0:T(8,128)(2,1)S(1)}, bf16[48,1536]{1,0:T(8,128)(2,1)S(1)}, u32[]{:S(2)}, u32[]{:S(2)}) %collective-permute-start.2) | collective-permute-done | bytes 147488 | tf_op jit(solution)/shard_map/ppermute | solution.py:724
  34.7 6.1 %collective-permute-start.10 = (bf16[48,1920]{1,0:T(8,128)(2,1)S(1)}, bf16[48,1920]{1,0:T(8,128)(2,1)S(1)}, u32[]{:S(2)}, u32[]{:S(2)}) collective-permute-start(bf16[48,1920]{1,0:T(8,128)(2,1)S(1)} %get-tuple-element.187), channel_id=1, source_target_pairs={{0,16},{2,18},{4,20},{6,22},{8,24},{10,26},{12,28},{14,30},{16,0},... | collective-permute-start | bytes 552968 | tf_op jit(solution)/shard_map/ppermute | solution.py:724
  47.6 4.1 %collective-permute-done.10 = bf16[48,1920]{1,0:T(8,128)(2,1)S(1)} collective-permute-done((bf16[48,1920]{1,0:T(8,128)(2,1)S(1)}, bf16[48,1920]{1,0:T(8,128)(2,1)S(1)}, u32[]{:S(2)}, u32[]{:S(2)}) %collective-permute-start.10) | collective-permute-done | bytes 184352 | tf_op jit(solution)/shard_map/ppermute | solution.py:724
  51.7 3.3 %collective-permute-done.11 = bf16[48,1920]{1,0:T(8,128)(2,1)S(1)} collective-permute-done((bf16[48,1920]{1,0:T(8,128)(2,1)S(1)}, bf16[48,1920]{1,0:T(8,128)(2,1)S(1)}, u32[]{:S(2)}, u32[]{:S(2)}) %collective-permute-start.11) | collective-permute-done | bytes 184352 | tf_op jit(solution)/shard_map/ppermute | solution.py:724
  72.9 3.1 %convolution_convert_fusion.1.pool_own.prev_own.cur_own = bf16[1408,1152]{1,0:T(8,128)(2,1)S(1)} fusion(bf16[1408,768]{1,0:T(8,128)(2,1)S(1)} %get-tuple-element.82, bf16[768,768]{1,0:T(8,128)(2,1)S(1)} %bitcast.274, bf16[768,384]{1,0:T(8,128)(2,1)S(1)} %slice.103), kind=kOutput, calls=%fused_computation.1 | convolution fusion | flops 2496577536 | bytes 7176192 | tf_op jit(solution)/shard_map/dot_general | solution.py:20
  76.1 5.8 %convolution_convert_fusion.pool_other.prev_other.cur_other = bf16[1408,1152]{1,0:T(8,128)(2,1)S(1)} fusion(bf16[1408,768]{1,0:T(8,128)(2,1)S(1)} %get-tuple-element.82, bf16[768,1152]{1,0:T(8,128)(2,1)} %collective-permute-done.14.other_ref), kind=kOutput, calls=%fused_computation | convolution fusion | flops 2493038592 | bytes 7176192 | tf_op jit(solution)/shard_map/dot_general | solution.py:20
  86.8 7.5 %attend.1 = (bf16[1024,768]{1,0:T(8,128)(2,1)S(1)}, f32[16,3,80,256]{3,2,1,0:T(8,128)S(1)}, bf16[2,256,768]{2,1,0:T(8,128)(2,1)S(1)}) custom-call(s32[2]{0:T(128)S(1)} %pad_add_fusion.info_ref, s32[256,1]{1,0:T(8,128)S(1)} %broadcast_in_dim_reshape_squeeze.8.sel_ref, f32[256,1]{1,0:T(8,128)S(1)} %compare_select_fusion.bias_ref, ...), custom_call_target="tpu_custom_call" | custom-call | flops 12000000000 | bytes 12000000 | tf_op jit(solution)/shard_map/attend/pallas_call | solution.py:153
  94.4 6.2 %collective-permute-done.16 = bf16[2,4,48,896]{3,2,1,0:T(8,128)(2,1)S(1)} collective-permute-done((bf16[2,4,48,896]{3,2,1,0:T(8,128)(2,1)S(1)}, bf16[2,4,48,896]{3,2,1,0:T(8,128)(2,1)S(1)}, u32[]{:S(2)}, u32[]{:S(2)}) %collective-permute-start.16) | collective-permute-done | bytes 688160 | tf_op jit(solution)/shard_map/ppermute | solution.py:702
  100.7 4.9 %collective-permute-done.15 = bf16[2,4,48,1024]{3,2,1,0:T(8,128)(2,1)S(1)} collective-permute-done((bf16[2,4,48,1024]{3,2,1,0:T(8,128)(2,1)S(1)}, bf16[2,4,48,1024]{3,2,1,0:T(8,128)(2,1)S(1)}, u32[]{:S(2)}, u32[]{:S(2)}) %collective-permute-start.15) | collective-permute-done | bytes 786464 | tf_op jit(solution)/shard_map/ppermute | solution.py:702
  108.3 5.5 %collective-permute-done.17.out_other.up_other = bf16[768,1920]{1,0:T(8,128)(2,1)} collective-permute-done((bf16[768,1920]{1,0:T(8,128)(2,1)S(1)}, bf16[768,1920]{1,0:T(8,128)(2,1)}, u32[]{:S(2)}, u32[]{:S(2)}) %collective-permute-start.17) | collective-permute-done | bytes 2949152 | tf_op jit(solution)/shard_map/ppermute | solution.py:702
  113.8 51.9 %mlp.1 = (bf16[1024,768]{1,0:T(8,128)(2,1)}, f32[1024,768]{1,0:T(8,128)}, bf16[1024,768]{1,0:T(8,128)(2,1)}, bf16[768,1536]{1,0:T(8,128)(2,1)}, bf16[768,1536]{1...) custom-call(s32[2]{0:T(128)} %copy-done.7, ...), custom_call_target="tpu_custom_call" | custom-call | flops 40000000000 | bytes 30000000 | tf_op jit(solution)/shard_map/mlp/pallas_call | solution.py:555
  166.4 4.3 %collective-permute-done.19 = bf16[768,1536]{1,0:T(8,128)(2,1)} collective-permute-done((bf16[768,1536]{1,0:T(8,128)(2,1)}, bf16[768,1536]{1,0:T(8,128)(2,1)}, u32[]{:S(2)}, u32[]{:S(2)}) %collective-permute-start.19) | collective-permute-done | bytes 2359328 | tf_op jit(solution)/shard_map/ppermute | solution.py:702
  170.7 3.0 add_convert_fusion.1
  183.4 9.4 %attend_back.1 = (bf16[1408,1152]{1,0:T(8,128)(2,1)S(1)}, bf16[1408,1152]{1,0:T(8,128)(2,1)S(1)}) custom-call(s32[2]{0:T(128)S(1)} %copy-done.8, s32[1,256]{1,0:T(1,128)S(1)} %broadcast_in_dim_reshape_squeeze.7.sel_ref, bf16[1408,1152]{1,0:T(8,128)(2,1)S(1)} %copy-done.23, bf16[1408,1152]{1,0:T(8,128)(2,1)S(1)} %copy-done.23, ...), custom_call_target="tpu_custom_call" | custom-call | flops 20000000000 | bytes 18000000 | tf_op jit(solution)/shard_map/attend_back/pallas_call | solution.py:288
  196.2 4.3 %convolution_convert_fusion.3 = bf16[768,1152]{1,0:T(8,128)(2,1)} fusion(bf16[1408,768]{1,0:T(8,128)(2,1)S(1)} %copy-done.14, bf16[1408,1152]{1,0:T(8,128)(2,1)S(1)} %get-tuple-element.106.dm_other), kind=kOutput, calls=%fused_computation.6 | convolution fusion | flops 2492301312 | bytes 7176192 | tf_op jit(solution)/shard_map/dot_general | solution.py:28
  215.5 3.3 %convolution_convert_fusion.2 = bf16[768,1152]{1,0:T(8,128)(2,1)S(1)} fusion(bf16[1408,768]{1,0:T(8,128)(2,1)S(1)} %copy-done.15, bf16[1408,1152]{1,0:T(8,128)(2,1)S(1)} %copy-done.10), kind=kOutput, calls=%fused_computation.5 | convolution fusion | flops 2492301312 | bytes 7176192 | tf_op jit(solution)/shard_map/dot_general | solution.py:28
  225.2 8.3 %project_back.1 = (f32[1408,768]{1,0:T(8,128)S(1)}, f32[8,768]{1,0:T(8,128)S(1)}) custom-call(bf16[1408,1152]{1,0:T(8,128)(2,1)S(1)} %copy-done.10, bf16[1408,1152]{1,0:T(8,128)(2,1)S(1)} %copy-done.12, bf16[768,1152]{1,0:T(8,128)(2,1)S(1)} %pad_maximum_fusion.1.own_ref, bf16[768,1152]{1,0:T(8,128)(2,1)} %collective-permute-done.14.other_ref, ...), custom_call_target="tpu_custom_call" | custom-call | flops 6000000000 | bytes 16000000 | tf_op jit(solution)/shard_map/project_back/pallas_call | solution.py:625
  238.0 8.4 %all-to-all-start = ((bf16[16,24,768]{2,1,0:T(8,128)(2,1)}), bf16[16,24,768]{2,1,0:T(8,128)(2,1)}, u32[]{:S(2)}, u32[]{:S(2)}) async-start(bf16[16,24,768]{2,1,0:T(8,128)(2,1)} %fusion.9), calls=%async_computation | async-start | bytes 1179648 | tf_op jit(solution)/shard_map/all_to_all | solution.py:961
  246.3 2.8 collective-permute-start.44
  261.7 3.9 %collective-permute-start.39 = (bf16[48,1920]{1,0:T(8,128)(2,1)S(1)}, bf16[48,1920]{1,0:T(8,128)(2,1)S(1)}, u32[]{:S(2)}, u32[]{:S(2)}) collective-permute-start(bf16[48,1920]{1,0:T(8,128)(2,1)S(1)} %get-tuple-element.156), channel_id=1, source_target_pairs={{0,8},{2,10},{4,12},{6,14},{8,16},{10,18},{12,20},{14,22},{16,24},... | collective-permute-start | bytes 552968 | tf_op jit(solution)/shard_map/ppermute | solution.py:796
  268.0 7.7 %collective-permute-done.44 = bf16[48,1536]{1,0:T(8,128)(2,1)S(1)} collective-permute-done((bf16[48,1536]{1,0:T(8,128)(2,1)}, bf16[48,1536]{1,0:T(8,128)(2,1)S(1)}, u32[]{:S(2)}, u32[]{:S(2)}) %collective-permute-start.44) | collective-permute-done | bytes 147488 | tf_op jit(solution)/shard_map/ppermute | solution.py:796
  277.8 7.1 %collective-permute-done.40 = bf16[48,1920]{1,0:T(8,128)(2,1)S(1)} collective-permute-done((bf16[48,1920]{1,0:T(8,128)(2,1)S(1)}, bf16[48,1920]{1,0:T(8,128)(2,1)S(1)}, u32[]{:S(2)}, u32[]{:S(2)}) %collective-permute-start.40) | collective-permute-done | bytes 184352 | tf_op jit(solution)/shard_map/ppermute | solution.py:796
  298.5 3.4 %input_back.1 = f32[1024,768]{1,0:T(8,128)} custom-call(bf16[1024,768]{1,0:T(8,128)(2,1)S(1)} %bitcast.264, f32[1408,768]{1,0:T(8,128)S(1)} %copy-done.1, f32[1024,768]{1,0:T(8,128)S(1)} %copy-done.2, f32[16,768]{1,0:T(8,128)S(1)} %slice.107.pool_ref, bf16[64,768]{1,0:T(8,128)(2,1)S(1)} %collective-permute-done.33.next_ref, f32[8,768]{1,0:T(8,128)S(1)} %copy-done.6), custom_call_target="tpu_custom_call" | custom-call | flops 3000000000 | bytes 12000000 | tf_op jit(solution)/shard_map/input_back/pallas_call | solution.py:661
  (321 shorter events, 126.3 us)
Async XLA Ops:
  7.2 106.6 %all-gather.2.cloned.1.call-start = ((), (), s32[]{:S(2)}) async-start(), calls=%async_computation.1 | async-start | bytes 4866048 | tf_op jit(solution)/shard_map/all_gather | solution.py:891
  34.7 17.1 %collective-permute-start.10 = (bf16[48,1920]{1,0:T(8,128)(2,1)S(1)}, bf16[48,1920]{1,0:T(8,128)(2,1)S(1)}, u32[]{:S(2)}, u32[]{:S(2)}) collective-permute-start(bf16[48,1920]{1,0:T(8,128)(2,1)S(1)} %get-tuple-element.187), channel_id=1, source_target_pairs={{0,16},{2,18},{4,20},{6,22},{8,24},{10,26},{12,28},{14,30},{16,0},... | collective-permute-start | bytes 552968 | tf_op jit(solution)/shard_map/ppermute | solution.py:724
  63.2 18.7 %collective-permute-start.13 = (bf16[4,48,896]{2,1,0:T(8,128)(2,1)S(1)}, bf16[4,48,896]{2,1,0:T(8,128)(2,1)}, u32[]{:S(2)}, u32[]{:S(2)}) collective-permute-start(bf16[4,48,896]{2,1,0:T(8,128)(2,1)S(1)} %pad_maximum_fusion.10), channel_id=1, source_target_pairs={{0,4},{2,6},{4,0},{6,2},{8,12},{10,14},{12,8},{14,10},{16,20},{18,... | collective-permute-start | bytes 1032200 | tf_op jit(solution)/shard_map/ppermute | solution.py:702
  65.7 16.3 %collective-permute-start.12 = (bf16[4,48,1024]{2,1,0:T(8,128)(2,1)}, bf16[4,48,1024]{2,1,0:T(8,128)(2,1)}, u32[]{:S(2)}, u32[]{:S(2)}) collective-permute-start(bf16[4,48,1024]{2,1,0:T(8,128)(2,1)} %slice.100), channel_id=1, source_target_pairs={{0,2},{2,0},{4,6},{6,4},{8,10},{10,8},{12,14},{14,12},{16,18},{18,... | collective-permute-start | bytes 1179656 | tf_op jit(solution)/shard_map/ppermute | solution.py:702
  83.3 17.3 %collective-permute-start.16 = (bf16[2,4,48,896]{3,2,1,0:T(8,128)(2,1)S(1)}, bf16[2,4,48,896]{3,2,1,0:T(8,128)(2,1)S(1)}, u32[]{:S(2)}, u32[]{:S(2)}) collective-permute-start(bf16[2,4,48,896]{3,2,1,0:T(8,128)(2,1)S(1)} %pad_maximum_fusion.5), channel_id=1, source_target_pairs={{0,2},{2,0},{4,6},{6,4},{8,10},{10,8},{12,14},{14,12},{16,18},{18,... | collective-permute-start | bytes 2064392 | tf_op jit(solution)/shard_map/ppermute | solution.py:702
  86.6 18.9 %collective-permute-start.15 = (bf16[2,4,48,1024]{3,2,1,0:T(8,128)(2,1)S(1)}, bf16[2,4,48,1024]{3,2,1,0:T(8,128)(2,1)S(1)}, u32[]{:S(2)}, u32[]{:S(2)}) collective-permute-start(bf16[2,4,48,1024]{3,2,1,0:T(8,128)(2,1)S(1)} %pad_maximum_fusion.2), channel_id=1, source_target_pairs={{0,4},{2,6},{4,0},{6,2},{8,12},{10,14},{12,8},{14,10},{16,20},{18,... | collective-permute-start | bytes 2359304 | tf_op jit(solution)/shard_map/ppermute | solution.py:702
  174.2 18.6 %collective-permute-start.23 = (bf16[4,2,48,768]{3,2,1,0:T(8,128)(2,1)S(1)}, bf16[4,2,48,768]{3,2,1,0:T(8,128)(2,1)S(1)}, u32[]{:S(2)}, u32[]{:S(2)}) collective-permute-start(bf16[4,2,48,768]{3,2,1,0:T(8,128)(2,1)S(1)} %dynamic-slice_bitcast_fusion.2), channel_id=1, source_target_pairs={{0,4},{2,6},{4,0},{6,2},{8,12},{10,14},{12,8},{14,10},{16,20},{18,... | collective-permute-start | bytes 1769480 | tf_op jit(solution)/shard_map/ppermute | solution.py:702
  174.7 18.2 %collective-permute-start.22 = (bf16[4,2,48,768]{3,2,0,1:T(8,128)(2,1)S(1)}, bf16[4,2,48,768]{3,2,0,1:T(8,128)(2,1)S(1)}, u32[]{:S(2)}, u32[]{:S(2)}) collective-permute-start(bf16[4,2,48,768]{3,2,0,1:T(8,128)(2,1)S(1)} %bitcast.290), channel_id=1, source_target_pairs={{0,2},{2,0},{4,6},{6,4},{8,10},{10,8},{12,14},{14,12},{16,18},{18,... | collective-permute-start | bytes 1769480 | tf_op jit(solution)/shard_map/ppermute | solution.py:702
  180.9 24.6 %collective-permute-start.21 = (bf16[4,2,48,896]{3,2,1,0:T(8,128)(2,1)}, bf16[4,2,48,896]{3,2,1,0:T(8,128)(2,1)}, u32[]{:S(2)}, u32[]{:S(2)}) collective-permute-start(bf16[4,2,48,896]{3,2,1,0:T(8,128)(2,1)} %dynamic-slice_bitcast_fusion.1), channel_id=1, source_target_pairs={{0,4},{2,6},{4,0},{6,2},{8,12},{10,14},{12,8},{14,10},{16,20},{18,... | collective-permute-start | bytes 2064392 | tf_op jit(solution)/shard_map/ppermute | solution.py:702
  181.7 25.4 %collective-permute-start.20 = (bf16[4,2,48,1024]{3,2,1,0:T(8,128)(2,1)}, bf16[4,2,48,1024]{3,2,1,0:T(8,128)(2,1)}, u32[]{:S(2)}, u32[]{:S(2)}) collective-permute-start(bf16[4,2,48,1024]{3,2,1,0:T(8,128)(2,1)} %dynamic-slice_bitcast_fusion), channel_id=1, source_target_pairs={{0,2},{2,0},{4,6},{6,4},{8,10},{10,8},{12,14},{14,12},{16,18},{18,... | collective-permute-start | bytes 2359304 | tf_op jit(solution)/shard_map/ppermute | solution.py:702
  202.3 16.5 %collective-permute-start.26 = (bf16[768,1152]{1,0:T(8,128)(2,1)}, bf16[768,1152]{1,0:T(8,128)(2,1)}, u32[]{:S(2)}, u32[]{:S(2)}) collective-permute-start(bf16[768,1152]{1,0:T(8,128)(2,1)} %convolution_convert_fusion.3), channel_id=1, source_target_pairs={{0,1},{1,0},{2,3},{3,2},{4,5},{5,4},{6,7},{7,6},{8,9},{9,8},{10,11... | collective-permute-start | bytes 5308424 | tf_op jit(solution)/shard_map/ppermute | solution.py:702
  203.1 19.5 %collective-permute-start.25 = (bf16[4,48,768]{2,1,0:T(8,128)(2,1)}, bf16[4,48,768]{2,1,0:T(8,128)(2,1)S(1)}, u32[]{:S(2)}, u32[]{:S(2)}) collective-permute-start(bf16[4,48,768]{2,1,0:T(8,128)(2,1)} %dynamic-slice_bitcast_fusion.6), channel_id=1, source_target_pairs={{0,2},{2,0},{4,6},{6,4},{8,10},{10,8},{12,14},{14,12},{16,18},{18,... | collective-permute-start | bytes 884744 | tf_op jit(solution)/shard_map/ppermute | solution.py:702
  203.8 20.4 %collective-permute-start.24 = (bf16[4,48,768]{2,1,0:T(8,128)(2,1)}, bf16[4,48,768]{2,1,0:T(8,128)(2,1)S(1)}, u32[]{:S(2)}, u32[]{:S(2)}) collective-permute-start(bf16[4,48,768]{2,1,0:T(8,128)(2,1)} %dynamic-slice_bitcast_fusion.7), channel_id=1, source_target_pairs={{0,4},{2,6},{4,0},{6,2},{8,12},{10,14},{12,8},{14,10},{16,20},{18,... | collective-permute-start | bytes 884744 | tf_op jit(solution)/shard_map/ppermute | solution.py:702
  209.7 43.9 %collective-permute-start.32 = (bf16[4,48,896]{2,1,0:T(8,128)(2,1)}, bf16[4,48,896]{2,1,0:T(8,128)(2,1)}, u32[]{:S(2)}, u32[]{:S(2)}) collective-permute-start(bf16[4,48,896]{2,1,0:T(8,128)(2,1)} %dynamic-slice_bitcast_fusion.5), channel_id=1, source_target_pairs={{0,2},{2,0},{4,6},{6,4},{8,10},{10,8},{12,14},{14,12},{16,18},{18,... | collective-permute-start | bytes 1032200 | tf_op jit(solution)/shard_map/ppermute | solution.py:702
  213.2 41.5 %collective-permute-start.31 = (bf16[4,48,1024]{2,1,0:T(8,128)(2,1)}, bf16[4,48,1024]{2,1,0:T(8,128)(2,1)}, u32[]{:S(2)}, u32[]{:S(2)}) collective-permute-start(bf16[4,48,1024]{2,1,0:T(8,128)(2,1)} %dynamic-slice_bitcast_fusion.4), channel_id=1, source_target_pairs={{0,4},{2,6},{4,0},{6,2},{8,12},{10,14},{12,8},{14,10},{16,20},{18,... | collective-permute-start | bytes 1179656 | tf_op jit(solution)/shard_map/ppermute | solution.py:702
  222.6 26.6 %collective-permute-start.28 = (bf16[4,2,48,640]{3,2,1,0:T(8,128)(2,1)}, bf16[4,2,48,640]{3,2,1,0:T(8,128)(2,1)}, u32[]{:S(2)}, u32[]{:S(2)}) collective-permute-start(bf16[4,2,48,640]{3,2,1,0:T(8,128)(2,1)} %dynamic-slice_bitcast_fusion.3), channel_id=1, source_target_pairs={{0,4},{2,6},{4,0},{6,2},{8,12},{10,14},{12,8},{14,10},{16,20},{18,... | collective-permute-start | bytes 1474568 | tf_op jit(solution)/shard_map/ppermute | solution.py:702
  222.6 23.7 %collective-permute-start.27 = (bf16[4,2,48,512]{3,2,0,1:T(8,128)(2,1)}, bf16[4,2,48,512]{3,2,0,1:T(8,128)(2,1)}, u32[]{:S(2)}, u32[]{:S(2)}) collective-permute-start(bf16[4,2,48,512]{3,2,0,1:T(8,128)(2,1)} %bitcast.257), channel_id=1, source_target_pairs={{0,2},{2,0},{4,6},{6,4},{8,10},{10,8},{12,14},{14,12},{16,18},{18,... | collective-permute-start | bytes 1179656 | tf_op jit(solution)/shard_map/ppermute | solution.py:702
  236.5 30.1 %collective-permute-start.43 = (bf16[48,1536]{1,0:T(8,128)(2,1)}, bf16[48,1536]{1,0:T(8,128)(2,1)}, u32[]{:S(2)}, u32[]{:S(2)}) collective-permute-start(bf16[48,1536]{1,0:T(8,128)(2,1)} %get-tuple-element.166), channel_id=1, source_target_pairs={{0,8},{2,10},{4,12},{6,14},{8,16},{10,18},{12,20},{14,22},{16,24},... | collective-permute-start | bytes 442376 | tf_op jit(solution)/shard_map/ppermute | solution.py:796
  238.0 55.7 %all-to-all-start = ((bf16[16,24,768]{2,1,0:T(8,128)(2,1)}), bf16[16,24,768]{2,1,0:T(8,128)(2,1)}, u32[]{:S(2)}, u32[]{:S(2)}) async-start(bf16[16,24,768]{2,1,0:T(8,128)(2,1)} %fusion.9), calls=%async_computation | async-start | bytes 1179648 | tf_op jit(solution)/shard_map/all_to_all | solution.py:961
  246.3 29.3 %collective-permute-start.44 = (bf16[48,1536]{1,0:T(8,128)(2,1)}, bf16[48,1536]{1,0:T(8,128)(2,1)S(1)}, u32[]{:S(2)}, u32[]{:S(2)}) collective-permute-start(bf16[48,1536]{1,0:T(8,128)(2,1)} %get-tuple-element.167), channel_id=1, source_target_pairs={{0,16},{2,18},{4,20},{6,22},{8,24},{10,26},{12,28},{14,30},{16,0},... | collective-permute-start | bytes 442376 | tf_op jit(solution)/shard_map/ppermute | solution.py:796
  249.2 27.0 %collective-permute-start.45 = (bf16[48,1536]{1,0:T(8,128)(2,1)}, bf16[48,1536]{1,0:T(8,128)(2,1)S(1)}, u32[]{:S(2)}, u32[]{:S(2)}) collective-permute-start(bf16[48,1536]{1,0:T(8,128)(2,1)} %get-tuple-element.164), channel_id=1, source_target_pairs={{0,24},{2,26},{4,28},{6,30},{8,0},{10,2},{12,4},{14,6},{16,8},{18,... | collective-permute-start | bytes 442376 | tf_op jit(solution)/shard_map/ppermute | solution.py:796
  260.4 34.4 %collective-permute-start.33 = (bf16[64,768]{1,0:T(8,128)(2,1)}, bf16[64,768]{1,0:T(8,128)(2,1)S(1)}, u32[]{:S(2)}, u32[]{:S(2)}) collective-permute-start(bf16[64,768]{1,0:T(8,128)(2,1)} %slice.108), channel_id=1, source_target_pairs={{2,0},{4,2},{6,4},{8,6},{10,8},{12,10},{14,12},{16,14},{18,16},{20... | collective-permute-start | bytes 294920 | tf_op jit(solution)/shard_map/ppermute | solution.py:683
  266.5 18.4 %collective-permute-start.40 = (bf16[48,1920]{1,0:T(8,128)(2,1)S(1)}, bf16[48,1920]{1,0:T(8,128)(2,1)S(1)}, u32[]{:S(2)}, u32[]{:S(2)}) collective-permute-start(bf16[48,1920]{1,0:T(8,128)(2,1)S(1)} %get-tuple-element.157), channel_id=1, source_target_pairs={{0,16},{2,18},{4,20},{6,22},{8,24},{10,26},{12,28},{14,30},{16,0},... | collective-permute-start | bytes 552968 | tf_op jit(solution)/shard_map/ppermute | solution.py:796
  285.1 16.8 %collective-permute-start.35 = (bf16[48,1152]{1,0:T(8,128)(2,1)}, bf16[48,1152]{1,0:T(8,128)(2,1)}, u32[]{:S(2)}, u32[]{:S(2)}) collective-permute-start(bf16[48,1152]{1,0:T(8,128)(2,1)} %get-tuple-element.182), channel_id=1, source_target_pairs={{0,8},{2,10},{4,12},{6,14},{8,16},{10,18},{12,20},{14,22},{16,24},... | collective-permute-start | bytes 331784 | tf_op jit(solution)/shard_map/ppermute | solution.py:796
  (70 other events, 444.9 us)
Sparse Core Ops, SparseCore 0:
  25.9 71.4 all-gather.1
